TPU v7x, 32 devices: a whole 2x2x4 slice. The times are simulated.
32 devices in a mesh: lat: 4 (over z), lon: 8 (over y, x, core).
Axes of the slice: x: 2, y: 2, z: 4, core: 2. Of those that a mesh axis runs over, the one named last changes fastest.
Arguments:
- control: float32 [16, 512, 512], P('lat', 'lon'), may hold values from -1.2 to 1.2
- vert_factor: float32 [4, 128, 128], replicated, may hold values from -0.5 to 0.5
- zonal_factor: float32 [512, 512], replicated, may hold values from -0.25 to 0.25
- obs_dest: int32 [24576, 1], P(('lat', 'lon')), may hold values from 0 to 31; in each aligned block of 768 rows (0 to 767, 768 to 1535, ...) at most 36 rows name the same one
- obs_cell: int32 [24576], P(('lat', 'lon')), may hold values from 0 to 255
- obs_offset: int32 [24576], P(('lat', 'lon')), may hold values from 0 to 96
- obs_count: int32 [32], P(('lat', 'lon')), may hold values from 384 to 768, as said below
- departure: float32 [24576], P(('lat', 'lon')), may hold values from -6 to 6
- obs_rinv: float32 [24576], P(('lat', 'lon')), may hold values from 0.25 to 4
- obs_weights: float32 [24576, 128], P(('lat', 'lon')), may hold values from 0 to 1
Outputs:
- gradient: float32 [16, 512, 512], P('lat', 'lon')
Inputs may be any that keep to these rules, and one draw needn't show every extreme that they name: Among the 768 observations of one device, at most 36 have the same obs_dest, and some value is taken exactly 36 times on some devices. `obs_count`: some device holds exactly 768 live observations.
All inputs are finite; a program needn't handle non-finite values.
Results may differ from a plain program's by a relative error of at most 0.000068.
Values sent between devices are 32-bit elements; how exact they have to be, the bound alone decides.
No kernel may reach another device: no remote copies, remote signals or barrier semaphores. Data moves between devices by JAX's collectives and lax.ppermute only.
A program may use at most 64 MiB of HBM per device.

v0:
```python
import jax
import jax.numpy as jnp
from jax import lax
from jax.sharding import PartitionSpec as P

F = 4
LEV = 128
KW = 32


def place_levels(blocks, offsets):
    level_ids = jnp.arange(LEV, dtype=jnp.int32)
    block_ids = jnp.arange(KW, dtype=jnp.int32)
    shift_mat = (
        level_ids[None, None, :] - offsets[:, None, None] == block_ids[None, :, None]
    ).astype(jnp.float32)
    placed = jnp.einsum("rfk,rkl->rfl", blocks, shift_mat, precision=lax.Precision.HIGHEST)
    return placed.reshape(blocks.shape[0], F * LEV)


def per_device(
    control,
    vert_factor,
    zonal_factor,
    obs_dest,
    obs_cell,
    obs_offset,
    obs_count,
    departure,
    obs_rinv,
    obs_weights,
):
    lat_count = lax.axis_size("lat")
    lon_count = lax.axis_size("lon")
    devices = lat_count * lon_count
    n_obs = obs_cell.shape[0]
    capacity = max(2, 3 * n_obs // (2 * devices))
    slots = devices * capacity
    lat_rows = control.shape[0]
    lon_cols = control.shape[1]
    depth = control.shape[2]
    columns = lat_rows * lon_cols
    positions = jnp.arange(n_obs, dtype=jnp.int32)
    live = positions < obs_count[0]
    scaled = jnp.where(live, obs_rinv * departure, jnp.float32(0.0))
    values = obs_weights * scaled[:, None]
    target = obs_dest[:, 0]
    onehot = (target[:, None] == jnp.arange(devices, dtype=jnp.int32)[None, :]).astype(jnp.int32)
    ranks = jnp.sum(jnp.cumsum(onehot, axis=0) * onehot, axis=1) - 1
    slot_of = target * capacity + ranks
    slot_hit = slot_of[None, :] == jnp.arange(slots, dtype=jnp.int32)[:, None]
    slot_mat = slot_hit.astype(jnp.float32)
    cell_label = jnp.sum(jnp.where(slot_hit, obs_cell[None, :], 0), axis=1)
    payload = jnp.dot(slot_mat, values, precision=lax.Precision.HIGHEST)
    offset_label = jnp.sum(jnp.where(slot_hit, obs_offset[None, :], 0), axis=1)
    labels = jnp.stack([cell_label, offset_label], axis=1)
    width = payload.shape[1]
    label_width = labels.shape[1]
    got, got_labels = (
        lax.all_to_all(
            payload.reshape(devices, capacity, width),
            ("lat", "lon"),
            split_axis=0,
            concat_axis=0,
            tiled=True,
        ),
        lax.all_to_all(
            labels.reshape(devices, capacity, label_width),
            ("lat", "lon"),
            split_axis=0,
            concat_axis=0,
            tiled=True,
        ),
    )
    got = got.reshape(slots, width)
    got_labels = got_labels.reshape(slots, label_width)
    cell_mat = (jnp.arange(columns, dtype=jnp.int32)[:, None] == got_labels[:, 0][None, :]).astype(
        jnp.float32
    )
    received = place_levels(got.reshape(slots, F, KW), got_labels[:, 1])
    adjoint = jnp.dot(cell_mat, received, precision=lax.Precision.HIGHEST)
    blocks = adjoint.reshape(lat_rows, lon_cols, F, LEV)
    vertical = jnp.einsum("abfk,fkl->aflb", blocks, vert_factor, precision=lax.Precision.HIGHEST)
    vertical = vertical.reshape(lat_rows, depth, lon_cols)
    product = jnp.einsum(
        "alm,mn->aln",
        lax.all_to_all(vertical, "lon", split_axis=1, concat_axis=2, tiled=True),
        zonal_factor,
        precision=lax.Precision.HIGHEST,
    )
    zonal = lax.all_to_all(product, "lon", split_axis=2, concat_axis=1, tiled=True)
    return control + jnp.transpose(zonal, (0, 2, 1))


def solution(mesh):
    return jax.shard_map(
        per_device,
        mesh=mesh,
        in_specs=(
            P("lat", "lon", None),
            P(),
            P(),
            P(("lat", "lon"), None),
            P(("lat", "lon")),
            P(("lat", "lon")),
            P(("lat", "lon")),
            P(("lat", "lon")),
            P(("lat", "lon")),
            P(("lat", "lon"), None),
        ),
        out_specs=P("lat", "lon", None),
        check_vma=False,
    )
```

profile of v0, /device:TPU:0, one launch (start us, length us, event | category | flops | bytes accessed | tf_op | source)
XLA Modules:
  0.0 98.8 jit_solution(2378894517570788425)
XLA Ops:
  0.0 0.0 copy-start
  0.0 0.8 reduce
  0.8 1.7 %reduce-window.6 = s32[32,6,128]{2,0,1:T(8,128)S(1)} reduce-window(s32[32,6,128]{2,0,1:T(8,128)S(1)} %fusion.16, s32[]{:T(128)} %constant.12.clone.1), window={size=1x1x128 pad=0_0x0_0x127_0}, to_apply=%region_0.1 | reduce-window | flops 3121152 | bytes 196612 | tf_op jit(solution)/shard_map/reduce-window
  2.6 0.3 slice_reduce_fusion
  2.8 0.1 fusion.15
  3.0 1.8 %select_reduce_fusion.1 = (s32[1152]{0:T(1024)S(1)}, s32[1152]{0:T(1024)S(1)}) fusion(s32[768]{0:T(1024)} %param.14, s32[768]{0:T(1024)S(1)} %add_add_fusion, s32[768]{0:T(1024)} %param.15), kind=kLoop, calls=%fused_computation.4 | loop fusion | flops 4421376 | bytes 18432 | tf_op jit(solution)/shard_map/reduce_sum | solution.py:53
  4.8 0.1 stack.10
  4.9 0.1 stack.9
  5.0 0.6 copy.31
  5.6 7.3 %all-to-all-start = ((s32[32,36,2]{1,2,0:T(2,128)}), s32[32,36,2]{1,2,0:T(2,128)S(1)}, u32[]{:S(2)}, u32[]{:S(2)}) async-start(s32[32,36,2]{1,2,0:T(2,128)} %copy.31), calls=%async_computation | async-start | bytes 65536 | tf_op jit(solution)/shard_map/all_to_all | solution.py:67
  13.6 0.7 multiply_select_fusion
  14.3 2.8 %fusion.2 = f32[1152,128]{1,0:T(8,128)S(1)} fusion(s32[768]{0:T(1024)S(1)} %add_add_fusion, f32[768,128]{1,0:T(8,128)} %param.19, f32[768]{0:T(1024)S(1)} %multiply_select_fusion), kind=kOutput, calls=%fused_computation.6 | convolution fusion | flops 1359937536 | bytes 989184 | tf_op jit(solution)/shard_map/dot_general | solution.py:54
  17.1 0.9 reshape.91
  17.9 2.3 %all-to-all-done = s32[32,36,2]{1,2,0:T(2,128)S(1)} async-done(((s32[32,36,2]{1,2,0:T(2,128)}), s32[32,36,2]{1,2,0:T(2,128)S(1)}, u32[]{:S(2)}, u32[]{:S(2)}) %all-to-all-start) | async-done | bytes 9248 | tf_op jit(solution)/shard_map/all_to_all | solution.py:67
  20.2 3.8 %all-to-all-start.1 = ((f32[32,36,128]{2,1,0:T(8,128)}), f32[32,36,128]{2,1,0:T(8,128)S(1)}, u32[]{:S(2)}, u32[]{:S(2)}) async-start(f32[32,36,128]{2,1,0:T(8,128)} %reshape.91), calls=%async_computation.1 | async-start | bytes 1310720 | tf_op jit(solution)/shard_map/all_to_all | solution.py:60
  24.0 0.1 reshape.90
  24.1 0.2 iota_subtract_fusion
  24.3 17.3 %all-to-all-done.1 = f32[32,36,128]{2,1,0:T(8,128)S(1)} async-done(((f32[32,36,128]{2,1,0:T(8,128)}), f32[32,36,128]{2,1,0:T(8,128)S(1)}, u32[]{:S(2)}, u32[]{:S(2)}) %all-to-all-start.1) | async-done | bytes 589856 | tf_op jit(solution)/shard_map/all_to_all | solution.py:60
  41.7 2.4 %reshape.98 = f32[1152,4,32]{2,1,0:T(4,128)} reshape(f32[32,36,128]{2,1,0:T(8,128)S(1)} %all-to-all-done.1) | data formatting | bytes 1179648 | tf_op jit(solution)/shard_map/reshape;reshape | solution.py:80
  44.1 10.5 %fusion = f32[1152,4,128]{2,1,0:T(4,128)S(1)} fusion(f32[1152,4,32]{2,1,0:T(4,128)} %reshape.98, s32[1152,128]{1,0:T(8,128)S(1)} %iota_subtract_fusion), kind=kOutput, calls=%fused_computation.1 | convolution fusion | flops 231211008 | bytes 3538944 | tf_op jit(solution)/shard_map/rfk,rkl->rfl/dot_general | solution.py:17
  54.6 1.6 %copy.54 = f32[144,8,4,128]{3,1,2,0:T(8,128)} copy(f32[144,8,4,128]{3,2,1,0:T(4,128)S(1)} %bitcast.78) | data formatting | bytes 4718592
  56.2 2.0 %copy.35 = f32[512,1152]{1,0:T(8,128)S(1)} copy(f32[512,1152]{0,1:T(8,128)} %bitcast.72) | data formatting | bytes 4718592 | tf_op jit(solution)/shard_map/dot_general | solution.py:81
  58.3 0.0 copy-start.1
  58.3 1.4 %fusion.4 = f32[4,64,4,128]{3,1,0,2:T(8,128)S(1)} fusion(f32[4,128,1152,1]{2,1,3,0:T(8,128)S(1)} %bitcast.71, s32[1152]{0:T(1024)S(1)} %get-tuple-element.5, s32[4,64]{1,0:T(4,128)S(1)} %multiply_add_fusion), kind=kOutput, calls=%fused_computation.10 | convolution fusion | flops 1812234240 | bytes 2889216 | tf_op jit(solution)/shard_map/dot_general | solution.py:81
  59.7 0.0 copy-done.1
  59.7 0.6 convolution_bitcast_fusion
  60.4 0.4 copy.45
  60.8 1.0 reshape.104
  61.7 13.1 %all_to_all.46 = f32[8,1,16384]{2,1,0:T(1,128)S(1)} all-to-all(f32[8,1,16384]{2,1,0:T(1,128)S(1)} %reshape.104), channel_id=1, replica_groups=mesh['lat'=4,'lon'=8] {'lon'}, dimensions={0} | all-to-all | bytes 1048576 | tf_op jit(solution)/shard_map/all_to_all | solution.py:87
  74.8 0.5 broadcast.71
  75.4 1.9 %reduce.8 = f32[8,16384]{1,0:T(8,128)S(1)} reduce(f32[8,1,16384]{2,1,0:T(1,128)S(1)} %all_to_all.46, f32[]{:T(128)} %broadcast.71), dimensions={1}, to_apply=%all_to_all.34.reduce_sub_computation | reduce | bytes 1048580 | tf_op jit(solution)/shard_map/all_to_all | solution.py:87
  77.3 0.7 reshape.105
  77.9 0.6 copy.55
  78.6 0.3 all_to_all.37
  78.8 0.0 copy-done
  78.9 1.1 %fusion.7 = f32[4,64,512]{2,1,0:T(8,128)S(1)} fusion(f32[4,64,512]{2,1,0:T(8,128)S(1)} %all_to_all.37, f32[512,512]{1,0:T(8,128)S(1)} %copy-done), kind=kOutput, calls=%fused_computation.13 | convolution fusion | flops 805306368 | bytes 2097152 | tf_op jit(solution)/shard_map/alm,mn->aln/dot_general | solution.py:85
  79.9 0.4 copy.40
  80.3 1.0 reshape.106
  81.3 12.2 %all_to_all.47 = f32[8,1,16384]{2,1,0:T(1,128)S(1)} all-to-all(f32[8,1,16384]{2,1,0:T(1,128)S(1)} %reshape.106), channel_id=1, replica_groups=mesh['lat'=4,'lon'=8] {'lon'}, dimensions={0} | all-to-all | bytes 1048576 | tf_op jit(solution)/shard_map/all_to_all | solution.py:91
  93.4 1.9 %reduce.9 = f32[8,16384]{1,0:T(8,128)S(1)} reduce(f32[8,1,16384]{2,1,0:T(1,128)S(1)} %all_to_all.47, f32[]{:T(128)} %broadcast.71), dimensions={1}, to_apply=%all_to_all.38.reduce_sub_computation | reduce | bytes 1048580 | tf_op jit(solution)/shard_map/all_to_all | solution.py:91
  95.3 0.7 reshape.107
  96.0 0.6 copy.41
  96.6 0.3 all_to_all.41
  96.9 1.9 %bitcast_add_fusion = f32[4,64,512]{2,1,0:T(8,128)} fusion(f32[4,64,512]{2,1,0:T(8,128)} %param.10, f32[4,512,64]{1,2,0:T(8,128)S(1)} %all_to_all.41), kind=kLoop, calls=%fused_computation.19 | loop fusion | flops 131072 | bytes 1572864 | tf_op jit(solution)/shard_map/add | solution.py:92
  (7 shorter events, 0.1 us)
Async XLA Ops:
  0.0 78.8 %copy-start = (f32[512,512]{1,0:T(8,128)S(1)}, f32[512,512]{1,0:T(8,128)}, u32[]{:S(2)}) copy-start(f32[512,512]{1,0:T(8,128)} %param.12) | copy-start | bytes 3145732
  5.6 14.6 %all-to-all-start = ((s32[32,36,2]{1,2,0:T(2,128)}), s32[32,36,2]{1,2,0:T(2,128)S(1)}, u32[]{:S(2)}, u32[]{:S(2)}) async-start(s32[32,36,2]{1,2,0:T(2,128)} %copy.31), calls=%async_computation | async-start | bytes 65536 | tf_op jit(solution)/shard_map/all_to_all | solution.py:67
  20.2 21.5 %all-to-all-start.1 = ((f32[32,36,128]{2,1,0:T(8,128)}), f32[32,36,128]{2,1,0:T(8,128)S(1)}, u32[]{:S(2)}, u32[]{:S(2)}) async-start(f32[32,36,128]{2,1,0:T(8,128)} %reshape.91), calls=%async_computation.1 | async-start | bytes 1310720 | tf_op jit(solution)/shard_map/all_to_all | solution.py:60
  58.3 1.5 %copy-start.1 = (f32[4,128,128]{2,1,0:T(8,128)S(1)}, f32[4,128,128]{2,1,0:T(8,128)}, u32[]{:S(2)}) copy-start(f32[4,128,128]{2,1,0:T(8,128)} %param.11) | copy-start | bytes 786436
where the time goes:
time: 99.4 us; the launch traced here: 98.8 us
  blocking collectives  25.3 us (25%)
  waiting for transfers between devices  19.6 us (20%)
  matrix products  16.3 us (16%)
  local copies, waits for them, and re-layouts  14.6 us (15%)
  other arithmetic  11.1 us (11%)
  starting transfers between devices  11.1 us (11%)
    all_to_all x1, waiting for transfers between devices, per_device(): lax.all_to_all(payload.reshape(devices, capacity, width), ('lat', 'lon'),...  17.3 us
    all_to_all x1, blocking collectives, per_device(): lax.all_to_all(vertical, 'lon', split_axis=1, concat_axis=2, tiled=True)  13.1 us
    all_to_all x1, blocking collectives, per_device(): lax.all_to_all(product, 'lon', split_axis=2, concat_axis=1, tiled=True)  12.2 us
    dot_general x1, matrix products, place_levels(): jnp.einsum('rfk,rkl->rfl', blocks, shift_mat, precision=lax.Precision.HIG...  10.5 us
    all_to_all x1, starting transfers between devices, per_device(): lax.all_to_all(labels.reshape(devices, capacity, label_width), ('lat', 'l...  7.3 us
    unnamed x9, local copies, waits for them, and re-layouts  4.94 us
    all_to_all x1, starting transfers between devices, per_device(): lax.all_to_all(payload.reshape(devices, capacity, width), ('lat', 'lon'),...  3.76 us
    dot_general x1, matrix products, per_device(): payload = jnp.dot(slot_mat, values, precision=lax.Precision.HIGHEST)  2.76 us
  transfers between devices with their start and end apart: 2, of which 2 were waited for; matrix products, arithmetic and copies ran while one was open for 5% of the time, Pallas kernels for 0%

commit v1 on v0

v1 whole, which is shorter than its diff:
```python
import functools

import jax
import jax.numpy as jnp
from jax import lax
from jax.experimental import pallas as pl
from jax.experimental.pallas import tpu as pltpu
from jax.sharding import PartitionSpec as P

F = 4
LEV = 128
KW = 32
LANES = 128
SUBLANES = 8
GROUPS = LANES // KW
MIB = 1 << 20


def iota(shape, axis):
    return lax.broadcasted_iota(jnp.int32, shape, axis)


def split(x):
    high = x.astype(jnp.bfloat16)
    return high, (x - high.astype(jnp.float32)).astype(jnp.bfloat16)


def dot(a, b):
    return jnp.dot(a, b, preferred_element_type=jnp.float32)


def call(kernel, out_shape, n_in, smem=(), vmem=24, flops=0, nbytes=0, scratch=()):
    specs = [
        pl.BlockSpec(memory_space=pltpu.SMEM if i in smem else pltpu.VMEM) for i in range(n_in)
    ]
    one = pl.BlockSpec(memory_space=pltpu.VMEM)
    return pl.pallas_call(
        kernel,
        out_shape=out_shape,
        in_specs=specs,
        out_specs=[one] * len(out_shape) if isinstance(out_shape, (list, tuple)) else one,
        scratch_shapes=list(scratch),
        compiler_params=pltpu.CompilerParams(vmem_limit_bytes=vmem * MIB),
        cost_estimate=pl.CostEstimate(flops=flops, bytes_accessed=nbytes, transcendentals=0),
    )


def message_rows(capacity):
    parts = -(-capacity // KW)
    return parts, -(-(capacity + 2 * parts) // SUBLANES) * SUBLANES


def pack_kernel(
    lons, members, capacity, count, dest, cell, offset, departure, rinv, weights, out, picked
):
    n = weights.shape[0]
    devices = out.shape[0]
    rows = out.shape[1]
    parts, _ = message_rows(capacity)
    quads = devices // GROUPS
    chunks = n // LANES
    dest_row = dest[...]
    hits = [
        iota((devices, LANES), 0) == dest_row[:, c * LANES : (c + 1) * LANES] for c in range(chunks)
    ]
    stacked = jnp.concatenate([hit.astype(jnp.bfloat16) for hit in hits], axis=0)
    before = (iota((LANES, 2 * LANES), 0) < iota((LANES, 2 * LANES), 1)).astype(jnp.bfloat16)
    counts = dot(stacked, before)
    carry = jnp.zeros((devices, LANES), jnp.float32)
    ranks = []
    for c in range(chunks):
        part = counts[c * devices : (c + 1) * devices]
        ranks.append(
            jnp.sum(jnp.where(hits[c], part[:, :LANES] + carry, 0.0), axis=0, keepdims=True)
        )
        carry = carry + part[:, LANES:]
    rank = jnp.concatenate(ranks, axis=1).astype(jnp.int32)
    position = dest_row * rows + rank
    group = dest_row & (GROUPS - 1)
    quad = dest_row >> (GROUPS.bit_length() - 1)
    lane = group * KW + (rank & (KW - 1))
    piece = rank >> (KW.bit_length() - 1)
    live = iota((1, n), 1) < count[0]
    scaled = jnp.where(live, rinv[...] * departure[...], jnp.float32(0.0))
    columns = jnp.concatenate(
        [
            scaled,
            lane.astype(jnp.float32),
            offset[...].astype(jnp.float32),
            jnp.zeros((SUBLANES - 3, n), jnp.float32),
        ],
        axis=0,
    ).T
    lane_id = iota((n, LANES), 1)
    source = (lane_id & -KW) | ((lane_id - columns[:, 2:3].astype(jnp.int32)) & (KW - 1))
    turned = jnp.take_along_axis(weights[...], source, axis=1, mode="promise_in_bounds")
    high, low = split(turned * columns[:, 0:1])
    lane_hit = (columns[:, 1:2].astype(jnp.int32) == lane_id).astype(jnp.bfloat16)
    label_rows = []
    for p in range(parts):
        for label in (cell, offset):
            mine = (iota((quads, n), 0) == quad) & (piece == p)
            label_rows.append(jnp.where(mine, label[...].astype(jnp.float32), 0.0))
    labels = dot(jnp.concatenate(label_rows, axis=0).astype(jnp.bfloat16), lane_hit)
    slot_hit = (iota((devices * rows, n), 0) == position).astype(jnp.bfloat16)
    both = dot(slot_hit, jnp.concatenate([high, low], axis=1))
    picked[...] = both[:, :LANES] + both[:, LANES:]
    lane_group = iota((rows, LANES), 1) >> (KW.bit_length() - 1)
    row_id = iota((rows, LANES), 0)
    for q in range(quads):
        band, member = q // members, q % members
        extra = jnp.zeros((rows, LANES), jnp.float32)
        for k in range(2 * parts):
            extra = jnp.where(row_id == capacity + k, labels[k * quads + q : k * quads + q + 1], extra)
        blocks = [
            picked[(q * GROUPS + g) * rows : (q * GROUPS + g + 1) * rows, :] for g in range(GROUPS)
        ]
        for f in range(F):
            message = extra
            for g in range(GROUPS):
                turned = blocks[g]
                if g != f:
                    turned = pltpu.roll(turned, (KW * (g - f)) % LANES, 1)
                message = jnp.where((lane_group == g) & (row_id < capacity), turned, message)
            out[band * lons + f * members + member] = message


def prepare_kernel(members, lon_cols, place, zonal, vert, zonal_high, zonal_low, vert_both, turned):
    f, h = place[0], place[1]
    width = GROUPS * lon_cols
    turned[...] = zonal[...].T
    for q in range(F):
        row = pl.multiple_of(((f ^ q) * members + h) * lon_cols, lon_cols)
        for e in range(members):
            source = lax.rem(h + members - e, members)
            part = turned[pl.ds(row, lon_cols), pl.ds(pl.multiple_of(source * width, LANES), width)]
            high, low = split(part)
            zonal_high[q * lon_cols : (q + 1) * lon_cols, e * width : (e + 1) * width] = high
            zonal_low[q * lon_cols : (q + 1) * lon_cols, e * width : (e + 1) * width] = low
    high, low = split(vert[f])
    vert_both[:, :LEV] = high
    vert_both[:, LEV:] = low


def place_kernel(capacity, lon_cols, received, vert_both, out):
    devices, rows, _ = received.shape
    parts, _ = message_rows(capacity)
    slots = devices * rows
    columns = out.shape[1] // LEV * lon_cols
    high, low = split(received[...].reshape(slots, LANES))
    row_id, lane_id = iota((rows, LANES), 0), iota((rows, LANES), 1)
    diagonal = (lane_id & (KW - 1)) == (row_id & (KW - 1))
    cells = jnp.where((row_id >= capacity) & ((lane_id & (KW - 1)) == 0), -1.0, 0.0)[None]
    offsets = jnp.zeros((1, rows, LANES), jnp.float32)
    for p in range(parts):
        mine = (diagonal & (row_id >> (KW.bit_length() - 1) == p) & (row_id < capacity))[None]
        at = capacity + 2 * p
        cells = jnp.where(mine, received[:, at : at + 1, :], cells)
        offsets = jnp.where(mine, received[:, at + 1 : at + 2, :], offsets)
    cells = cells.reshape(slots, LANES).astype(jnp.bfloat16)
    offsets = offsets.reshape(slots, LANES).astype(jnp.bfloat16)
    wide = (LANES, GROUPS * LEV)
    spread = (iota(wide, 0) >> 5 == iota(wide, 1) >> 7).astype(jnp.bfloat16)
    tile = (
        (iota(wide, 0) >> 5 == iota(wide, 1) >> 7) & ((iota(wide, 0) & 31) == (iota(wide, 1) & 31))
    ).astype(jnp.bfloat16)
    picker = (iota((SUBLANES, LANES), 0) == iota((SUBLANES, LANES), 1) >> 5).astype(jnp.bfloat16)
    cell_rows = lax.dot_general(
        picker, cells, (((1,), (1,)), ((), ())), preferred_element_type=jnp.float32
    ).astype(jnp.int32)
    middle = iota((slots, LEV), 1).astype(jnp.float32) - (KW - 1) / 2
    for g in range(GROUPS):
        part = slice(g * LEV, (g + 1) * LEV)
        inside = jnp.abs(middle - dot(offsets, spread[:, part])) < KW / 2
        placed = jnp.concatenate(
            [
                jnp.where(inside, dot(high, tile[:, part]), 0.0).astype(jnp.bfloat16),
                jnp.where(inside, dot(low, tile[:, part]), 0.0).astype(jnp.bfloat16),
            ],
            axis=1,
        )
        hit = (iota((columns, slots), 0) == cell_rows[g : g + 1]).astype(jnp.bfloat16)
        both = dot(hit, placed)
        adjoint_high, adjoint_low = split(both[:, :LEV] + both[:, LEV:])
        first = dot(adjoint_high, vert_both[...])
        vertical = first[:, :LEV] + first[:, LEV:] + dot(adjoint_low, vert_both[:, :LEV])
        for a in range(columns // lon_cols):
            out[g * lon_cols : (g + 1) * lon_cols, a * LEV : (a + 1) * LEV] = vertical[
                a * lon_cols : (a + 1) * lon_cols
            ]


def zonal_term(e, width, zonal_high, zonal_low, vertical):
    part = slice(e * width, (e + 1) * width)
    high, low = split(vertical[...])
    first = dot(zonal_high[:, part], high) + dot(zonal_low[:, part], high)
    return first + dot(zonal_high[:, part], low)


def own_kernel(zonal_high, zonal_low, vertical, out):
    out[...] = zonal_term(0, vertical.shape[0], zonal_high, zonal_low, vertical)


def zonal_kernel(members, lon_cols, *refs):
    zonal_high, zonal_low, total = refs[:3]
    verticals, outs = refs[3 : 2 + members], refs[2 + members :]
    product = total[...]
    for e, vertical in enumerate(verticals, 1):
        product = product + zonal_term(e, vertical.shape[0], zonal_high, zonal_low, vertical)
    for q in range(F):
        outs[q][...] = product[q * lon_cols : (q + 1) * lon_cols]


def finish_kernel(place, control, *refs):
    parts, out = refs[:F], refs[F]
    for q in range(F):
        at = pl.ds(pl.multiple_of((place[0] ^ q) * LEV, LEV), LEV)
        for a in range(control.shape[0]):
            out[a, :, at] = control[a, :, at] + parts[q][:, a * LEV : (a + 1) * LEV]


def per_device(
    control,
    vert_factor,
    zonal_factor,
    obs_dest,
    obs_cell,
    obs_offset,
    obs_count,
    departure,
    obs_rinv,
    obs_weights,
):
    lats = lax.axis_size("lat")
    lons = lax.axis_size("lon")
    devices = lats * lons
    members = lons // F
    n_obs = obs_cell.shape[0]
    capacity = max(2, 3 * n_obs // (2 * devices))
    _, rows = message_rows(capacity)
    lat_rows, lon_cols, _ = control.shape
    width = GROUPS * lon_cols
    wide = lat_rows * LEV
    f32, bf16 = jnp.float32, jnp.bfloat16
    position = lax.axis_index("lon").astype(jnp.int32)
    place = jnp.stack([position // members, position % members])
    messages = call(
        functools.partial(pack_kernel, lons, members, capacity),
        jax.ShapeDtypeStruct((devices, rows, LANES), f32),
        7,
        smem=(0,),
        scratch=[pltpu.VMEM((devices * rows, LANES), f32)],
        flops=4 * devices * rows * n_obs * LANES,
        nbytes=1 << 20,
    )(
        obs_count,
        obs_dest.reshape(1, n_obs),
        obs_cell.reshape(1, n_obs),
        obs_offset.reshape(1, n_obs),
        departure.reshape(1, n_obs),
        obs_rinv.reshape(1, n_obs),
        obs_weights,
    )
    received = lax.all_to_all(messages, ("lat", "lon"), 0, 0, tiled=True)
    zonal_high, zonal_low, vert_both = call(
        functools.partial(prepare_kernel, members, lon_cols),
        [
            jax.ShapeDtypeStruct((F * lon_cols, members * width), bf16),
            jax.ShapeDtypeStruct((F * lon_cols, members * width), bf16),
            jax.ShapeDtypeStruct((LEV, 2 * LEV), bf16),
        ],
        3,
        smem=(0,),
        scratch=[pltpu.VMEM(zonal_factor.shape, f32)],
        nbytes=2 << 20,
    )(place, zonal_factor, vert_factor)
    vertical = call(
        functools.partial(place_kernel, capacity, lon_cols),
        jax.ShapeDtypeStruct((width, wide), f32),
        2,
        vmem=32,
        flops=16 * devices * rows * lat_rows * width * LEV,
        nbytes=2 << 20,
    )(received, vert_both)
    others = [
        lax.ppermute(
            vertical,
            "lon",
            [
                (i, i // members * members + (i % members + e) % members)
                for i in range(lons)
            ],
        )
        for e in range(1, members)
    ]
    total = call(
        own_kernel,
        jax.ShapeDtypeStruct((F * lon_cols, wide), f32),
        3,
        flops=6 * F * lon_cols * width * wide,
        nbytes=1 << 20,
    )(zonal_high, zonal_low, vertical)
    blocks = call(
        functools.partial(zonal_kernel, members, lon_cols),
        [jax.ShapeDtypeStruct((lon_cols, wide), f32)] * F,
        2 + members,
        flops=6 * F * lon_cols * width * wide,
        nbytes=1 << 20,
    )(zonal_high, zonal_low, total, *others)
    parts = [blocks[0]] + [
        lax.ppermute(
            blocks[q],
            "lon",
            [(i, (i // members ^ q) * members + i % members) for i in range(lons)],
        )
        for q in range(1, F)
    ]
    return call(
        finish_kernel,
        jax.ShapeDtypeStruct(control.shape, f32),
        2 + F,
        smem=(0,),
        nbytes=2 << 20,
    )(place, control, *parts)


def solution(mesh):
    return jax.shard_map(
        per_device,
        mesh=mesh,
        in_specs=(
            P("lat", "lon", None),
            P(),
            P(),
            P(("lat", "lon"), None),
            P(("lat", "lon")),
            P(("lat", "lon")),
            P(("lat", "lon")),
            P(("lat", "lon")),
            P(("lat", "lon")),
            P(("lat", "lon"), None),
        ),
        out_specs=P("lat", "lon", None),
        check_vma=False,
    )
```

time: 99.4 us -> 48.9 us (0.49)
  blocking collectives: 25.3 us -> 0 us
  matrix products: 16.3 us -> 0 us
  local copies, waits for them, and re-layouts: 14.6 us -> 3.1 us
  other arithmetic: 11.1 us -> 0.08 us
  Pallas kernels: 0 us -> 9.28 us
  waiting for transfers between devices: 19.6 us -> 24.4 us
    all_to_all x2 -> x0, blocking collectives: 25.3 us -> none  [the longest x1 13.1 us: per_device(): lax.all_to_all(vertical, 'lon', split_axis=1, concat_axis=2, tiled=True)]
    dot_general x5 -> x0, matrix products: 16.3 us -> none  [the longest x1 10.5 us: place_levels(): jnp.einsum('rfk,rkl->rfl', blocks, shift_mat, precision=lax.Precision.HIG...]
    pallas_call x0 -> x6, Pallas kernels: none -> 9.28 us  [the longest x1 3.49 us: per_device(): call(functools.partial(place_kernel, capacity, lon_cols), jax.ShapeDtypeS...]
    ppermute x0 -> x4, waiting for transfers between devices: none -> 7.55 us  [the longest x3 6.11 us: per_device(): lax.ppermute(blocks[q], 'lon', [(i, (i // members ^ q) * members + i % me...]
    all_to_all x2 -> x0, other arithmetic: 3.77 us -> none  [the longest x1 1.88 us: per_device(): lax.all_to_all(product, 'lon', split_axis=2, concat_axis=1, tiled=True)]
    all_to_all x2 -> x1, starting transfers between devices: 11.1 us -> 7.3 us  [per_device(): received = lax.all_to_all(messages, ('lat', 'lon'), 0, 0, tiled=True)]
    ppermute x0 -> x4, starting transfers between devices: none -> 3.7 us  [the longest x3 3.55 us: per_device(): lax.ppermute(blocks[q], 'lon', [(i, (i // members ^ q) * members + i % me...]
    another operation x4 -> x0, local copies, waits for them, and re-layouts: 3.27 us -> none  [the longest x1 2.43 us: per_device(): received = place_levels(got.reshape(slots, F, KW), got_labels[:, 1])]
  transfers between devices with their start and end apart: 2 -> 5, of which waited for: 2 -> 4; matrix products, arithmetic and copies ran while one was open for 5% -> 0% of each run, Pallas kernels for 0% -> 3%
where the time goes in v1:
time: 48.9 us; the launch traced here: 48.6 us
  waiting for transfers between devices  24.4 us (50%)
  starting transfers between devices  11 us (22%)
  Pallas kernels  9.28 us (19%)
  local copies, waits for them, and re-layouts  3.1 us (6%)
  between operations  0.75 us (2%)
    all_to_all x1, waiting for transfers between devices, per_device(): received = lax.all_to_all(messages, ('lat', 'lon'), 0, 0, tiled=True)  16.9 us
    all_to_all x1, starting transfers between devices, per_device(): received = lax.all_to_all(messages, ('lat', 'lon'), 0, 0, tiled=True)  7.3 us
    ppermute x3, waiting for transfers between devices, per_device(): lax.ppermute(blocks[q], 'lon', [(i, (i // members ^ q) * members + i % me...  6.11 us
    ppermute x3, starting transfers between devices, per_device(): lax.ppermute(blocks[q], 'lon', [(i, (i // members ^ q) * members + i % me...  3.55 us
    pallas_call x1, Pallas kernels, per_device(): call(functools.partial(place_kernel, capacity, lon_cols), jax.ShapeDtypeS...  3.49 us
    pallas_call x1, Pallas kernels, per_device(): call(functools.partial(pack_kernel, lons, members, capacity), jax.ShapeDt...  2.67 us
    unnamed x16, local copies, waits for them, and re-layouts  2.39 us
    ppermute x1, waiting for transfers between devices, per_device(): lax.ppermute(vertical, 'lon', [(i, i // members * members + (i % members...  1.44 us
  transfers between devices with their start and end apart: 5, of which 4 were waited for; matrix products, arithmetic and copies ran while one was open for 0% of the time, Pallas kernels for 3%

profile of v1, /device:TPU:0, one launch (start us, length us, event | category | flops | bytes accessed | tf_op | source)
XLA Modules:
  0.0 48.6 jit_solution(15975430260609418243)
XLA Ops:
  0.0 0.0 copy-start.5
  0.0 0.7 %reshape.16.cell = s32[1,768]{1,0:T(1,128)S(1)} reshape(s32[768]{0:T(1024)} %param.14) | data formatting | bytes 6144 | tf_op jit(solution)/shard_map/reshape | solution.py:258
  0.7 0.0 copy-done.5
  0.7 0.0 copy-start.6
  0.7 0.7 %copy-done.6 = f32[768]{0:T(1024)S(1)} copy-done((f32[768]{0:T(1024)S(1)}, f32[768]{0:T(1024)}, u32[]{:S(2)}) %copy-start.6) | copy-done | bytes 3096
  1.4 0.0 copy-start.7
  1.4 0.7 %copy-done.7 = f32[768]{0:T(1024)S(1)} copy-done((f32[768]{0:T(1024)S(1)}, f32[768]{0:T(1024)}, u32[]{:S(2)}) %copy-start.7) | copy-done | bytes 3096
  2.1 0.0 copy-start.4
  2.8 0.0 copy-done.4
  2.8 0.0 copy-start.3
  2.8 1.0 %copy-done.3 = f32[768,128]{1,0:T(8,128)S(1)} copy-done((f32[768,128]{1,0:T(8,128)S(1)}, f32[768,128]{1,0:T(8,128)}, u32[]{:S(2)}) %copy-start.3) | copy-done | bytes 393240
  3.8 2.7 %shard_map.101 = f32[32,40,128]{2,1,0:T(8,128)} custom-call(s32[1]{0:T(128)S(6)} %copy.11.count, s32[1,768]{1,0:T(1,128)S(1)} %bitcast.3, s32[1,768]{1,0:T(1,128)S(1)} %reshape.16.cell, s32[1,768]{1,0:T(1,128)S(1)} %reshape.17.offset, f32[1,768]{1,0:T(1,128)S(1)} %reshape.18.departure, f32[1,768]{1,0:T(1,128)S(1)} %reshape.19.rinv, f32[768,128]{1,0:T(8,128)S(1)} %copy-done.3), custom_call_target="tpu_custom_call" | custom-call | flops 503316480 | bytes 1048576 | tf_op jit(solution)/shard_map/pallas_call | solution.py:247
  6.4 0.0 copy-start
  6.4 0.0 copy-start.2
  6.4 7.3 %all-to-all-start = ((f32[32,40,128]{2,1,0:T(8,128)}), f32[32,40,128]{2,1,0:T(8,128)S(1)}, u32[]{:S(2)}, u32[]{:S(2)}) async-start(f32[32,40,128]{2,1,0:T(8,128)} %shard_map.101), calls=%async_computation | async-start | bytes 1310720 | tf_op jit(solution)/shard_map/all_to_all | solution.py:264
  13.8 0.1 pad_add_fusion.place
  13.8 0.0 copy-done
  13.8 0.0 copy-done.2
  13.8 0.9 %shard_map.100 = (bf16[256,512]{1,0:T(8,128)(2,1)S(1)}, bf16[256,512]{1,0:T(8,128)(2,1)S(1)}, bf16[128,256]{1,0:T(8,128)(2,1)S(1)}) custom-call(s32[2]{0:T(128)S(1)} %pad_add_fusion.place, f32[512,512]{1,0:T(8,128)S(1)} %copy-done, f32[4,128,128]{2,1,0:T(8,128)S(1)} %copy-done.2), custom_call_target="tpu_custom_call" | custom-call | bytes 2097152 | tf_op jit(solution)/shard_map/pallas_call | solution.py:265
  14.8 16.9 %all-to-all-done.received = f32[32,40,128]{2,1,0:T(8,128)S(1)} async-done(((f32[32,40,128]{2,1,0:T(8,128)}), f32[32,40,128]{2,1,0:T(8,128)S(1)}, u32[]{:S(2)}, u32[]{:S(2)}) %all-to-all-start) | async-done | bytes 655392 | tf_op jit(solution)/shard_map/all_to_all | solution.py:264
  31.7 3.5 %shard_map.102.vertical = f32[256,512]{1,0:T(8,128)S(1)} custom-call(f32[32,40,128]{2,1,0:T(8,128)S(1)} %all-to-all-done.received, bf16[128,256]{1,0:T(8,128)(2,1)S(1)} %get-tuple-element.14.vert_both), custom_call_target="tpu_custom_call" | custom-call | flops 2684354560 | bytes 2097152 | tf_op jit(solution)/shard_map/pallas_call | solution.py:277
  35.2 0.1 collective-permute-start
  35.3 0.4 shard_map.103.refs_2_
  35.7 0.0 copy-start.1
  35.7 1.4 %collective-permute-done.refs_3_ = f32[256,512]{1,0:T(8,128)S(1)} collective-permute-done((f32[256,512]{1,0:T(8,128)S(1)}, f32[256,512]{1,0:T(8,128)S(1)}, u32[]{:S(2)}, u32[]{:S(2)}) %collective-permute-start) | collective-permute-done | bytes 524320 | tf_op jit(solution)/shard_map/ppermute | solution.py:286
  37.1 0.4 shard_map.104
  37.5 1.4 %collective-permute-start.1 = (f32[64,512]{1,0:T(8,128)S(1)}, f32[64,512]{1,0:T(8,128)S(1)}, u32[]{:S(2)}, u32[]{:S(2)}) collective-permute-start(f32[64,512]{1,0:T(8,128)S(1)} %get-tuple-element.16), channel_id=1, source_target_pairs={{0,2},{1,3},{2,0},{3,1},{4,6},{5,7},{6,4},{7,5},{8,10},{9,11},{10,... | collective-permute-start | bytes 393224 | tf_op jit(solution)/shard_map/ppermute | solution.py:311
  38.9 1.5 %collective-permute-start.2 = (f32[64,512]{1,0:T(8,128)S(1)}, f32[64,512]{1,0:T(8,128)S(1)}, u32[]{:S(2)}, u32[]{:S(2)}) collective-permute-start(f32[64,512]{1,0:T(8,128)S(1)} %get-tuple-element.17), channel_id=1, source_target_pairs={{0,4},{1,5},{2,6},{3,7},{4,0},{5,1},{6,2},{7,3},{8,12},{9,13},{10,... | collective-permute-start | bytes 393224 | tf_op jit(solution)/shard_map/ppermute | solution.py:311
  40.4 0.6 %collective-permute-start.3 = (f32[64,512]{1,0:T(8,128)S(1)}, f32[64,512]{1,0:T(8,128)S(1)}, u32[]{:S(2)}, u32[]{:S(2)}) collective-permute-start(f32[64,512]{1,0:T(8,128)S(1)} %get-tuple-element.18), channel_id=1, source_target_pairs={{0,6},{1,7},{2,4},{3,5},{4,2},{5,3},{6,0},{7,1},{8,14},{9,15},{10,... | collective-permute-start | bytes 393224 | tf_op jit(solution)/shard_map/ppermute | solution.py:311
  41.1 2.3 %collective-permute-done.1.refs_1_ = f32[64,512]{1,0:T(8,128)S(1)} collective-permute-done((f32[64,512]{1,0:T(8,128)S(1)}, f32[64,512]{1,0:T(8,128)S(1)}, u32[]{:S(2)}, u32[]{:S(2)}) %collective-permute-start.1) | collective-permute-done | bytes 131104 | tf_op jit(solution)/shard_map/ppermute | solution.py:311
  43.4 3.8 %collective-permute-done.2.refs_2_ = f32[64,512]{1,0:T(8,128)S(1)} collective-permute-done((f32[64,512]{1,0:T(8,128)S(1)}, f32[64,512]{1,0:T(8,128)S(1)}, u32[]{:S(2)}, u32[]{:S(2)}) %collective-permute-start.2) | collective-permute-done | bytes 131104 | tf_op jit(solution)/shard_map/ppermute | solution.py:311
  47.2 0.0 collective-permute-done.3.refs_3_
  47.2 0.0 copy-done.1
  47.2 1.4 %shard_map.105 = f32[4,64,512]{2,1,0:T(8,128)} custom-call(s32[2]{0:T(128)S(1)} %pad_add_fusion.place, f32[4,64,512]{2,1,0:T(8,128)S(1)} %copy-done.1, f32[64,512]{1,0:T(8,128)S(1)} %get-tuple-element.15.refs_0_, f32[64,512]{1,0:T(8,128)S(1)} %collective-permute-done.1.refs_1_, f32[64,512]{1,0:T(8,128)S(1)} %collective-permute-done.2.refs_2_, ...), custom_call_target="tpu_custom_call" | custom-call | bytes 2097152 | tf_op jit(solution)/shard_map/pallas_call | solution.py:318
  (3 shorter events, 0.0 us)
Async XLA Ops:
  0.0 0.7 %copy-start.5 = (s32[768]{0:T(1024)S(1)}, s32[768]{0:T(1024)}, u32[]{:S(2)}) copy-start(s32[768]{0:T(1024)} %param.15) | copy-start | bytes 9220
  0.7 0.7 %copy-start.6 = (f32[768]{0:T(1024)S(1)}, f32[768]{0:T(1024)}, u32[]{:S(2)}) copy-start(f32[768]{0:T(1024)} %param.17) | copy-start | bytes 9220
  1.4 0.7 %copy-start.7 = (f32[768]{0:T(1024)S(1)}, f32[768]{0:T(1024)}, u32[]{:S(2)}) copy-start(f32[768]{0:T(1024)} %param.18) | copy-start | bytes 9220
  2.1 0.7 %copy-start.4 = (s32[768,1]{0,1:T(1,128)S(1)}, s32[768,1]{0,1:T(1,128)}, u32[]{:S(2)}) copy-start(s32[768,1]{0,1:T(1,128)} %param.13) | copy-start | bytes 9220
  2.8 1.0 %copy-start.3 = (f32[768,128]{1,0:T(8,128)S(1)}, f32[768,128]{1,0:T(8,128)}, u32[]{:S(2)}) copy-start(f32[768,128]{1,0:T(8,128)} %weights.1) | copy-start | bytes 1179652
  6.4 7.4 %copy-start = (f32[512,512]{1,0:T(8,128)S(1)}, f32[512,512]{1,0:T(8,128)}, u32[]{:S(2)}) copy-start(f32[512,512]{1,0:T(8,128)} %zonal.1) | copy-start | bytes 3145732
  6.4 7.4 %copy-start.2 = (f32[4,128,128]{2,1,0:T(8,128)S(1)}, f32[4,128,128]{2,1,0:T(8,128)}, u32[]{:S(2)}) copy-start(f32[4,128,128]{2,1,0:T(8,128)} %vert.1) | copy-start | bytes 786436
  6.4 25.2 %all-to-all-start = ((f32[32,40,128]{2,1,0:T(8,128)}), f32[32,40,128]{2,1,0:T(8,128)S(1)}, u32[]{:S(2)}, u32[]{:S(2)}) async-start(f32[32,40,128]{2,1,0:T(8,128)} %shard_map.101), calls=%async_computation | async-start | bytes 1310720 | tf_op jit(solution)/shard_map/all_to_all | solution.py:264
  35.2 2.0 %collective-permute-start = (f32[256,512]{1,0:T(8,128)S(1)}, f32[256,512]{1,0:T(8,128)S(1)}, u32[]{:S(2)}, u32[]{:S(2)}) collective-permute-start(f32[256,512]{1,0:T(8,128)S(1)} %shard_map.102.vertical), channel_id=1, source_target_pairs={{0,1},{1,0},{2,3},{3,2},{4,5},{5,4},{6,7},{7,6},{8,9},{9,8},{10,11... | collective-permute-start | bytes 1572872 | tf_op jit(solution)/shard_map/ppermute | solution.py:286
  35.7 11.5 %copy-start.1 = (f32[4,64,512]{2,1,0:T(8,128)S(1)}, f32[4,64,512]{2,1,0:T(8,128)}, u32[]{:S(2)}) copy-start(f32[4,64,512]{2,1,0:T(8,128)} %control.1) | copy-start | bytes 1572868
  37.5 5.9 %collective-permute-start.1 = (f32[64,512]{1,0:T(8,128)S(1)}, f32[64,512]{1,0:T(8,128)S(1)}, u32[]{:S(2)}, u32[]{:S(2)}) collective-permute-start(f32[64,512]{1,0:T(8,128)S(1)} %get-tuple-element.16), channel_id=1, source_target_pairs={{0,2},{1,3},{2,0},{3,1},{4,6},{5,7},{6,4},{7,5},{8,10},{9,11},{10,... | collective-permute-start | bytes 393224 | tf_op jit(solution)/shard_map/ppermute | solution.py:311
  38.9 8.2 %collective-permute-start.2 = (f32[64,512]{1,0:T(8,128)S(1)}, f32[64,512]{1,0:T(8,128)S(1)}, u32[]{:S(2)}, u32[]{:S(2)}) collective-permute-start(f32[64,512]{1,0:T(8,128)S(1)} %get-tuple-element.17), channel_id=1, source_target_pairs={{0,4},{1,5},{2,6},{3,7},{4,0},{5,1},{6,2},{7,3},{8,12},{9,13},{10,... | collective-permute-start | bytes 393224 | tf_op jit(solution)/shard_map/ppermute | solution.py:311
  40.4 6.8 %collective-permute-start.3 = (f32[64,512]{1,0:T(8,128)S(1)}, f32[64,512]{1,0:T(8,128)S(1)}, u32[]{:S(2)}, u32[]{:S(2)}) collective-permute-start(f32[64,512]{1,0:T(8,128)S(1)} %get-tuple-element.18), channel_id=1, source_target_pairs={{0,6},{1,7},{2,4},{3,5},{4,2},{5,3},{6,0},{7,1},{8,14},{9,15},{10,... | collective-permute-start | bytes 393224 | tf_op jit(solution)/shard_map/ppermute | solution.py:311

commit v2 on v0

v2 whole, which is shorter than its diff:
```python
import functools

import jax
import jax.numpy as jnp
from jax import lax
from jax.experimental import pallas as pl
from jax.experimental.pallas import tpu as pltpu
from jax.sharding import PartitionSpec as P

F = 4
LEV = 128
KW = 32
LANES = 128
SUBLANES = 8
GROUPS = LANES // KW
NEAR = 2
MIB = 1 << 20


def iota(shape, axis):
    return lax.broadcasted_iota(jnp.int32, shape, axis)


def split(x):
    high = x.astype(jnp.bfloat16)
    return high, (x - high.astype(jnp.float32)).astype(jnp.bfloat16)


def dot(a, b):
    return jnp.dot(a, b, preferred_element_type=jnp.float32)


def one_hot(labels, size):
    hit = iota((size, labels.shape[1]), 0).astype(jnp.bfloat16) == labels.astype(jnp.bfloat16)
    return jnp.where(hit, jnp.bfloat16(1), jnp.bfloat16(0))


def message_rows(capacity):
    parts = -(-capacity // KW)
    return parts, -(-(capacity + 2 * parts) // SUBLANES) * SUBLANES


def pack_kernel(members, capacity, lats, *refs):
    sources, far, near = refs[:7], refs[7 : 7 + F], refs[7 + F : 7 + F + NEAR]
    held, arrived = refs[7 + F + NEAR : -1], refs[-1]
    loads = [
        pltpu.make_async_copy(source, target, arrived.at[i])
        for i, (source, target) in enumerate(zip(sources, held))
    ]
    for load in loads:
        load.start()
    count, dest, cell, offset, departure, rinv, weights = held
    n = weights.shape[0]
    rows = far[0].shape[2]
    lons = F * members
    devices = lats * lons
    field = lax.axis_index("lon") // members
    parts, _ = message_rows(capacity)
    quads = devices // GROUPS
    chunks = n // LANES
    loads[1].wait()
    dest_row = dest[...] ^ (lax.axis_index("lat") * lons)
    hits = [
        iota((devices, LANES), 0) == dest_row[:, c * LANES : (c + 1) * LANES] for c in range(chunks)
    ]
    stacked = jnp.concatenate([hit.astype(jnp.bfloat16) for hit in hits], axis=0)
    before = (iota((LANES, 2 * LANES), 0) < iota((LANES, 2 * LANES), 1)).astype(jnp.bfloat16)
    counts = dot(stacked, before)
    carry = jnp.zeros((devices, LANES), jnp.float32)
    ranks = []
    for c in range(chunks):
        part = counts[c * devices : (c + 1) * devices]
        ranks.append(
            jnp.sum(jnp.where(hits[c], part[:, :LANES] + carry, 0.0), axis=0, keepdims=True)
        )
        carry = carry + part[:, LANES:]
    rank = jnp.concatenate(ranks, axis=1).astype(jnp.int32)
    group = dest_row & (GROUPS - 1)
    quad = dest_row >> (GROUPS.bit_length() - 1)
    slot = group * rows + rank
    lane = group * KW + (rank & (KW - 1))
    piece = rank >> (KW.bit_length() - 1)
    for i in (0, 2, 3, 4, 5):
        loads[i].wait()
    cell_row, offset_row = cell[...].reshape(1, n), offset[...].reshape(1, n)
    live = iota((1, n), 1) < count[0, 0]
    scaled = jnp.where(
        live, rinv[...].reshape(1, n) * departure[...].reshape(1, n), jnp.float32(0.0)
    )
    columns = jnp.concatenate(
        [
            scaled,
            lane.astype(jnp.float32),
            offset_row.astype(jnp.float32),
            jnp.zeros((SUBLANES - 3, n), jnp.float32),
        ],
        axis=0,
    ).T
    lane_id = iota((n, LANES), 1)
    lane_hit = (columns[:, 1:2].astype(jnp.int32) == lane_id).astype(jnp.bfloat16)
    label_rows = []
    for p in range(parts):
        for label in (cell_row, offset_row):
            mine = (iota((quads, n), 0) == quad) & (piece == p)
            label_rows.append(jnp.where(mine, label.astype(jnp.float32), 0.0))
    labels = dot(jnp.concatenate(label_rows, axis=0).astype(jnp.bfloat16), lane_hit)
    source = (lane_id & -KW) | ((lane_id - columns[:, 2:3].astype(jnp.int32)) & (KW - 1))
    loads[6].wait()
    turned = jnp.take_along_axis(weights[...], source, axis=1, mode="promise_in_bounds")
    high, low = split(turned * columns[:, 0:1])
    pieces = jnp.concatenate([high, low], axis=1)
    lane_group = iota((rows, LANES), 1) >> (KW.bit_length() - 1)
    row_id = iota((rows, LANES), 0)
    for distance in (*range(NEAR, lats), *reversed(range(NEAR))):
        for half in range(members):
            at = distance * members + half
            extra = jnp.zeros((rows, LANES), jnp.float32)
            for i in range(2 * parts):
                label = labels[i * quads + at : i * quads + at + 1]
                extra = jnp.where(row_id == capacity + i, label, extra)
            slot_hit = one_hot(jnp.where(quad == at, slot, -1), GROUPS * rows)
            both = dot(slot_hit, pieces)
            picked = both[:, :LANES] + both[:, LANES:]
            for q in range(F):
                message = extra
                for g in range(GROUPS):
                    shift = (KW * (g - (field ^ q))) & (LANES - 1)
                    turned = pltpu.roll(picked[g * rows : (g + 1) * rows], shift, 1)
                    message = jnp.where((lane_group == g) & (row_id < capacity), turned, message)
                if distance < NEAR:
                    near[distance][q, half] = message
                else:
                    far[q][distance - NEAR, half] = message


def prepare_kernel(members, lon_cols, zonal, vert, zonal_high, zonal_low, vert_both, turned):
    position = lax.axis_index("lon")
    f, h = position // members, lax.rem(position, members)
    turned[...] = zonal[...].T
    for e in range(members):
        for q in range(F):
            block = (f ^ q) * members + lax.rem(h + e, members)
            part = turned[pl.ds(pl.multiple_of(block * lon_cols, lon_cols), lon_cols), :]
            at = slice((e * F + q) * lon_cols, (e * F + q + 1) * lon_cols)
            zonal_high[at], zonal_low[at] = split(part)
    high, low = split(vert[f])
    vert_both[:, :LEV] = high
    vert_both[:, LEV:] = low


def scatter(pieces, half, capacity, columns):
    rows = pieces[0].shape[0]
    count = len(pieces)
    slots = -(-count * rows // LANES) * LANES
    parts, _ = message_rows(capacity)
    row_id, lane_id = iota((rows, LANES), 0), iota((rows, LANES), 1)
    piece_id = row_id >> (KW.bit_length() - 1)
    diagonal = ((lane_id & (KW - 1)) == (row_id & (KW - 1))) & (row_id < capacity)
    empty = jnp.where((row_id >= capacity) & ((lane_id & (KW - 1)) == 0), -1.0, 0.0)
    cells, offsets = [], []
    for piece in pieces:
        cell, offset = empty, jnp.zeros((rows, LANES), jnp.float32)
        for p in range(parts):
            mine = diagonal & (piece_id == p)
            at = capacity + 2 * p
            cell = jnp.where(mine, piece[at : at + 1], cell)
            offset = jnp.where(mine, piece[at + 1 : at + 2], offset)
        cells.append(cell)
        offsets.append(offset)
    spare = slots - count * rows
    if spare:
        pieces = pieces + [jnp.zeros((spare, LANES), jnp.float32)]
        cells.append(jnp.full((spare, LANES), -1.0, jnp.float32))
        offsets.append(jnp.zeros((spare, LANES), jnp.float32))
    values = jnp.concatenate(pieces, axis=0)
    cells = jnp.concatenate(cells, axis=0).astype(jnp.bfloat16)
    offsets = jnp.concatenate(offsets, axis=0).astype(jnp.bfloat16)
    wide = (LANES, GROUPS * LEV)
    spread = (
        iota(wide, 0) >> (KW.bit_length() - 1) == iota(wide, 1) >> (LEV.bit_length() - 1)
    ).astype(jnp.bfloat16)
    picker = (
        iota((SUBLANES, LANES), 0) == iota((SUBLANES, LANES), 1) >> (KW.bit_length() - 1)
    ).astype(jnp.bfloat16)
    cell_rows = lax.dot_general(
        picker, cells, (((1,), (1,)), ((), ())), preferred_element_type=jnp.float32
    )
    middle = iota((slots, LEV), 1).astype(jnp.float32) - (KW - 1) / 2
    sums = []
    for g in range(GROUPS):
        if g % 2 == 0:
            starts = dot(offsets, spread[:, g * LEV : (g + 2) * LEV])
        inside = jnp.abs(middle - starts[:, (g % 2) * LEV : (g % 2 + 1) * LEV]) < KW / 2
        source = g * KW + (iota((slots, LANES), 1) & (KW - 1))
        tiled = jnp.take_along_axis(values, source, axis=1, mode="promise_in_bounds")
        placed = jnp.concatenate(split(jnp.where(inside, tiled, 0.0)), axis=1)
        both = dot(one_hot(cell_rows[g : g + 1], columns), placed)
        sums.append(both[:, :LEV] + both[:, LEV:])
    return sums


def early_kernel(capacity, *refs):
    received, out = refs[:-1], refs[-1]
    halves, columns = received[0].shape[1], out.shape[1]
    for half in range(halves):
        pieces = [ref[k, half] for ref in received for k in range(ref.shape[0])]
        for g, total in enumerate(scatter(pieces, half, capacity, columns)):
            out[half * GROUPS + g] = total


def late_kernel(capacity, lon_cols, count, *refs):
    received = refs[:count]
    early, zonal_high, zonal_low, vert_both, high_out, low_out, *partials = refs[count:]
    halves, columns = received[0].shape[1], early.shape[1]
    for half in range(halves):
        pieces = [ref[k, half] for ref in received for k in range(ref.shape[0])]
        for g, total in enumerate(scatter(pieces, half, capacity, columns)):
            block = half * GROUPS + g
            adjoint_high, adjoint_low = split(early[block] + total)
            first = dot(adjoint_high, vert_both[...])
            vertical = first[:, :LEV] + first[:, LEV:] + dot(adjoint_low, vert_both[:, :LEV])
            high, low = split(vertical)
            for a in range(columns // lon_cols):
                at = slice(block * lon_cols, (block + 1) * lon_cols)
                rows = slice(a * lon_cols, (a + 1) * lon_cols)
                high_out[at, a * LEV : (a + 1) * LEV] = high[rows]
                low_out[at, a * LEV : (a + 1) * LEV] = low[rows]
    for e, partial in enumerate(partials, 1):
        partial[...] = zonal_product(e, zonal_high, zonal_low, high_out, low_out, partial.shape[0])


def zonal_product(e, zonal_high, zonal_low, high, low, size):
    at = slice(e * size, (e + 1) * size)
    first = dot(zonal_high[at], high[...]) + dot(zonal_low[at], high[...])
    return first + dot(zonal_high[at], low[...])


def own_kernel(zonal_high, zonal_low, high, low, out):
    out[...] = zonal_product(0, zonal_high, zonal_low, high, low, out.shape[0])


def sum_kernel(lon_cols, *refs):
    terms, outs = refs[:-F], refs[-F:]
    for q in range(F):
        at = slice(q * lon_cols, (q + 1) * lon_cols)
        total = terms[0][at]
        for term in terms[1:]:
            total = total + term[at]
        outs[q][...] = total


def finish_kernel(members, control, *refs):
    parts, out = refs[:F], refs[F]
    field = lax.axis_index("lon") // members
    for q in range(F):
        at = pl.ds(pl.multiple_of((field ^ q) * LEV, LEV), LEV)
        for a in range(control.shape[0]):
            out[a, :, at] = control[a, :, at] + parts[q][:, a * LEV : (a + 1) * LEV]


def call(kernel, out_shape, n_in, vmem=24, flops=0, nbytes=0, scratch=()):
    one = pl.BlockSpec(memory_space=pltpu.VMEM)
    return pl.pallas_call(
        kernel,
        out_shape=out_shape,
        in_specs=[one] * n_in,
        out_specs=[one] * len(out_shape) if isinstance(out_shape, (list, tuple)) else one,
        scratch_shapes=list(scratch),
        compiler_params=pltpu.CompilerParams(vmem_limit_bytes=vmem * MIB),
        cost_estimate=pl.CostEstimate(flops=flops, bytes_accessed=nbytes, transcendentals=0),
    )


def along_lat(x, d):
    lats = lax.axis_size("lat")
    return lax.ppermute(x, "lat", [(i, i ^ d) for i in range(lats)])


def to_field(x, q, members):
    if q == 0:
        return x
    lons = lax.axis_size("lon")
    return lax.ppermute(
        x, "lon", [(i, (i // members ^ q) * members + i % members) for i in range(lons)]
    )


def to_member(x, e, members):
    lons = lax.axis_size("lon")
    return lax.ppermute(
        x, "lon", [(i, i // members * members + (i + e) % members) for i in range(lons)]
    )


def per_device(
    control,
    vert_factor,
    zonal_factor,
    obs_dest,
    obs_cell,
    obs_offset,
    obs_count,
    departure,
    obs_rinv,
    obs_weights,
):
    lats = lax.axis_size("lat")
    lons = lax.axis_size("lon")
    devices = lats * lons
    members = lons // F
    n_obs = obs_cell.shape[0]
    capacity = max(2, 3 * n_obs // (2 * devices))
    _, rows = message_rows(capacity)
    lat_rows, lon_cols, _ = control.shape
    columns = lat_rows * lon_cols
    blocks = lons
    all_lons = lons * lon_cols
    share = F * lon_cols
    wide = lat_rows * LEV
    f32, bf16 = jnp.float32, jnp.bfloat16
    far_messages = jax.ShapeDtypeStruct((lats - NEAR, members, rows, LANES), f32)
    near_messages = jax.ShapeDtypeStruct((F, members, rows, LANES), f32)
    messages = pl.pallas_call(
        functools.partial(pack_kernel, members, capacity, lats),
        out_shape=[far_messages] * F + [near_messages] * NEAR,
        in_specs=[pl.BlockSpec(memory_space=pltpu.HBM)] * 7,
        out_specs=[pl.BlockSpec(memory_space=pltpu.VMEM)] * (F + NEAR),
        scratch_shapes=[
            pltpu.SMEM((1, 1), jnp.int32),
            pltpu.VMEM((1, n_obs), jnp.int32),
            pltpu.VMEM((n_obs,), jnp.int32),
            pltpu.VMEM((n_obs,), jnp.int32),
            pltpu.VMEM((n_obs,), f32),
            pltpu.VMEM((n_obs,), f32),
            pltpu.VMEM((n_obs, LANES), f32),
            pltpu.SemaphoreType.DMA((7,)),
        ],
        compiler_params=pltpu.CompilerParams(vmem_limit_bytes=24 * MIB),
        cost_estimate=pl.CostEstimate(
            flops=4 * devices * rows * n_obs * LANES, bytes_accessed=1 << 20, transcendentals=0
        ),
    )(
        obs_count.reshape(1, 1),
        *(
            pltpu.with_memory_space_constraint(x, pltpu.HBM)
            for x in (
                obs_dest.reshape(1, n_obs),
                obs_cell,
                obs_offset,
                departure,
                obs_rinv,
                obs_weights,
            )
        )
    )
    far = [to_field(messages[q], q, members) for q in range(F)]
    late = [
        along_lat(jnp.stack([part[k] for part in far]), d) for k, d in enumerate(range(NEAR, lats))
    ]
    near = [messages[F]] + [along_lat(messages[F + d], d) for d in range(1, NEAR)]
    near = [to_field(jnp.stack([part[q] for part in near]), q, members) for q in range(F)]
    zonal_high, zonal_low, vert_both = call(
        functools.partial(prepare_kernel, members, lon_cols),
        [
            jax.ShapeDtypeStruct((members * share, all_lons), bf16),
            jax.ShapeDtypeStruct((members * share, all_lons), bf16),
            jax.ShapeDtypeStruct((LEV, 2 * LEV), bf16),
        ],
        2,
        scratch=[pltpu.VMEM(zonal_factor.shape, f32)],
        nbytes=2 << 20,
    )(zonal_factor, vert_factor)
    early = call(
        functools.partial(early_kernel, capacity),
        jax.ShapeDtypeStruct((blocks, columns, LEV), f32),
        F,
        vmem=24,
        flops=4 * blocks * columns * NEAR * F * rows * LEV,
        nbytes=2 << 20,
    )(*near)
    partial = jax.ShapeDtypeStruct((share, wide), f32)
    half_vertical = jax.ShapeDtypeStruct((all_lons, wide), bf16)
    high, low, *partials = call(
        functools.partial(late_kernel, capacity, lon_cols, len(late)),
        [half_vertical] * 2 + [partial] * (members - 1),
        4 + len(late),
        vmem=24,
        flops=6 * members * share * all_lons * wide,
        nbytes=2 << 20,
    )(*late, early, zonal_high, zonal_low, vert_both)
    others = [to_member(partials[e - 1], e, members) for e in range(1, members)]
    own = call(
        own_kernel, partial, 4, flops=6 * share * all_lons * wide, nbytes=1 << 20
    )(zonal_high, zonal_low, high, low)
    products = call(
        functools.partial(sum_kernel, lon_cols),
        [jax.ShapeDtypeStruct((lon_cols, wide), f32)] * F,
        members,
        nbytes=1 << 20,
    )(own, *others)
    parts = [to_field(products[q], q, members) for q in range(F)]
    return call(
        functools.partial(finish_kernel, members),
        jax.ShapeDtypeStruct(control.shape, f32),
        1 + F,
        nbytes=2 << 20,
    )(control, *parts)


def solution(mesh):
    return jax.shard_map(
        per_device,
        mesh=mesh,
        in_specs=(
            P("lat", "lon", None),
            P(),
            P(),
            P(("lat", "lon"), None),
            P(("lat", "lon")),
            P(("lat", "lon")),
            P(("lat", "lon")),
            P(("lat", "lon")),
            P(("lat", "lon")),
            P(("lat", "lon"), None),
        ),
        out_specs=P("lat", "lon", None),
        check_vma=False,
    )
```

time: 99.4 us -> 42.6 us (0.43)
  the two profiles are of different devices: /device:TPU:0 before, /device:TPU:16 now
where the time goes in v2:
time: 42.6 us; the launch traced here: 42.4 us
  waiting for transfers between devices  17.1 us (40%)
  starting transfers between devices  15.5 us (36%)
  Pallas kernels  8.97 us (21%)
  between operations  0.79 us (2%)
    ppermute x9, waiting for transfers between devices, to_field(): lax.ppermute(x, 'lon', [(i, (i // members ^ q) * members + i % members) f...  11.5 us
    ppermute x9, starting transfers between devices, to_field(): lax.ppermute(x, 'lon', [(i, (i // members ^ q) * members + i % members) f...  10.7 us
    ppermute x3, starting transfers between devices, along_lat(): return lax.ppermute(x, 'lat', [(i, i ^ d) for i in range(lats)])  4.75 us
    ppermute x3, waiting for transfers between devices, along_lat(): return lax.ppermute(x, 'lat', [(i, i ^ d) for i in range(lats)])  4.26 us
    pallas_call x1, Pallas kernels, per_device(): pl.pallas_call(functools.partial(pack_kernel, members, capacity, lats), o...  2.86 us
    pallas_call x1, Pallas kernels, per_device(): call(functools.partial(late_kernel, capacity, lon_cols, len(late)), [half...  2.53 us
    pallas_call x1, Pallas kernels, per_device(): call(functools.partial(early_kernel, capacity), jax.ShapeDtypeStruct((blo...  1.57 us
    ppermute x1, waiting for transfers between devices, to_member(): lax.ppermute(x, 'lon', [(i, i // members * members + (i + e) % members) f...  1.31 us
  transfers between devices with their start and end apart: 13, of which 9 were waited for; matrix products, arithmetic and copies ran while one was open for 0% of the time, Pallas kernels for 6%

profile of v2, /device:TPU:16, one launch (start us, length us, event | category | flops | bytes accessed | tf_op | source)
XLA Modules:
  0.0 42.4 jit_solution(9295446570070680243)
XLA Ops:
  0.7 0.0 copy-start
  0.7 2.9 %shard_map.101 = (f32[2,2,40,128]{3,2,1,0:T(8,128)S(1)}, f32[2,2,40,128]{3,2,1,0:T(8,128)S(1)}, f32[2,2,40,128]{3,2,1,0:T(8,128)S(1)}, f32[2,2,40,128]{3,2,1,0:T...) custom-call(s32[1,1]{1,0:T(1,128)} %bitcast.2.refs_0_, s32[1,768]{1,0:T(1,128)} %bitcast.3, ...), custom_call_target="tpu_custom_call" | custom-call | flops 503316480 | bytes 1048576 | tf_op jit(solution)/shard_map/pallas_call | solution.py:323
  3.5 0.0 copy-start.2
  3.5 1.6 %collective-permute-start = (f32[2,2,40,128]{3,2,1,0:T(8,128)S(1)}, f32[2,2,40,128]{3,2,1,0:T(8,128)S(1)}, u32[]{:S(2)}, u32[]{:S(2)}) collective-permute-start(f32[2,2,40,128]{3,2,1,0:T(8,128)S(1)} %get-tuple-element.24), channel_id=1, source_target_pairs={{0,2},{1,3},{2,0},{3,1},{4,6},{5,7},{6,4},{7,5},{8,10},{9,11},{10,... | collective-permute-start | bytes 245768 | tf_op jit(solution)/shard_map/ppermute | solution.py:283
  5.1 1.5 %collective-permute-start.1 = (f32[2,2,40,128]{3,2,1,0:T(8,128)S(1)}, f32[2,2,40,128]{3,2,1,0:T(8,128)S(1)}, u32[]{:S(2)}, u32[]{:S(2)}) collective-permute-start(f32[2,2,40,128]{3,2,1,0:T(8,128)S(1)} %get-tuple-element.25), channel_id=1, source_target_pairs={{0,4},{1,5},{2,6},{3,7},{4,0},{5,1},{6,2},{7,3},{8,12},{9,13},{10,... | collective-permute-start | bytes 245768 | tf_op jit(solution)/shard_map/ppermute | solution.py:283
  6.6 0.5 %collective-permute-start.2 = (f32[2,2,40,128]{3,2,1,0:T(8,128)S(1)}, f32[2,2,40,128]{3,2,1,0:T(8,128)S(1)}, u32[]{:S(2)}, u32[]{:S(2)}) collective-permute-start(f32[2,2,40,128]{3,2,1,0:T(8,128)S(1)} %get-tuple-element.26), channel_id=1, source_target_pairs={{0,6},{1,7},{2,4},{3,5},{4,2},{5,3},{6,0},{7,1},{8,14},{9,15},{10,... | collective-permute-start | bytes 245768 | tf_op jit(solution)/shard_map/ppermute | solution.py:283
  7.1 1.6 %collective-permute-start.5 = (f32[4,2,40,128]{3,2,1,0:T(8,128)S(1)}, f32[4,2,40,128]{3,2,1,0:T(8,128)S(1)}, u32[]{:S(2)}, u32[]{:S(2)}) collective-permute-start(f32[4,2,40,128]{3,2,1,0:T(8,128)S(1)} %get-tuple-element.28), channel_id=1, source_target_pairs={{0,8},{8,0},{16,24},{24,16},{1,9},{9,1},{17,25},{25,17},{2,10},{10... | collective-permute-start | bytes 491528 | tf_op jit(solution)/shard_map/ppermute | solution.py:276
  8.7 0.0 copy-done
  8.7 0.0 copy-done.2
  8.7 0.5 %shard_map.100 = (bf16[512,512]{1,0:T(8,128)(2,1)S(1)}, bf16[512,512]{1,0:T(8,128)(2,1)S(1)}, bf16[128,256]{1,0:T(8,128)(2,1)S(1)}) custom-call(f32[512,512]{1,0:T(8,128)S(1)} %copy-done, f32[4,128,128]{2,1,0:T(8,128)S(1)} %copy-done.2), custom_call_target="tpu_custom_call" | custom-call | bytes 2097152 | tf_op jit(solution)/shard_map/pallas_call | solution.py:362
  9.2 0.0 collective-permute-done
  9.2 1.2 %collective-permute-done.1 = f32[2,2,40,128]{3,2,1,0:T(8,128)S(1)} collective-permute-done((f32[2,2,40,128]{3,2,1,0:T(8,128)S(1)}, f32[2,2,40,128]{3,2,1,0:T(8,128)S(1)}, u32[]{:S(2)}, u32[]{:S(2)}) %collective-permute-start.1) | collective-permute-done | bytes 81952 | tf_op jit(solution)/shard_map/ppermute | solution.py:283
  10.4 1.5 %collective-permute-done.2 = f32[2,2,40,128]{3,2,1,0:T(8,128)S(1)} collective-permute-done((f32[2,2,40,128]{3,2,1,0:T(8,128)S(1)}, f32[2,2,40,128]{3,2,1,0:T(8,128)S(1)}, u32[]{:S(2)}, u32[]{:S(2)}) %collective-permute-start.2) | collective-permute-done | bytes 81952 | tf_op jit(solution)/shard_map/ppermute | solution.py:283
  12.0 0.4 collective-permute-start.3
  12.4 2.8 %collective-permute-start.4 = (f32[4,2,40,128]{3,2,1,0:T(8,128)S(1)}, f32[4,2,40,128]{3,2,1,0:T(8,128)S(1)}, u32[]{:S(2)}, u32[]{:S(2)}) collective-permute-start(f32[4,2,40,128]{3,2,1,0:T(8,128)S(1)} %pad_maximum_fusion.1), channel_id=1, source_target_pairs={{0,24},{8,16},{16,8},{24,0},{1,25},{9,17},{17,9},{25,1},{2,26},{10... | collective-permute-start | bytes 491528 | tf_op jit(solution)/shard_map/ppermute | solution.py:276
  15.2 0.0 collective-permute-done.5
  15.2 0.6 %collective-permute-start.6 = (f32[2,2,40,128]{3,2,1,0:T(8,128)S(1)}, f32[2,2,40,128]{3,2,1,0:T(8,128)S(1)}, u32[]{:S(2)}, u32[]{:S(2)}) collective-permute-start(f32[2,2,40,128]{3,2,1,0:T(8,128)S(1)} %pad_maximum_fusion.3), channel_id=1, source_target_pairs={{0,2},{1,3},{2,0},{3,1},{4,6},{5,7},{6,4},{7,5},{8,10},{9,11},{10,... | collective-permute-start | bytes 245768 | tf_op jit(solution)/shard_map/ppermute | solution.py:283
  15.8 0.8 %collective-permute-start.7 = (f32[2,2,40,128]{3,2,1,0:T(8,128)S(1)}, f32[2,2,40,128]{3,2,1,0:T(8,128)S(1)}, u32[]{:S(2)}, u32[]{:S(2)}) collective-permute-start(f32[2,2,40,128]{3,2,1,0:T(8,128)S(1)} %pad_maximum_fusion.4), channel_id=1, source_target_pairs={{0,4},{1,5},{2,6},{3,7},{4,0},{5,1},{6,2},{7,3},{8,12},{9,13},{10,... | collective-permute-start | bytes 245768 | tf_op jit(solution)/shard_map/ppermute | solution.py:283
  16.6 2.1 %collective-permute-start.8 = (f32[2,2,40,128]{3,2,1,0:T(8,128)S(1)}, f32[2,2,40,128]{3,2,1,0:T(8,128)S(1)}, u32[]{:S(2)}, u32[]{:S(2)}) collective-permute-start(f32[2,2,40,128]{3,2,1,0:T(8,128)S(1)} %pad_maximum_fusion.5), channel_id=1, source_target_pairs={{0,6},{1,7},{2,4},{3,5},{4,2},{5,3},{6,0},{7,1},{8,14},{9,15},{10,... | collective-permute-start | bytes 245768 | tf_op jit(solution)/shard_map/ppermute | solution.py:283
  18.8 0.9 %collective-permute-done.6.refs_1_ = f32[2,2,40,128]{3,2,1,0:T(8,128)S(1)} collective-permute-done((f32[2,2,40,128]{3,2,1,0:T(8,128)S(1)}, f32[2,2,40,128]{3,2,1,0:T(8,128)S(1)}, u32[]{:S(2)}, u32[]{:S(2)}) %collective-permute-start.6) | collective-permute-done | bytes 81952 | tf_op jit(solution)/shard_map/ppermute | solution.py:283
  19.7 0.5 %collective-permute-done.7.refs_2_ = f32[2,2,40,128]{3,2,1,0:T(8,128)S(1)} collective-permute-done((f32[2,2,40,128]{3,2,1,0:T(8,128)S(1)}, f32[2,2,40,128]{3,2,1,0:T(8,128)S(1)}, u32[]{:S(2)}, u32[]{:S(2)}) %collective-permute-start.7) | collective-permute-done | bytes 81952 | tf_op jit(solution)/shard_map/ppermute | solution.py:283
  20.2 1.7 %collective-permute-done.8.refs_3_ = f32[2,2,40,128]{3,2,1,0:T(8,128)S(1)} collective-permute-done((f32[2,2,40,128]{3,2,1,0:T(8,128)S(1)}, f32[2,2,40,128]{3,2,1,0:T(8,128)S(1)}, u32[]{:S(2)}, u32[]{:S(2)}) %collective-permute-start.8) | collective-permute-done | bytes 81952 | tf_op jit(solution)/shard_map/ppermute | solution.py:283
  22.0 1.6 %shard_map.102.refs_2_ = f32[8,256,128]{2,1,0:T(8,128)S(1)} custom-call(f32[2,2,40,128]{3,2,1,0:T(8,128)S(1)} %pad_maximum_fusion.2.refs_0_, f32[2,2,40,128]{3,2,1,0:T(8,128)S(1)} %collective-permute-done.6.refs_1_, f32[2,2,40,128]{3,2,1,0:T(8,128)S(1)} %collective-permute-done.7.refs_2_, f32[2,2,40,128]{3,2,1,0:T(8,128)S(1)} %collective-permute-done.8.refs_3_), custom_call_target="tpu_custom_call" | custom-call | flops 335544320 | bytes 2097152 | tf_op jit(solution)/shard_map/pallas_call | solution.py:373
  23.5 0.0 collective-permute-done.3.refs_0_
  23.6 4.3 %collective-permute-done.4.refs_1_ = f32[4,2,40,128]{3,2,1,0:T(8,128)S(1)} collective-permute-done((f32[4,2,40,128]{3,2,1,0:T(8,128)S(1)}, f32[4,2,40,128]{3,2,1,0:T(8,128)S(1)}, u32[]{:S(2)}, u32[]{:S(2)}) %collective-permute-start.4) | collective-permute-done | bytes 163872 | tf_op jit(solution)/shard_map/ppermute | solution.py:276
  27.8 2.5 %shard_map.103 = (bf16[512,512]{1,0:T(8,128)(2,1)S(1)}, bf16[512,512]{1,0:T(8,128)(2,1)S(1)}, f32[256,512]{1,0:T(8,128)S(1)}) custom-call(f32[4,2,40,128]{3,2,1,0:T(8,128)S(1)} %collective-permute-done.3.refs_0_, f32[4,2,40,128]{3,2,1,0:T(8,128)S(1)} %collective-permute-done.4.refs_1_, f32[8,256,128]{2,1,0:T(8,128)S(1)} %shard_map.102.refs_2_, ...), custom_call_target="tpu_custom_call" | custom-call | flops 805306368 | bytes 2097152 | tf_op jit(solution)/shard_map/pallas_call | solution.py:383
  30.4 0.1 collective-permute-start.9
  30.4 0.6 %shard_map.104.refs_0_ = f32[256,512]{1,0:T(8,128)S(1)} custom-call(bf16[512,512]{1,0:T(8,128)(2,1)S(1)} %get-tuple-element.21.refs_3_.zonal_high, bf16[512,512]{1,0:T(8,128)(2,1)S(1)} %get-tuple-element.22.refs_4_.zonal_low, bf16[512,512]{1,0:T(8,128)(2,1)S(1)} %get-tuple-element.30.high, bf16[512,512]{1,0:T(8,128)(2,1)S(1)} %get-tuple-element.31.low), custom_call_target="tpu_custom_call" | custom-call | flops 402653184 | bytes 1048576 | tf_op jit(solution)/shard_map/pallas_call | solution.py:392
  31.0 0.0 copy-start.1
  31.0 1.3 %collective-permute-done.9.refs_1_ = f32[256,512]{1,0:T(8,128)S(1)} collective-permute-done((f32[256,512]{1,0:T(8,128)S(1)}, f32[256,512]{1,0:T(8,128)S(1)}, u32[]{:S(2)}, u32[]{:S(2)}) %collective-permute-start.9) | collective-permute-done | bytes 524320 | tf_op jit(solution)/shard_map/ppermute | solution.py:290
  32.3 0.1 shard_map.105
  32.4 1.1 %collective-permute-start.10 = (f32[64,512]{1,0:T(8,128)S(1)}, f32[64,512]{1,0:T(8,128)S(1)}, u32[]{:S(2)}, u32[]{:S(2)}) collective-permute-start(f32[64,512]{1,0:T(8,128)S(1)} %get-tuple-element.34), channel_id=1, source_target_pairs={{0,2},{1,3},{2,0},{3,1},{4,6},{5,7},{6,4},{7,5},{8,10},{9,11},{10,... | collective-permute-start | bytes 393224 | tf_op jit(solution)/shard_map/ppermute | solution.py:283
  33.4 0.6 %collective-permute-start.11 = (f32[64,512]{1,0:T(8,128)S(1)}, f32[64,512]{1,0:T(8,128)S(1)}, u32[]{:S(2)}, u32[]{:S(2)}) collective-permute-start(f32[64,512]{1,0:T(8,128)S(1)} %get-tuple-element.35), channel_id=1, source_target_pairs={{0,4},{1,5},{2,6},{3,7},{4,0},{5,1},{6,2},{7,3},{8,12},{9,13},{10,... | collective-permute-start | bytes 393224 | tf_op jit(solution)/shard_map/ppermute | solution.py:283
  34.1 1.9 %collective-permute-start.12 = (f32[64,512]{1,0:T(8,128)S(1)}, f32[64,512]{1,0:T(8,128)S(1)}, u32[]{:S(2)}, u32[]{:S(2)}) collective-permute-start(f32[64,512]{1,0:T(8,128)S(1)} %get-tuple-element.36), channel_id=1, source_target_pairs={{0,6},{1,7},{2,4},{3,5},{4,2},{5,3},{6,0},{7,1},{8,14},{9,15},{10,... | collective-permute-start | bytes 393224 | tf_op jit(solution)/shard_map/ppermute | solution.py:283
  35.9 2.9 %collective-permute-done.10.refs_1_ = f32[64,512]{1,0:T(8,128)S(1)} collective-permute-done((f32[64,512]{1,0:T(8,128)S(1)}, f32[64,512]{1,0:T(8,128)S(1)}, u32[]{:S(2)}, u32[]{:S(2)}) %collective-permute-start.10) | collective-permute-done | bytes 131104 | tf_op jit(solution)/shard_map/ppermute | solution.py:283
  38.8 2.7 %collective-permute-done.11.refs_2_ = f32[64,512]{1,0:T(8,128)S(1)} collective-permute-done((f32[64,512]{1,0:T(8,128)S(1)}, f32[64,512]{1,0:T(8,128)S(1)}, u32[]{:S(2)}, u32[]{:S(2)}) %collective-permute-start.11) | collective-permute-done | bytes 131104 | tf_op jit(solution)/shard_map/ppermute | solution.py:283
  41.5 0.0 collective-permute-done.12.refs_3_
  41.5 0.0 copy-done.1
  41.5 0.9 %shard_map.106 = f32[4,64,512]{2,1,0:T(8,128)} custom-call(f32[4,64,512]{2,1,0:T(8,128)S(1)} %copy-done.1, f32[64,512]{1,0:T(8,128)S(1)} %get-tuple-element.33.refs_0_, f32[64,512]{1,0:T(8,128)S(1)} %collective-permute-done.10.refs_1_, f32[64,512]{1,0:T(8,128)S(1)} %collective-permute-done.11.refs_2_, f32[64,512]{1,0:T(8,128)S(1)} %collective-permute-done.12.refs_3_), custom_call_target="tpu_custom_call" | custom-call | bytes 2097152 | tf_op jit(solution)/shard_map/pallas_call | solution.py:402
  (11 shorter events, 0.1 us)
Async XLA Ops:
  0.7 8.0 %copy-start = (f32[512,512]{1,0:T(8,128)S(1)}, f32[512,512]{1,0:T(8,128)}, u32[]{:S(2)}) copy-start(f32[512,512]{1,0:T(8,128)} %zonal.1) | copy-start | bytes 3145732
  3.5 5.2 %copy-start.2 = (f32[4,128,128]{2,1,0:T(8,128)S(1)}, f32[4,128,128]{2,1,0:T(8,128)}, u32[]{:S(2)}) copy-start(f32[4,128,128]{2,1,0:T(8,128)} %vert.1) | copy-start | bytes 786436
  3.5 5.7 %collective-permute-start = (f32[2,2,40,128]{3,2,1,0:T(8,128)S(1)}, f32[2,2,40,128]{3,2,1,0:T(8,128)S(1)}, u32[]{:S(2)}, u32[]{:S(2)}) collective-permute-start(f32[2,2,40,128]{3,2,1,0:T(8,128)S(1)} %get-tuple-element.24), channel_id=1, source_target_pairs={{0,2},{1,3},{2,0},{3,1},{4,6},{5,7},{6,4},{7,5},{8,10},{9,11},{10,... | collective-permute-start | bytes 245768 | tf_op jit(solution)/shard_map/ppermute | solution.py:283
  5.1 5.3 %collective-permute-start.1 = (f32[2,2,40,128]{3,2,1,0:T(8,128)S(1)}, f32[2,2,40,128]{3,2,1,0:T(8,128)S(1)}, u32[]{:S(2)}, u32[]{:S(2)}) collective-permute-start(f32[2,2,40,128]{3,2,1,0:T(8,128)S(1)} %get-tuple-element.25), channel_id=1, source_target_pairs={{0,4},{1,5},{2,6},{3,7},{4,0},{5,1},{6,2},{7,3},{8,12},{9,13},{10,... | collective-permute-start | bytes 245768 | tf_op jit(solution)/shard_map/ppermute | solution.py:283
  6.6 5.3 %collective-permute-start.2 = (f32[2,2,40,128]{3,2,1,0:T(8,128)S(1)}, f32[2,2,40,128]{3,2,1,0:T(8,128)S(1)}, u32[]{:S(2)}, u32[]{:S(2)}) collective-permute-start(f32[2,2,40,128]{3,2,1,0:T(8,128)S(1)} %get-tuple-element.26), channel_id=1, source_target_pairs={{0,6},{1,7},{2,4},{3,5},{4,2},{5,3},{6,0},{7,1},{8,14},{9,15},{10,... | collective-permute-start | bytes 245768 | tf_op jit(solution)/shard_map/ppermute | solution.py:283
  7.1 8.1 %collective-permute-start.5 = (f32[4,2,40,128]{3,2,1,0:T(8,128)S(1)}, f32[4,2,40,128]{3,2,1,0:T(8,128)S(1)}, u32[]{:S(2)}, u32[]{:S(2)}) collective-permute-start(f32[4,2,40,128]{3,2,1,0:T(8,128)S(1)} %get-tuple-element.28), channel_id=1, source_target_pairs={{0,8},{8,0},{16,24},{24,16},{1,9},{9,1},{17,25},{25,17},{2,10},{10... | collective-permute-start | bytes 491528 | tf_op jit(solution)/shard_map/ppermute | solution.py:276
  12.0 11.6 %collective-permute-start.3 = (f32[4,2,40,128]{3,2,1,0:T(8,128)S(1)}, f32[4,2,40,128]{3,2,1,0:T(8,128)S(1)}, u32[]{:S(2)}, u32[]{:S(2)}) collective-permute-start(f32[4,2,40,128]{3,2,1,0:T(8,128)S(1)} %pad_maximum_fusion), channel_id=1, source_target_pairs={{0,16},{8,24},{16,0},{24,8},{1,17},{9,25},{17,1},{25,9},{2,18},{10... | collective-permute-start | bytes 491528 | tf_op jit(solution)/shard_map/ppermute | solution.py:276
  12.4 15.4 %collective-permute-start.4 = (f32[4,2,40,128]{3,2,1,0:T(8,128)S(1)}, f32[4,2,40,128]{3,2,1,0:T(8,128)S(1)}, u32[]{:S(2)}, u32[]{:S(2)}) collective-permute-start(f32[4,2,40,128]{3,2,1,0:T(8,128)S(1)} %pad_maximum_fusion.1), channel_id=1, source_target_pairs={{0,24},{8,16},{16,8},{24,0},{1,25},{9,17},{17,9},{25,1},{2,26},{10... | collective-permute-start | bytes 491528 | tf_op jit(solution)/shard_map/ppermute | solution.py:276
  15.2 4.5 %collective-permute-start.6 = (f32[2,2,40,128]{3,2,1,0:T(8,128)S(1)}, f32[2,2,40,128]{3,2,1,0:T(8,128)S(1)}, u32[]{:S(2)}, u32[]{:S(2)}) collective-permute-start(f32[2,2,40,128]{3,2,1,0:T(8,128)S(1)} %pad_maximum_fusion.3), channel_id=1, source_target_pairs={{0,2},{1,3},{2,0},{3,1},{4,6},{5,7},{6,4},{7,5},{8,10},{9,11},{10,... | collective-permute-start | bytes 245768 | tf_op jit(solution)/shard_map/ppermute | solution.py:283
  15.8 4.4 %collective-permute-start.7 = (f32[2,2,40,128]{3,2,1,0:T(8,128)S(1)}, f32[2,2,40,128]{3,2,1,0:T(8,128)S(1)}, u32[]{:S(2)}, u32[]{:S(2)}) collective-permute-start(f32[2,2,40,128]{3,2,1,0:T(8,128)S(1)} %pad_maximum_fusion.4), channel_id=1, source_target_pairs={{0,4},{1,5},{2,6},{3,7},{4,0},{5,1},{6,2},{7,3},{8,12},{9,13},{10,... | collective-permute-start | bytes 245768 | tf_op jit(solution)/shard_map/ppermute | solution.py:283
  16.6 5.3 %collective-permute-start.8 = (f32[2,2,40,128]{3,2,1,0:T(8,128)S(1)}, f32[2,2,40,128]{3,2,1,0:T(8,128)S(1)}, u32[]{:S(2)}, u32[]{:S(2)}) collective-permute-start(f32[2,2,40,128]{3,2,1,0:T(8,128)S(1)} %pad_maximum_fusion.5), channel_id=1, source_target_pairs={{0,6},{1,7},{2,4},{3,5},{4,2},{5,3},{6,0},{7,1},{8,14},{9,15},{10,... | collective-permute-start | bytes 245768 | tf_op jit(solution)/shard_map/ppermute | solution.py:283
  30.4 2.0 %collective-permute-start.9 = (f32[256,512]{1,0:T(8,128)S(1)}, f32[256,512]{1,0:T(8,128)S(1)}, u32[]{:S(2)}, u32[]{:S(2)}) collective-permute-start(f32[256,512]{1,0:T(8,128)S(1)} %get-tuple-element.32), channel_id=1, source_target_pairs={{0,1},{1,0},{2,3},{3,2},{4,5},{5,4},{6,7},{7,6},{8,9},{9,8},{10,11... | collective-permute-start | bytes 1572872 | tf_op jit(solution)/shard_map/ppermute | solution.py:290
  31.0 10.5 %copy-start.1 = (f32[4,64,512]{2,1,0:T(8,128)S(1)}, f32[4,64,512]{2,1,0:T(8,128)}, u32[]{:S(2)}) copy-start(f32[4,64,512]{2,1,0:T(8,128)} %control.1) | copy-start | bytes 1572868
  32.4 6.4 %collective-permute-start.10 = (f32[64,512]{1,0:T(8,128)S(1)}, f32[64,512]{1,0:T(8,128)S(1)}, u32[]{:S(2)}, u32[]{:S(2)}) collective-permute-start(f32[64,512]{1,0:T(8,128)S(1)} %get-tuple-element.34), channel_id=1, source_target_pairs={{0,2},{1,3},{2,0},{3,1},{4,6},{5,7},{6,4},{7,5},{8,10},{9,11},{10,... | collective-permute-start | bytes 393224 | tf_op jit(solution)/shard_map/ppermute | solution.py:283
  33.4 8.1 %collective-permute-start.11 = (f32[64,512]{1,0:T(8,128)S(1)}, f32[64,512]{1,0:T(8,128)S(1)}, u32[]{:S(2)}, u32[]{:S(2)}) collective-permute-start(f32[64,512]{1,0:T(8,128)S(1)} %get-tuple-element.35), channel_id=1, source_target_pairs={{0,4},{1,5},{2,6},{3,7},{4,0},{5,1},{6,2},{7,3},{8,12},{9,13},{10,... | collective-permute-start | bytes 393224 | tf_op jit(solution)/shard_map/ppermute | solution.py:283
  34.1 7.5 %collective-permute-start.12 = (f32[64,512]{1,0:T(8,128)S(1)}, f32[64,512]{1,0:T(8,128)S(1)}, u32[]{:S(2)}, u32[]{:S(2)}) collective-permute-start(f32[64,512]{1,0:T(8,128)S(1)} %get-tuple-element.36), channel_id=1, source_target_pairs={{0,6},{1,7},{2,4},{3,5},{4,2},{5,3},{6,0},{7,1},{8,14},{9,15},{10,... | collective-permute-start | bytes 393224 | tf_op jit(solution)/shard_map/ppermute | solution.py:283

commit v3 on v2

--- a/solution.py
+++ b/solution.py
@@ -59,7 +59,9 @@
     quads = devices // GROUPS
     chunks = n // LANES
     loads[1].wait()
-    dest_row = dest[...] ^ (lax.axis_index("lat") * lons)
+    lat = lax.axis_index("lat")
+    band = dest[...] // lons ^ lat
+    dest_row = (band ^ ((band & lat & 2) >> 1)) * lons + lax.rem(dest[...], lons)
     hits = [
         iota((devices, LANES), 0) == dest_row[:, c * LANES : (c + 1) * LANES] for c in range(chunks)
     ]
@@ -111,15 +113,26 @@
     pieces = jnp.concatenate([high, low], axis=1)
     lane_group = iota((rows, LANES), 1) >> (KW.bit_length() - 1)
     row_id = iota((rows, LANES), 0)
-    for distance in (*range(NEAR, lats), *reversed(range(NEAR))):
+    size = GROUPS * rows
+    order = (*range(NEAR, lats), *reversed(range(NEAR)))
+    hits = jnp.concatenate(
+        [
+            one_hot(jnp.where(quad == distance * members + half, slot, -1), size)
+            for distance in order
+            for half in range(members)
+        ],
+        axis=0,
+    )
+    all_both = dot(hits, pieces)
+    for step, distance in enumerate(order):
         for half in range(members):
             at = distance * members + half
             extra = jnp.zeros((rows, LANES), jnp.float32)
             for i in range(2 * parts):
                 label = labels[i * quads + at : i * quads + at + 1]
                 extra = jnp.where(row_id == capacity + i, label, extra)
-            slot_hit = one_hot(jnp.where(quad == at, slot, -1), GROUPS * rows)
-            both = dot(slot_hit, pieces)
+            place = step * members + half
+            both = all_both[place * size : (place + 1) * size]
             picked = both[:, :LANES] + both[:, LANES:]
             for q in range(F):
                 message = extra
@@ -144,8 +157,10 @@
             at = slice((e * F + q) * lon_cols, (e * F + q + 1) * lon_cols)
             zonal_high[at], zonal_low[at] = split(part)
     high, low = split(vert[f])
-    vert_both[:, :LEV] = high
-    vert_both[:, LEV:] = low
+    vert_both[:LEV, :LEV] = high
+    vert_both[:LEV, LEV:] = low
+    vert_both[LEV:, :LEV] = high
+    vert_both[LEV:, LEV:] = jnp.zeros_like(low)
 
 
 def scatter(pieces, half, capacity, columns):
@@ -217,8 +232,8 @@
         for g, total in enumerate(scatter(pieces, half, capacity, columns)):
             block = half * GROUPS + g
             adjoint_high, adjoint_low = split(early[block] + total)
-            first = dot(adjoint_high, vert_both[...])
-            vertical = first[:, :LEV] + first[:, LEV:] + dot(adjoint_low, vert_both[:, :LEV])
+            both = dot(jnp.concatenate([adjoint_high, adjoint_low], axis=1), vert_both[...])
+            vertical = both[:, :LEV] + both[:, LEV:]
             high, low = split(vertical)
             for a in range(columns // lon_cols):
                 at = slice(block * lon_cols, (block + 1) * lon_cols)
@@ -273,7 +288,7 @@
 
 def along_lat(x, d):
     lats = lax.axis_size("lat")
-    return lax.ppermute(x, "lat", [(i, i ^ d) for i in range(lats)])
+    return lax.ppermute(x, "lat", [(i, i ^ d ^ ((i & d & 2) >> 1)) for i in range(lats)])
 
 
 def to_field(x, q, members):
@@ -355,7 +370,8 @@
     )
     far = [to_field(messages[q], q, members) for q in range(F)]
     late = [
-        along_lat(jnp.stack([part[k] for part in far]), d) for k, d in enumerate(range(NEAR, lats))
+        along_lat(jnp.stack([part[d - NEAR] for part in far]), d)
+        for d in reversed(range(NEAR, lats))
     ]
     near = [messages[F]] + [along_lat(messages[F + d], d) for d in range(1, NEAR)]
     near = [to_field(jnp.stack([part[q] for part in near]), q, members) for q in range(F)]
@@ -364,7 +380,7 @@
         [
             jax.ShapeDtypeStruct((members * share, all_lons), bf16),
             jax.ShapeDtypeStruct((members * share, all_lons), bf16),
-            jax.ShapeDtypeStruct((LEV, 2 * LEV), bf16),
+            jax.ShapeDtypeStruct((2 * LEV, 2 * LEV), bf16),
         ],
         2,
         scratch=[pltpu.VMEM(zonal_factor.shape, f32)],

time: 42.6 us -> 41.7 us (0.979)
  the two profiles are of different devices: /device:TPU:16 before, /device:TPU:0 now
where the time goes in v3:
time: 41.7 us; the launch traced here: 41.6 us
  starting transfers between devices  17.5 us (42%)
  waiting for transfers between devices  14.3 us (34%)
  Pallas kernels  8.89 us (21%)
  between operations  0.81 us (2%)
    ppermute x9, starting transfers between devices, to_field(): lax.ppermute(x, 'lon', [(i, (i // members ^ q) * members + i % members) f...  11.7 us
    ppermute x9, waiting for transfers between devices, to_field(): lax.ppermute(x, 'lon', [(i, (i // members ^ q) * members + i % members) f...  11.6 us
    ppermute x3, starting transfers between devices, along_lat(): lax.ppermute(x, 'lat', [(i, i ^ d ^ (i & d & 2) >> 1) for i in range(lats)])  5.74 us
    pallas_call x1, Pallas kernels, per_device(): pl.pallas_call(functools.partial(pack_kernel, members, capacity, lats), o...  2.96 us
    pallas_call x1, Pallas kernels, per_device(): call(functools.partial(late_kernel, capacity, lon_cols, len(late)), [half...  2.34 us
    pallas_call x1, Pallas kernels, per_device(): call(functools.partial(early_kernel, capacity), jax.ShapeDtypeStruct((blo...  1.57 us
    ppermute x3, waiting for transfers between devices, along_lat(): lax.ppermute(x, 'lat', [(i, i ^ d ^ (i & d & 2) >> 1) for i in range(lats)])  1.43 us
    ppermute x1, waiting for transfers between devices, to_member(): lax.ppermute(x, 'lon', [(i, i // members * members + (i + e) % members) f...  1.31 us
  transfers between devices with their start and end apart: 13, of which 9 were waited for; matrix products, arithmetic and copies ran while one was open for 0% of the time, Pallas kernels for 6%

profile of v3, /device:TPU:0, one launch (start us, length us, event | category | flops | bytes accessed | tf_op | source)
XLA Modules:
  0.0 41.6 jit_solution(11140264571419605087)
XLA Ops:
  0.7 0.0 copy-start
  0.7 3.0 %shard_map.101 = (f32[2,2,40,128]{3,2,1,0:T(8,128)S(1)}, f32[2,2,40,128]{3,2,1,0:T(8,128)S(1)}, f32[2,2,40,128]{3,2,1,0:T(8,128)S(1)}, f32[2,2,40,128]{3,2,1,0:T...) custom-call(s32[1,1]{1,0:T(1,128)} %bitcast.2.refs_0_, s32[1,768]{1,0:T(1,128)} %bitcast.3, ...), custom_call_target="tpu_custom_call" | custom-call | flops 503316480 | bytes 1048576 | tf_op jit(solution)/shard_map/pallas_call | solution.py:338
  3.6 0.0 copy-start.2
  3.6 3.0 %collective-permute-start = (f32[2,2,40,128]{3,2,1,0:T(8,128)S(1)}, f32[2,2,40,128]{3,2,1,0:T(8,128)S(1)}, u32[]{:S(2)}, u32[]{:S(2)}) collective-permute-start(f32[2,2,40,128]{3,2,1,0:T(8,128)S(1)} %get-tuple-element.24), channel_id=1, source_target_pairs={{0,2},{1,3},{2,0},{3,1},{4,6},{5,7},{6,4},{7,5},{8,10},{9,11},{10,... | collective-permute-start | bytes 245768 | tf_op jit(solution)/shard_map/ppermute | solution.py:298
  6.6 1.5 %collective-permute-start.1 = (f32[2,2,40,128]{3,2,1,0:T(8,128)S(1)}, f32[2,2,40,128]{3,2,1,0:T(8,128)S(1)}, u32[]{:S(2)}, u32[]{:S(2)}) collective-permute-start(f32[2,2,40,128]{3,2,1,0:T(8,128)S(1)} %get-tuple-element.25), channel_id=1, source_target_pairs={{0,4},{1,5},{2,6},{3,7},{4,0},{5,1},{6,2},{7,3},{8,12},{9,13},{10,... | collective-permute-start | bytes 245768 | tf_op jit(solution)/shard_map/ppermute | solution.py:298
  8.2 0.0 collective-permute-start.2
  8.2 2.0 %collective-permute-start.5 = (f32[4,2,40,128]{3,2,1,0:T(8,128)S(1)}, f32[4,2,40,128]{3,2,1,0:T(8,128)S(1)}, u32[]{:S(2)}, u32[]{:S(2)}) collective-permute-start(f32[4,2,40,128]{3,2,1,0:T(8,128)S(1)} %get-tuple-element.28), channel_id=1, source_target_pairs={{0,8},{8,0},{16,24},{24,16},{1,9},{9,1},{17,25},{25,17},{2,10},{10... | collective-permute-start | bytes 491528 | tf_op jit(solution)/shard_map/ppermute | solution.py:291
  10.2 0.0 copy-done
  10.3 0.0 copy-done.2
  10.3 0.5 %shard_map.100 = (bf16[512,512]{1,0:T(8,128)(2,1)S(1)}, bf16[512,512]{1,0:T(8,128)(2,1)S(1)}, bf16[256,256]{1,0:T(8,128)(2,1)S(1)}) custom-call(f32[512,512]{1,0:T(8,128)S(1)} %copy-done, f32[4,128,128]{2,1,0:T(8,128)S(1)} %copy-done.2), custom_call_target="tpu_custom_call" | custom-call | bytes 2097152 | tf_op jit(solution)/shard_map/pallas_call | solution.py:378
  10.8 0.0 collective-permute-done
  10.8 1.2 %collective-permute-done.1 = f32[2,2,40,128]{3,2,1,0:T(8,128)S(1)} collective-permute-done((f32[2,2,40,128]{3,2,1,0:T(8,128)S(1)}, f32[2,2,40,128]{3,2,1,0:T(8,128)S(1)}, u32[]{:S(2)}, u32[]{:S(2)}) %collective-permute-start.1) | collective-permute-done | bytes 81952 | tf_op jit(solution)/shard_map/ppermute | solution.py:298
  12.0 1.5 %collective-permute-done.2 = f32[2,2,40,128]{3,2,1,0:T(8,128)S(1)} collective-permute-done((f32[2,2,40,128]{3,2,1,0:T(8,128)S(1)}, f32[2,2,40,128]{3,2,1,0:T(8,128)S(1)}, u32[]{:S(2)}, u32[]{:S(2)}) %collective-permute-start.2) | collective-permute-done | bytes 81952 | tf_op jit(solution)/shard_map/ppermute | solution.py:298
  13.5 3.7 %collective-permute-start.3 = (f32[4,2,40,128]{3,2,1,0:T(8,128)S(1)}, f32[4,2,40,128]{3,2,1,0:T(8,128)S(1)}, u32[]{:S(2)}, u32[]{:S(2)}) collective-permute-start(f32[4,2,40,128]{3,2,1,0:T(8,128)S(1)} %pad_maximum_fusion), channel_id=1, source_target_pairs={{0,24},{8,16},{16,0},{24,8},{1,25},{9,17},{17,1},{25,9},{2,26},{10... | collective-permute-start | bytes 491528 | tf_op jit(solution)/shard_map/ppermute | solution.py:291
  17.2 0.1 collective-permute-start.4
  17.3 0.0 collective-permute-done.5
  17.3 0.6 %collective-permute-start.6 = (f32[2,2,40,128]{3,2,1,0:T(8,128)S(1)}, f32[2,2,40,128]{3,2,1,0:T(8,128)S(1)}, u32[]{:S(2)}, u32[]{:S(2)}) collective-permute-start(f32[2,2,40,128]{3,2,1,0:T(8,128)S(1)} %pad_maximum_fusion.3), channel_id=1, source_target_pairs={{0,2},{1,3},{2,0},{3,1},{4,6},{5,7},{6,4},{7,5},{8,10},{9,11},{10,... | collective-permute-start | bytes 245768 | tf_op jit(solution)/shard_map/ppermute | solution.py:298
  17.9 0.7 %collective-permute-start.7 = (f32[2,2,40,128]{3,2,1,0:T(8,128)S(1)}, f32[2,2,40,128]{3,2,1,0:T(8,128)S(1)}, u32[]{:S(2)}, u32[]{:S(2)}) collective-permute-start(f32[2,2,40,128]{3,2,1,0:T(8,128)S(1)} %pad_maximum_fusion.4), channel_id=1, source_target_pairs={{0,4},{1,5},{2,6},{3,7},{4,0},{5,1},{6,2},{7,3},{8,12},{9,13},{10,... | collective-permute-start | bytes 245768 | tf_op jit(solution)/shard_map/ppermute | solution.py:298
  18.7 2.2 %collective-permute-start.8 = (f32[2,2,40,128]{3,2,1,0:T(8,128)S(1)}, f32[2,2,40,128]{3,2,1,0:T(8,128)S(1)}, u32[]{:S(2)}, u32[]{:S(2)}) collective-permute-start(f32[2,2,40,128]{3,2,1,0:T(8,128)S(1)} %pad_maximum_fusion.5), channel_id=1, source_target_pairs={{0,6},{1,7},{2,4},{3,5},{4,2},{5,3},{6,0},{7,1},{8,14},{9,15},{10,... | collective-permute-start | bytes 245768 | tf_op jit(solution)/shard_map/ppermute | solution.py:298
  20.9 0.9 %collective-permute-done.6.refs_1_ = f32[2,2,40,128]{3,2,1,0:T(8,128)S(1)} collective-permute-done((f32[2,2,40,128]{3,2,1,0:T(8,128)S(1)}, f32[2,2,40,128]{3,2,1,0:T(8,128)S(1)}, u32[]{:S(2)}, u32[]{:S(2)}) %collective-permute-start.6) | collective-permute-done | bytes 81952 | tf_op jit(solution)/shard_map/ppermute | solution.py:298
  21.8 0.5 %collective-permute-done.7.refs_2_ = f32[2,2,40,128]{3,2,1,0:T(8,128)S(1)} collective-permute-done((f32[2,2,40,128]{3,2,1,0:T(8,128)S(1)}, f32[2,2,40,128]{3,2,1,0:T(8,128)S(1)}, u32[]{:S(2)}, u32[]{:S(2)}) %collective-permute-start.7) | collective-permute-done | bytes 81952 | tf_op jit(solution)/shard_map/ppermute | solution.py:298
  22.4 1.6 %collective-permute-done.8.refs_3_ = f32[2,2,40,128]{3,2,1,0:T(8,128)S(1)} collective-permute-done((f32[2,2,40,128]{3,2,1,0:T(8,128)S(1)}, f32[2,2,40,128]{3,2,1,0:T(8,128)S(1)}, u32[]{:S(2)}, u32[]{:S(2)}) %collective-permute-start.8) | collective-permute-done | bytes 81952 | tf_op jit(solution)/shard_map/ppermute | solution.py:298
  24.0 1.6 %shard_map.102.refs_2_ = f32[8,256,128]{2,1,0:T(8,128)S(1)} custom-call(f32[2,2,40,128]{3,2,1,0:T(8,128)S(1)} %pad_maximum_fusion.2.refs_0_, f32[2,2,40,128]{3,2,1,0:T(8,128)S(1)} %collective-permute-done.6.refs_1_, f32[2,2,40,128]{3,2,1,0:T(8,128)S(1)} %collective-permute-done.7.refs_2_, f32[2,2,40,128]{3,2,1,0:T(8,128)S(1)} %collective-permute-done.8.refs_3_), custom_call_target="tpu_custom_call" | custom-call | flops 335544320 | bytes 2097152 | tf_op jit(solution)/shard_map/pallas_call | solution.py:389
  25.6 1.4 %collective-permute-done.3.refs_0_ = f32[4,2,40,128]{3,2,1,0:T(8,128)S(1)} collective-permute-done((f32[4,2,40,128]{3,2,1,0:T(8,128)S(1)}, f32[4,2,40,128]{3,2,1,0:T(8,128)S(1)}, u32[]{:S(2)}, u32[]{:S(2)}) %collective-permute-start.3) | collective-permute-done | bytes 163872 | tf_op jit(solution)/shard_map/ppermute | solution.py:291
  27.0 0.0 collective-permute-done.4.refs_1_
  27.0 2.3 %shard_map.103 = (bf16[512,512]{1,0:T(8,128)(2,1)S(1)}, bf16[512,512]{1,0:T(8,128)(2,1)S(1)}, f32[256,512]{1,0:T(8,128)S(1)}) custom-call(f32[4,2,40,128]{3,2,1,0:T(8,128)S(1)} %collective-permute-done.3.refs_0_, f32[4,2,40,128]{3,2,1,0:T(8,128)S(1)} %collective-permute-done.4.refs_1_, f32[8,256,128]{2,1,0:T(8,128)S(1)} %shard_map.102.refs_2_, ...), custom_call_target="tpu_custom_call" | custom-call | flops 805306368 | bytes 2097152 | tf_op jit(solution)/shard_map/pallas_call | solution.py:399
  29.4 0.1 collective-permute-start.9
  29.4 0.6 %shard_map.104.refs_0_ = f32[256,512]{1,0:T(8,128)S(1)} custom-call(bf16[512,512]{1,0:T(8,128)(2,1)S(1)} %get-tuple-element.21.refs_3_.zonal_high, bf16[512,512]{1,0:T(8,128)(2,1)S(1)} %get-tuple-element.22.refs_4_.zonal_low, bf16[512,512]{1,0:T(8,128)(2,1)S(1)} %get-tuple-element.30.high, bf16[512,512]{1,0:T(8,128)(2,1)S(1)} %get-tuple-element.31.low), custom_call_target="tpu_custom_call" | custom-call | flops 402653184 | bytes 1048576 | tf_op jit(solution)/shard_map/pallas_call | solution.py:408
  30.0 0.0 copy-start.1
  30.0 1.3 %collective-permute-done.9.refs_1_ = f32[256,512]{1,0:T(8,128)S(1)} collective-permute-done((f32[256,512]{1,0:T(8,128)S(1)}, f32[256,512]{1,0:T(8,128)S(1)}, u32[]{:S(2)}, u32[]{:S(2)}) %collective-permute-start.9) | collective-permute-done | bytes 524320 | tf_op jit(solution)/shard_map/ppermute | solution.py:305
  31.3 0.1 shard_map.105
  31.4 1.2 %collective-permute-start.10 = (f32[64,512]{1,0:T(8,128)S(1)}, f32[64,512]{1,0:T(8,128)S(1)}, u32[]{:S(2)}, u32[]{:S(2)}) collective-permute-start(f32[64,512]{1,0:T(8,128)S(1)} %get-tuple-element.34), channel_id=1, source_target_pairs={{0,2},{1,3},{2,0},{3,1},{4,6},{5,7},{6,4},{7,5},{8,10},{9,11},{10,... | collective-permute-start | bytes 393224 | tf_op jit(solution)/shard_map/ppermute | solution.py:298
  32.6 1.0 %collective-permute-start.11 = (f32[64,512]{1,0:T(8,128)S(1)}, f32[64,512]{1,0:T(8,128)S(1)}, u32[]{:S(2)}, u32[]{:S(2)}) collective-permute-start(f32[64,512]{1,0:T(8,128)S(1)} %get-tuple-element.35), channel_id=1, source_target_pairs={{0,4},{1,5},{2,6},{3,7},{4,0},{5,1},{6,2},{7,3},{8,12},{9,13},{10,... | collective-permute-start | bytes 393224 | tf_op jit(solution)/shard_map/ppermute | solution.py:298
  33.6 1.4 %collective-permute-start.12 = (f32[64,512]{1,0:T(8,128)S(1)}, f32[64,512]{1,0:T(8,128)S(1)}, u32[]{:S(2)}, u32[]{:S(2)}) collective-permute-start(f32[64,512]{1,0:T(8,128)S(1)} %get-tuple-element.36), channel_id=1, source_target_pairs={{0,6},{1,7},{2,4},{3,5},{4,2},{5,3},{6,0},{7,1},{8,14},{9,15},{10,... | collective-permute-start | bytes 393224 | tf_op jit(solution)/shard_map/ppermute | solution.py:298
  34.9 2.8 %collective-permute-done.10.refs_1_ = f32[64,512]{1,0:T(8,128)S(1)} collective-permute-done((f32[64,512]{1,0:T(8,128)S(1)}, f32[64,512]{1,0:T(8,128)S(1)}, u32[]{:S(2)}, u32[]{:S(2)}) %collective-permute-start.10) | collective-permute-done | bytes 131104 | tf_op jit(solution)/shard_map/ppermute | solution.py:298
  37.7 3.0 %collective-permute-done.11.refs_2_ = f32[64,512]{1,0:T(8,128)S(1)} collective-permute-done((f32[64,512]{1,0:T(8,128)S(1)}, f32[64,512]{1,0:T(8,128)S(1)}, u32[]{:S(2)}, u32[]{:S(2)}) %collective-permute-start.11) | collective-permute-done | bytes 131104 | tf_op jit(solution)/shard_map/ppermute | solution.py:298
  40.7 0.0 collective-permute-done.12.refs_3_
  40.7 0.0 copy-done.1
  40.7 0.9 %shard_map.106 = f32[4,64,512]{2,1,0:T(8,128)} custom-call(f32[4,64,512]{2,1,0:T(8,128)S(1)} %copy-done.1, f32[64,512]{1,0:T(8,128)S(1)} %get-tuple-element.33.refs_0_, f32[64,512]{1,0:T(8,128)S(1)} %collective-permute-done.10.refs_1_, f32[64,512]{1,0:T(8,128)S(1)} %collective-permute-done.11.refs_2_, f32[64,512]{1,0:T(8,128)S(1)} %collective-permute-done.12.refs_3_), custom_call_target="tpu_custom_call" | custom-call | bytes 2097152 | tf_op jit(solution)/shard_map/pallas_call | solution.py:418
  (11 shorter events, 0.1 us)
Async XLA Ops:
  0.7 9.6 %copy-start = (f32[512,512]{1,0:T(8,128)S(1)}, f32[512,512]{1,0:T(8,128)}, u32[]{:S(2)}) copy-start(f32[512,512]{1,0:T(8,128)} %zonal.1) | copy-start | bytes 3145732
  3.6 6.6 %copy-start.2 = (f32[4,128,128]{2,1,0:T(8,128)S(1)}, f32[4,128,128]{2,1,0:T(8,128)}, u32[]{:S(2)}) copy-start(f32[4,128,128]{2,1,0:T(8,128)} %vert.1) | copy-start | bytes 786436
  3.6 7.1 %collective-permute-start = (f32[2,2,40,128]{3,2,1,0:T(8,128)S(1)}, f32[2,2,40,128]{3,2,1,0:T(8,128)S(1)}, u32[]{:S(2)}, u32[]{:S(2)}) collective-permute-start(f32[2,2,40,128]{3,2,1,0:T(8,128)S(1)} %get-tuple-element.24), channel_id=1, source_target_pairs={{0,2},{1,3},{2,0},{3,1},{4,6},{5,7},{6,4},{7,5},{8,10},{9,11},{10,... | collective-permute-start | bytes 245768 | tf_op jit(solution)/shard_map/ppermute | solution.py:298
  6.6 5.3 %collective-permute-start.1 = (f32[2,2,40,128]{3,2,1,0:T(8,128)S(1)}, f32[2,2,40,128]{3,2,1,0:T(8,128)S(1)}, u32[]{:S(2)}, u32[]{:S(2)}) collective-permute-start(f32[2,2,40,128]{3,2,1,0:T(8,128)S(1)} %get-tuple-element.25), channel_id=1, source_target_pairs={{0,4},{1,5},{2,6},{3,7},{4,0},{5,1},{6,2},{7,3},{8,12},{9,13},{10,... | collective-permute-start | bytes 245768 | tf_op jit(solution)/shard_map/ppermute | solution.py:298
  8.2 5.3 %collective-permute-start.2 = (f32[2,2,40,128]{3,2,1,0:T(8,128)S(1)}, f32[2,2,40,128]{3,2,1,0:T(8,128)S(1)}, u32[]{:S(2)}, u32[]{:S(2)}) collective-permute-start(f32[2,2,40,128]{3,2,1,0:T(8,128)S(1)} %get-tuple-element.26), channel_id=1, source_target_pairs={{0,6},{1,7},{2,4},{3,5},{4,2},{5,3},{6,0},{7,1},{8,14},{9,15},{10,... | collective-permute-start | bytes 245768 | tf_op jit(solution)/shard_map/ppermute | solution.py:298
  8.2 9.1 %collective-permute-start.5 = (f32[4,2,40,128]{3,2,1,0:T(8,128)S(1)}, f32[4,2,40,128]{3,2,1,0:T(8,128)S(1)}, u32[]{:S(2)}, u32[]{:S(2)}) collective-permute-start(f32[4,2,40,128]{3,2,1,0:T(8,128)S(1)} %get-tuple-element.28), channel_id=1, source_target_pairs={{0,8},{8,0},{16,24},{24,16},{1,9},{9,1},{17,25},{25,17},{2,10},{10... | collective-permute-start | bytes 491528 | tf_op jit(solution)/shard_map/ppermute | solution.py:291
  13.5 13.5 %collective-permute-start.3 = (f32[4,2,40,128]{3,2,1,0:T(8,128)S(1)}, f32[4,2,40,128]{3,2,1,0:T(8,128)S(1)}, u32[]{:S(2)}, u32[]{:S(2)}) collective-permute-start(f32[4,2,40,128]{3,2,1,0:T(8,128)S(1)} %pad_maximum_fusion), channel_id=1, source_target_pairs={{0,24},{8,16},{16,0},{24,8},{1,25},{9,17},{17,1},{25,9},{2,26},{10... | collective-permute-start | bytes 491528 | tf_op jit(solution)/shard_map/ppermute | solution.py:291
  17.2 9.8 %collective-permute-start.4 = (f32[4,2,40,128]{3,2,1,0:T(8,128)S(1)}, f32[4,2,40,128]{3,2,1,0:T(8,128)S(1)}, u32[]{:S(2)}, u32[]{:S(2)}) collective-permute-start(f32[4,2,40,128]{3,2,1,0:T(8,128)S(1)} %pad_maximum_fusion.1), channel_id=1, source_target_pairs={{0,16},{8,24},{16,8},{24,0},{1,17},{9,25},{17,9},{25,1},{2,18},{10... | collective-permute-start | bytes 491528 | tf_op jit(solution)/shard_map/ppermute | solution.py:291
  17.3 4.5 %collective-permute-start.6 = (f32[2,2,40,128]{3,2,1,0:T(8,128)S(1)}, f32[2,2,40,128]{3,2,1,0:T(8,128)S(1)}, u32[]{:S(2)}, u32[]{:S(2)}) collective-permute-start(f32[2,2,40,128]{3,2,1,0:T(8,128)S(1)} %pad_maximum_fusion.3), channel_id=1, source_target_pairs={{0,2},{1,3},{2,0},{3,1},{4,6},{5,7},{6,4},{7,5},{8,10},{9,11},{10,... | collective-permute-start | bytes 245768 | tf_op jit(solution)/shard_map/ppermute | solution.py:298
  17.9 4.4 %collective-permute-start.7 = (f32[2,2,40,128]{3,2,1,0:T(8,128)S(1)}, f32[2,2,40,128]{3,2,1,0:T(8,128)S(1)}, u32[]{:S(2)}, u32[]{:S(2)}) collective-permute-start(f32[2,2,40,128]{3,2,1,0:T(8,128)S(1)} %pad_maximum_fusion.4), channel_id=1, source_target_pairs={{0,4},{1,5},{2,6},{3,7},{4,0},{5,1},{6,2},{7,3},{8,12},{9,13},{10,... | collective-permute-start | bytes 245768 | tf_op jit(solution)/shard_map/ppermute | solution.py:298
  18.7 5.3 %collective-permute-start.8 = (f32[2,2,40,128]{3,2,1,0:T(8,128)S(1)}, f32[2,2,40,128]{3,2,1,0:T(8,128)S(1)}, u32[]{:S(2)}, u32[]{:S(2)}) collective-permute-start(f32[2,2,40,128]{3,2,1,0:T(8,128)S(1)} %pad_maximum_fusion.5), channel_id=1, source_target_pairs={{0,6},{1,7},{2,4},{3,5},{4,2},{5,3},{6,0},{7,1},{8,14},{9,15},{10,... | collective-permute-start | bytes 245768 | tf_op jit(solution)/shard_map/ppermute | solution.py:298
  29.4 2.0 %collective-permute-start.9 = (f32[256,512]{1,0:T(8,128)S(1)}, f32[256,512]{1,0:T(8,128)S(1)}, u32[]{:S(2)}, u32[]{:S(2)}) collective-permute-start(f32[256,512]{1,0:T(8,128)S(1)} %get-tuple-element.32), channel_id=1, source_target_pairs={{0,1},{1,0},{2,3},{3,2},{4,5},{5,4},{6,7},{7,6},{8,9},{9,8},{10,11... | collective-permute-start | bytes 1572872 | tf_op jit(solution)/shard_map/ppermute | solution.py:305
  30.0 10.7 %copy-start.1 = (f32[4,64,512]{2,1,0:T(8,128)S(1)}, f32[4,64,512]{2,1,0:T(8,128)}, u32[]{:S(2)}) copy-start(f32[4,64,512]{2,1,0:T(8,128)} %control.1) | copy-start | bytes 1572868
  31.4 6.3 %collective-permute-start.10 = (f32[64,512]{1,0:T(8,128)S(1)}, f32[64,512]{1,0:T(8,128)S(1)}, u32[]{:S(2)}, u32[]{:S(2)}) collective-permute-start(f32[64,512]{1,0:T(8,128)S(1)} %get-tuple-element.34), channel_id=1, source_target_pairs={{0,2},{1,3},{2,0},{3,1},{4,6},{5,7},{6,4},{7,5},{8,10},{9,11},{10,... | collective-permute-start | bytes 393224 | tf_op jit(solution)/shard_map/ppermute | solution.py:298
  32.6 8.1 %collective-permute-start.11 = (f32[64,512]{1,0:T(8,128)S(1)}, f32[64,512]{1,0:T(8,128)S(1)}, u32[]{:S(2)}, u32[]{:S(2)}) collective-permute-start(f32[64,512]{1,0:T(8,128)S(1)} %get-tuple-element.35), channel_id=1, source_target_pairs={{0,4},{1,5},{2,6},{3,7},{4,0},{5,1},{6,2},{7,3},{8,12},{9,13},{10,... | collective-permute-start | bytes 393224 | tf_op jit(solution)/shard_map/ppermute | solution.py:298
  33.6 7.1 %collective-permute-start.12 = (f32[64,512]{1,0:T(8,128)S(1)}, f32[64,512]{1,0:T(8,128)S(1)}, u32[]{:S(2)}, u32[]{:S(2)}) collective-permute-start(f32[64,512]{1,0:T(8,128)S(1)} %get-tuple-element.36), channel_id=1, source_target_pairs={{0,6},{1,7},{2,4},{3,5},{4,2},{5,3},{6,0},{7,1},{8,14},{9,15},{10,... | collective-permute-start | bytes 393224 | tf_op jit(solution)/shard_map/ppermute | solution.py:298

commit v4 on v3

--- a/solution.py
+++ b/solution.py
@@ -42,7 +42,7 @@
 
 def pack_kernel(members, capacity, lats, *refs):
     sources, far, near = refs[:7], refs[7 : 7 + F], refs[7 + F : 7 + F + NEAR]
-    held, arrived = refs[7 + F + NEAR : -1], refs[-1]
+    held, by_field, arrived = refs[7 + F + NEAR : -2], refs[-2], refs[-1]
     loads = [
         pltpu.make_async_copy(source, target, arrived.at[i])
         for i, (source, target) in enumerate(zip(sources, held))
@@ -111,9 +111,11 @@
     turned = jnp.take_along_axis(weights[...], source, axis=1, mode="promise_in_bounds")
     high, low = split(turned * columns[:, 0:1])
     pieces = jnp.concatenate([high, low], axis=1)
-    lane_group = iota((rows, LANES), 1) >> (KW.bit_length() - 1)
-    row_id = iota((rows, LANES), 0)
+    even = iota((rows, LANES), 1) & KW == 0
+    lower = iota((rows, LANES), 1) < LANES // 2
     size = GROUPS * rows
+    tail = capacity // SUBLANES * SUBLANES
+    row_id = iota((rows - tail, LANES), 0) + tail
     order = (*range(NEAR, lats), *reversed(range(NEAR)))
     hits = jnp.concatenate(
         [
@@ -123,27 +125,39 @@
         ],
         axis=0,
     )
-    all_both = dot(hits, pieces)
+    both = dot(hits, pieces)
     for step, distance in enumerate(order):
         for half in range(members):
-            at = distance * members + half
-            extra = jnp.zeros((rows, LANES), jnp.float32)
+            at = (step * members + half) * size
+            picked = both[at : at + size, :LANES] + both[at : at + size, LANES:]
+            blocks = [picked[g * rows : (g + 1) * rows] for g in range(GROUPS)]
+            pairs = [
+                part
+                for i in (0, 2)
+                for part in (
+                    jnp.where(even, blocks[i], pltpu.roll(blocks[i + 1], KW, 1)),
+                    jnp.where(even, pltpu.roll(blocks[i], LANES - KW, 1), blocks[i + 1]),
+                )
+            ]
+            fields = [
+                jnp.where(lower, pairs[0], pltpu.roll(pairs[2], LANES // 2, 1)),
+                jnp.where(lower, pairs[1], pltpu.roll(pairs[3], LANES // 2, 1)),
+                jnp.where(lower, pltpu.roll(pairs[0], LANES // 2, 1), pairs[2]),
+                jnp.where(lower, pltpu.roll(pairs[1], LANES // 2, 1), pairs[3]),
+            ]
+            extra = jnp.zeros((rows - tail, LANES), jnp.float32)
             for i in range(2 * parts):
-                label = labels[i * quads + at : i * quads + at + 1]
-                extra = jnp.where(row_id == capacity + i, label, extra)
-            place = step * members + half
-            both = all_both[place * size : (place + 1) * size]
-            picked = both[:, :LANES] + both[:, LANES:]
-            for q in range(F):
-                message = extra
-                for g in range(GROUPS):
-                    shift = (KW * (g - (field ^ q))) & (LANES - 1)
-                    turned = pltpu.roll(picked[g * rows : (g + 1) * rows], shift, 1)
-                    message = jnp.where((lane_group == g) & (row_id < capacity), turned, message)
+                k = i * quads + distance * members + half
+                extra = jnp.where(row_id == capacity + i, labels[k : k + 1], extra)
+            for f in range(F):
+                message = jnp.concatenate([fields[f][:tail], fields[f][tail:] + extra], axis=0)
                 if distance < NEAR:
-                    near[distance][q, half] = message
+                    near[distance][field ^ f, half] = message
                 else:
-                    far[q][distance - NEAR, half] = message
+                    by_field[distance - NEAR, half, f] = message
+            if distance >= NEAR:
+                for q in range(F):
+                    far[q][distance - NEAR, half] = by_field[distance - NEAR, half, field ^ q]
 
 
 def prepare_kernel(members, lon_cols, zonal, vert, zonal_high, zonal_low, vert_both, turned):
@@ -172,7 +186,7 @@
     piece_id = row_id >> (KW.bit_length() - 1)
     diagonal = ((lane_id & (KW - 1)) == (row_id & (KW - 1))) & (row_id < capacity)
     empty = jnp.where((row_id >= capacity) & ((lane_id & (KW - 1)) == 0), -1.0, 0.0)
-    cells, offsets = [], []
+    labels = []
     for piece in pieces:
         cell, offset = empty, jnp.zeros((rows, LANES), jnp.float32)
         for p in range(parts):
@@ -180,36 +194,40 @@
             at = capacity + 2 * p
             cell = jnp.where(mine, piece[at : at + 1], cell)
             offset = jnp.where(mine, piece[at + 1 : at + 2], offset)
-        cells.append(cell)
-        offsets.append(offset)
+        labels.append(jnp.concatenate([cell, offset], axis=1))
     spare = slots - count * rows
     if spare:
         pieces = pieces + [jnp.zeros((spare, LANES), jnp.float32)]
-        cells.append(jnp.full((spare, LANES), -1.0, jnp.float32))
-        offsets.append(jnp.zeros((spare, LANES), jnp.float32))
-    values = jnp.concatenate(pieces, axis=0)
-    cells = jnp.concatenate(cells, axis=0).astype(jnp.bfloat16)
-    offsets = jnp.concatenate(offsets, axis=0).astype(jnp.bfloat16)
-    wide = (LANES, GROUPS * LEV)
-    spread = (
-        iota(wide, 0) >> (KW.bit_length() - 1) == iota(wide, 1) >> (LEV.bit_length() - 1)
+        labels.append(jnp.full((spare, 2 * LANES), -1.0, jnp.float32))
+    picker = (
+        iota((2 * GROUPS, 2 * LANES), 0) == iota((2 * GROUPS, 2 * LANES), 1) >> (KW.bit_length() - 1)
     ).astype(jnp.bfloat16)
-    picker = (
-        iota((SUBLANES, LANES), 0) == iota((SUBLANES, LANES), 1) >> (KW.bit_length() - 1)
+    along = (((1,), (1,)), ((), ()))
+    label_rows = lax.dot_general(
+        picker,
+        jnp.concatenate(labels, axis=0).astype(jnp.bfloat16),
+        along,
+        preferred_element_type=jnp.float32,
     ).astype(jnp.bfloat16)
-    cell_rows = lax.dot_general(
-        picker, cells, (((1,), (1,)), ((), ())), preferred_element_type=jnp.float32
-    )
-    middle = iota((slots, LEV), 1).astype(jnp.float32) - (KW - 1) / 2
+    high, low = split(jnp.concatenate(pieces, axis=0).T)
+    middle = iota((LEV, slots), 0).astype(jnp.bfloat16) - jnp.bfloat16((KW - 1) / 2)
     sums = []
     for g in range(GROUPS):
-        if g % 2 == 0:
-            starts = dot(offsets, spread[:, g * LEV : (g + 2) * LEV])
-        inside = jnp.abs(middle - starts[:, (g % 2) * LEV : (g % 2 + 1) * LEV]) < KW / 2
-        source = g * KW + (iota((slots, LANES), 1) & (KW - 1))
-        tiled = jnp.take_along_axis(values, source, axis=1, mode="promise_in_bounds")
-        placed = jnp.concatenate(split(jnp.where(inside, tiled, 0.0)), axis=1)
-        both = dot(one_hot(cell_rows[g : g + 1], columns), placed)
+        at = slice(g * KW, (g + 1) * KW)
+        inside = jnp.abs(middle - label_rows[GROUPS + g : GROUPS + g + 1]) < jnp.bfloat16(KW / 2)
+        placed = jnp.concatenate(
+            [
+                jnp.where(inside, jnp.concatenate([piece[at]] * (LEV // KW), axis=0), jnp.bfloat16(0))
+                for piece in (high, low)
+            ],
+            axis=0,
+        )
+        both = lax.dot_general(
+            one_hot(label_rows[g : g + 1], columns),
+            placed,
+            along,
+            preferred_element_type=jnp.float32,
+        )
         sums.append(both[:, :LEV] + both[:, LEV:])
     return sums
 
@@ -264,13 +282,20 @@
         outs[q][...] = total
 
 
-def finish_kernel(members, control, *refs):
-    parts, out = refs[:F], refs[F]
+def finish_kernel(members, distances, *refs):
+    count = len(distances)
+    control, parts = refs[0], refs[1 : 1 + count]
+    out, held, sent = refs[-3:]
     field = lax.axis_index("lon") // members
-    for q in range(F):
+    copies = []
+    for i, q in enumerate(distances):
         at = pl.ds(pl.multiple_of((field ^ q) * LEV, LEV), LEV)
         for a in range(control.shape[0]):
-            out[a, :, at] = control[a, :, at] + parts[q][:, a * LEV : (a + 1) * LEV]
+            held[i, a] = control[a, :, at] + parts[i][:, a * LEV : (a + 1) * LEV]
+        copies.append(pltpu.make_async_copy(held.at[i], out.at[:, :, at], sent.at[i]))
+        copies[-1].start()
+    for copy in copies:
+        copy.wait()
 
 
 def call(kernel, out_shape, n_in, vmem=24, flops=0, nbytes=0, scratch=()):
@@ -348,6 +373,7 @@
             pltpu.VMEM((n_obs,), f32),
             pltpu.VMEM((n_obs,), f32),
             pltpu.VMEM((n_obs, LANES), f32),
+            pltpu.VMEM((lats - NEAR, members, F, rows, LANES), f32),
             pltpu.SemaphoreType.DMA((7,)),
         ],
         compiler_params=pltpu.CompilerParams(vmem_limit_bytes=24 * MIB),
@@ -368,12 +394,13 @@
             )
         )
     )
-    far = [to_field(messages[q], q, members) for q in range(F)]
+    far, near = list(messages[:F]), list(messages[F:])
+    far = [to_field(far[q], q, members) for q in range(F)]
     late = [
         along_lat(jnp.stack([part[d - NEAR] for part in far]), d)
         for d in reversed(range(NEAR, lats))
     ]
-    near = [messages[F]] + [along_lat(messages[F + d], d) for d in range(1, NEAR)]
+    near = near[:1] + [along_lat(near[d], d) for d in range(1, NEAR)]
     near = [to_field(jnp.stack([part[q] for part in near]), q, members) for q in range(F)]
     zonal_high, zonal_low, vert_both = call(
         functools.partial(prepare_kernel, members, lon_cols),
@@ -415,12 +442,28 @@
         nbytes=1 << 20,
     )(own, *others)
     parts = [to_field(products[q], q, members) for q in range(F)]
-    return call(
-        functools.partial(finish_kernel, members),
-        jax.ShapeDtypeStruct(control.shape, f32),
-        1 + F,
-        nbytes=2 << 20,
-    )(control, *parts)
+    out = ()
+    for distances in ((0, 1), (2, 3)):
+        count = len(distances)
+        out = (
+            pl.pallas_call(
+                functools.partial(finish_kernel, members, distances),
+                out_shape=jax.ShapeDtypeStruct(control.shape, f32),
+                in_specs=[pl.BlockSpec(memory_space=pltpu.VMEM)] * (1 + count)
+                + [pl.BlockSpec(memory_space=pltpu.HBM)] * len(out),
+                out_specs=pl.BlockSpec(memory_space=pltpu.HBM),
+                scratch_shapes=[
+                    pltpu.VMEM((count, lat_rows, lon_cols, LEV), f32),
+                    pltpu.SemaphoreType.DMA((count,)),
+                ],
+                input_output_aliases={1 + count: 0} if out else {},
+                compiler_params=pltpu.CompilerParams(vmem_limit_bytes=24 * MIB),
+                cost_estimate=pl.CostEstimate(
+                    flops=0, bytes_accessed=count << 19, transcendentals=0
+                ),
+            )(control, *(parts[q] for q in distances), *out),
+        )
+    return out[0]
 
 
 def solution(mesh):

time: 41.7 us -> 40.8 us (0.978)
  Pallas kernels: 8.89 us -> 8.35 us
    ppermute x9, waiting for transfers between devices: 11.6 us -> 10.8 us  [to_field(): lax.ppermute(x, 'lon', [(i, (i // members ^ q) * members + i % members) f...]
    pallas_call x1 -> x2, Pallas kernels: 0.9 us -> 1.51 us  [per_device(): pl.pallas_call(functools.partial(finish_kernel, members, distances), out_...]
    pallas_call x1, Pallas kernels: 2.34 us -> 1.9 us  [per_device(): call(functools.partial(late_kernel, capacity, lon_cols, len(late)), [half...]
  transfers between devices with their start and end apart: 13 -> 13, of which waited for: 9 -> 9; matrix products, arithmetic and copies ran while one was open for 0% -> 0% of each run, Pallas kernels for 6% -> 7%
where the time goes in v4:
time: 40.8 us; the launch traced here: 40.7 us
  starting transfers between devices  17.4 us (43%)
  waiting for transfers between devices  14 us (34%)
  Pallas kernels  8.35 us (20%)
  between operations  0.82 us (2%)
    ppermute x9, starting transfers between devices, to_field(): lax.ppermute(x, 'lon', [(i, (i // members ^ q) * members + i % members) f...  11.6 us
    ppermute x9, waiting for transfers between devices, to_field(): lax.ppermute(x, 'lon', [(i, (i // members ^ q) * members + i % members) f...  10.8 us
    ppermute x3, starting transfers between devices, along_lat(): lax.ppermute(x, 'lat', [(i, i ^ d ^ (i & d & 2) >> 1) for i in range(lats)])  5.74 us
    pallas_call x1, Pallas kernels, per_device(): pl.pallas_call(functools.partial(pack_kernel, members, capacity, lats), o...  2.65 us
    pallas_call x1, Pallas kernels, per_device(): call(functools.partial(late_kernel, capacity, lon_cols, len(late)), [half...  1.9 us
    ppermute x3, waiting for transfers between devices, along_lat(): lax.ppermute(x, 'lat', [(i, i ^ d ^ (i & d & 2) >> 1) for i in range(lats)])  1.84 us
    pallas_call x2, Pallas kernels, per_device(): pl.pallas_call(functools.partial(finish_kernel, members, distances), out_...  1.51 us
    ppermute x1, waiting for transfers between devices, to_member(): lax.ppermute(x, 'lon', [(i, i // members * members + (i + e) % members) f...  1.31 us
  transfers between devices with their start and end apart: 13, of which 9 were waited for; matrix products, arithmetic and copies ran while one was open for 0% of the time, Pallas kernels for 7%

profile of v4, /device:TPU:0, one launch (start us, length us, event | category | flops | bytes accessed | tf_op | source)
XLA Modules:
  0.0 40.7 jit_solution(4399460558703517300)
XLA Ops:
  0.7 0.0 copy-start.1
  0.7 2.6 %shard_map.101 = (f32[2,2,40,128]{3,2,1,0:T(8,128)S(1)}, f32[2,2,40,128]{3,2,1,0:T(8,128)S(1)}, f32[2,2,40,128]{3,2,1,0:T(8,128)S(1)}, f32[2,2,40,128]{3,2,1,0:T...) custom-call(s32[1,1]{1,0:T(1,128)} %bitcast.2.refs_0_, s32[1,768]{1,0:T(1,128)} %bitcast.3, ...), custom_call_target="tpu_custom_call" | custom-call | flops 503316480 | bytes 1048576 | tf_op jit(solution)/shard_map/pallas_call | solution.py:363
  3.3 0.0 copy-start.2
  3.3 3.0 %collective-permute-start = (f32[2,2,40,128]{3,2,1,0:T(8,128)S(1)}, f32[2,2,40,128]{3,2,1,0:T(8,128)S(1)}, u32[]{:S(2)}, u32[]{:S(2)}) collective-permute-start(f32[2,2,40,128]{3,2,1,0:T(8,128)S(1)} %get-tuple-element.24), channel_id=1, source_target_pairs={{0,2},{1,3},{2,0},{3,1},{4,6},{5,7},{6,4},{7,5},{8,10},{9,11},{10,... | collective-permute-start | bytes 245768 | tf_op jit(solution)/shard_map/ppermute | solution.py:323
  6.3 1.5 %collective-permute-start.1 = (f32[2,2,40,128]{3,2,1,0:T(8,128)S(1)}, f32[2,2,40,128]{3,2,1,0:T(8,128)S(1)}, u32[]{:S(2)}, u32[]{:S(2)}) collective-permute-start(f32[2,2,40,128]{3,2,1,0:T(8,128)S(1)} %get-tuple-element.25), channel_id=1, source_target_pairs={{0,4},{1,5},{2,6},{3,7},{4,0},{5,1},{6,2},{7,3},{8,12},{9,13},{10,... | collective-permute-start | bytes 245768 | tf_op jit(solution)/shard_map/ppermute | solution.py:323
  7.8 0.0 collective-permute-start.2
  7.9 2.0 %collective-permute-start.5 = (f32[4,2,40,128]{3,2,1,0:T(8,128)S(1)}, f32[4,2,40,128]{3,2,1,0:T(8,128)S(1)}, u32[]{:S(2)}, u32[]{:S(2)}) collective-permute-start(f32[4,2,40,128]{3,2,1,0:T(8,128)S(1)} %get-tuple-element.28), channel_id=1, source_target_pairs={{0,8},{8,0},{16,24},{24,16},{1,9},{9,1},{17,25},{25,17},{2,10},{10... | collective-permute-start | bytes 491528 | tf_op jit(solution)/shard_map/ppermute | solution.py:316
  9.9 0.0 copy-done.1
  9.9 0.0 copy-done.2
  9.9 0.5 %shard_map.100 = (bf16[512,512]{1,0:T(8,128)(2,1)S(1)}, bf16[512,512]{1,0:T(8,128)(2,1)S(1)}, bf16[256,256]{1,0:T(8,128)(2,1)S(1)}) custom-call(f32[512,512]{1,0:T(8,128)S(1)} %copy-done.1, f32[4,128,128]{2,1,0:T(8,128)S(1)} %copy-done.2), custom_call_target="tpu_custom_call" | custom-call | bytes 2097152 | tf_op jit(solution)/shard_map/pallas_call | solution.py:405
  10.4 0.0 collective-permute-done
  10.5 1.2 %collective-permute-done.1 = f32[2,2,40,128]{3,2,1,0:T(8,128)S(1)} collective-permute-done((f32[2,2,40,128]{3,2,1,0:T(8,128)S(1)}, f32[2,2,40,128]{3,2,1,0:T(8,128)S(1)}, u32[]{:S(2)}, u32[]{:S(2)}) %collective-permute-start.1) | collective-permute-done | bytes 81952 | tf_op jit(solution)/shard_map/ppermute | solution.py:323
  11.7 1.5 %collective-permute-done.2 = f32[2,2,40,128]{3,2,1,0:T(8,128)S(1)} collective-permute-done((f32[2,2,40,128]{3,2,1,0:T(8,128)S(1)}, f32[2,2,40,128]{3,2,1,0:T(8,128)S(1)}, u32[]{:S(2)}, u32[]{:S(2)}) %collective-permute-start.2) | collective-permute-done | bytes 81952 | tf_op jit(solution)/shard_map/ppermute | solution.py:323
  13.2 3.6 %collective-permute-start.3 = (f32[4,2,40,128]{3,2,1,0:T(8,128)S(1)}, f32[4,2,40,128]{3,2,1,0:T(8,128)S(1)}, u32[]{:S(2)}, u32[]{:S(2)}) collective-permute-start(f32[4,2,40,128]{3,2,1,0:T(8,128)S(1)} %pad_maximum_fusion), channel_id=1, source_target_pairs={{0,24},{8,16},{16,0},{24,8},{1,25},{9,17},{17,1},{25,9},{2,26},{10... | collective-permute-start | bytes 491528 | tf_op jit(solution)/shard_map/ppermute | solution.py:316
  16.9 0.1 collective-permute-start.4
  16.9 0.0 collective-permute-done.5
  17.0 0.6 %collective-permute-start.6 = (f32[2,2,40,128]{3,2,1,0:T(8,128)S(1)}, f32[2,2,40,128]{3,2,1,0:T(8,128)S(1)}, u32[]{:S(2)}, u32[]{:S(2)}) collective-permute-start(f32[2,2,40,128]{3,2,1,0:T(8,128)S(1)} %pad_maximum_fusion.3), channel_id=1, source_target_pairs={{0,2},{1,3},{2,0},{3,1},{4,6},{5,7},{6,4},{7,5},{8,10},{9,11},{10,... | collective-permute-start | bytes 245768 | tf_op jit(solution)/shard_map/ppermute | solution.py:323
  17.6 0.7 %collective-permute-start.7 = (f32[2,2,40,128]{3,2,1,0:T(8,128)S(1)}, f32[2,2,40,128]{3,2,1,0:T(8,128)S(1)}, u32[]{:S(2)}, u32[]{:S(2)}) collective-permute-start(f32[2,2,40,128]{3,2,1,0:T(8,128)S(1)} %pad_maximum_fusion.4), channel_id=1, source_target_pairs={{0,4},{1,5},{2,6},{3,7},{4,0},{5,1},{6,2},{7,3},{8,12},{9,13},{10,... | collective-permute-start | bytes 245768 | tf_op jit(solution)/shard_map/ppermute | solution.py:323
  18.3 2.2 %collective-permute-start.8 = (f32[2,2,40,128]{3,2,1,0:T(8,128)S(1)}, f32[2,2,40,128]{3,2,1,0:T(8,128)S(1)}, u32[]{:S(2)}, u32[]{:S(2)}) collective-permute-start(f32[2,2,40,128]{3,2,1,0:T(8,128)S(1)} %pad_maximum_fusion.5), channel_id=1, source_target_pairs={{0,6},{1,7},{2,4},{3,5},{4,2},{5,3},{6,0},{7,1},{8,14},{9,15},{10,... | collective-permute-start | bytes 245768 | tf_op jit(solution)/shard_map/ppermute | solution.py:323
  20.6 0.9 %collective-permute-done.6.refs_1_ = f32[2,2,40,128]{3,2,1,0:T(8,128)S(1)} collective-permute-done((f32[2,2,40,128]{3,2,1,0:T(8,128)S(1)}, f32[2,2,40,128]{3,2,1,0:T(8,128)S(1)}, u32[]{:S(2)}, u32[]{:S(2)}) %collective-permute-start.6) | collective-permute-done | bytes 81952 | tf_op jit(solution)/shard_map/ppermute | solution.py:323
  21.5 0.5 %collective-permute-done.7.refs_2_ = f32[2,2,40,128]{3,2,1,0:T(8,128)S(1)} collective-permute-done((f32[2,2,40,128]{3,2,1,0:T(8,128)S(1)}, f32[2,2,40,128]{3,2,1,0:T(8,128)S(1)}, u32[]{:S(2)}, u32[]{:S(2)}) %collective-permute-start.7) | collective-permute-done | bytes 81952 | tf_op jit(solution)/shard_map/ppermute | solution.py:323
  22.0 1.6 %collective-permute-done.8.refs_3_ = f32[2,2,40,128]{3,2,1,0:T(8,128)S(1)} collective-permute-done((f32[2,2,40,128]{3,2,1,0:T(8,128)S(1)}, f32[2,2,40,128]{3,2,1,0:T(8,128)S(1)}, u32[]{:S(2)}, u32[]{:S(2)}) %collective-permute-start.8) | collective-permute-done | bytes 81952 | tf_op jit(solution)/shard_map/ppermute | solution.py:323
  23.7 1.2 %shard_map.102.refs_2_ = f32[8,256,128]{2,1,0:T(8,128)S(1)} custom-call(f32[2,2,40,128]{3,2,1,0:T(8,128)S(1)} %pad_maximum_fusion.2.refs_0_, f32[2,2,40,128]{3,2,1,0:T(8,128)S(1)} %collective-permute-done.6.refs_1_, f32[2,2,40,128]{3,2,1,0:T(8,128)S(1)} %collective-permute-done.7.refs_2_, f32[2,2,40,128]{3,2,1,0:T(8,128)S(1)} %collective-permute-done.8.refs_3_), custom_call_target="tpu_custom_call" | custom-call | flops 335544320 | bytes 2097152 | tf_op jit(solution)/shard_map/pallas_call | solution.py:416
  24.9 1.8 %collective-permute-done.3.refs_0_ = f32[4,2,40,128]{3,2,1,0:T(8,128)S(1)} collective-permute-done((f32[4,2,40,128]{3,2,1,0:T(8,128)S(1)}, f32[4,2,40,128]{3,2,1,0:T(8,128)S(1)}, u32[]{:S(2)}, u32[]{:S(2)}) %collective-permute-start.3) | collective-permute-done | bytes 163872 | tf_op jit(solution)/shard_map/ppermute | solution.py:316
  26.7 0.0 collective-permute-done.4.refs_1_
  26.7 1.9 %shard_map.103 = (bf16[512,512]{1,0:T(8,128)(2,1)S(1)}, bf16[512,512]{1,0:T(8,128)(2,1)S(1)}, f32[256,512]{1,0:T(8,128)S(1)}) custom-call(f32[4,2,40,128]{3,2,1,0:T(8,128)S(1)} %collective-permute-done.3.refs_0_, f32[4,2,40,128]{3,2,1,0:T(8,128)S(1)} %collective-permute-done.4.refs_1_, f32[8,256,128]{2,1,0:T(8,128)S(1)} %shard_map.102.refs_2_, ...), custom_call_target="tpu_custom_call" | custom-call | flops 805306368 | bytes 2097152 | tf_op jit(solution)/shard_map/pallas_call | solution.py:426
  28.6 0.1 collective-permute-start.9
  28.7 0.6 %shard_map.104.refs_0_ = f32[256,512]{1,0:T(8,128)S(1)} custom-call(bf16[512,512]{1,0:T(8,128)(2,1)S(1)} %get-tuple-element.21.refs_3_.zonal_high, bf16[512,512]{1,0:T(8,128)(2,1)S(1)} %get-tuple-element.22.refs_4_.zonal_low, bf16[512,512]{1,0:T(8,128)(2,1)S(1)} %get-tuple-element.30.high, bf16[512,512]{1,0:T(8,128)(2,1)S(1)} %get-tuple-element.31.low), custom_call_target="tpu_custom_call" | custom-call | flops 402653184 | bytes 1048576 | tf_op jit(solution)/shard_map/pallas_call | solution.py:435
  29.3 0.0 copy-start
  29.3 1.3 %collective-permute-done.9.refs_1_ = f32[256,512]{1,0:T(8,128)S(1)} collective-permute-done((f32[256,512]{1,0:T(8,128)S(1)}, f32[256,512]{1,0:T(8,128)S(1)}, u32[]{:S(2)}, u32[]{:S(2)}) %collective-permute-start.9) | collective-permute-done | bytes 524320 | tf_op jit(solution)/shard_map/ppermute | solution.py:330
  30.6 0.1 shard_map.105
  30.6 1.2 %collective-permute-start.12 = (f32[64,512]{1,0:T(8,128)S(1)}, f32[64,512]{1,0:T(8,128)S(1)}, u32[]{:S(2)}, u32[]{:S(2)}) collective-permute-start(f32[64,512]{1,0:T(8,128)S(1)} %get-tuple-element.36), channel_id=1, source_target_pairs={{0,2},{1,3},{2,0},{3,1},{4,6},{5,7},{6,4},{7,5},{8,10},{9,11},{10,... | collective-permute-start | bytes 393224 | tf_op jit(solution)/shard_map/ppermute | solution.py:323
  31.9 1.0 %collective-permute-start.10 = (f32[64,512]{1,0:T(8,128)S(1)}, f32[64,512]{1,0:T(8,128)S(1)}, u32[]{:S(2)}, u32[]{:S(2)}) collective-permute-start(f32[64,512]{1,0:T(8,128)S(1)} %get-tuple-element.33), channel_id=1, source_target_pairs={{0,4},{1,5},{2,6},{3,7},{4,0},{5,1},{6,2},{7,3},{8,12},{9,13},{10,... | collective-permute-start | bytes 393224 | tf_op jit(solution)/shard_map/ppermute | solution.py:323
  32.9 1.3 %collective-permute-start.11 = (f32[64,512]{1,0:T(8,128)S(1)}, f32[64,512]{1,0:T(8,128)S(1)}, u32[]{:S(2)}, u32[]{:S(2)}) collective-permute-start(f32[64,512]{1,0:T(8,128)S(1)} %get-tuple-element.34), channel_id=1, source_target_pairs={{0,6},{1,7},{2,4},{3,5},{4,2},{5,3},{6,0},{7,1},{8,14},{9,15},{10,... | collective-permute-start | bytes 393224 | tf_op jit(solution)/shard_map/ppermute | solution.py:323
  34.2 2.8 %collective-permute-done.12.refs_2_ = f32[64,512]{1,0:T(8,128)S(1)} collective-permute-done((f32[64,512]{1,0:T(8,128)S(1)}, f32[64,512]{1,0:T(8,128)S(1)}, u32[]{:S(2)}, u32[]{:S(2)}) %collective-permute-start.12) | collective-permute-done | bytes 131104 | tf_op jit(solution)/shard_map/ppermute | solution.py:323
  36.9 0.0 copy-done
  37.0 0.8 %shard_map.106.refs_3_ = f32[4,64,512]{2,1,0:T(8,128)} custom-call(f32[4,64,512]{2,1,0:T(8,128)S(1)} %copy-done, f32[64,512]{1,0:T(8,128)S(1)} %get-tuple-element.35.refs_1_, f32[64,512]{1,0:T(8,128)S(1)} %collective-permute-done.12.refs_2_), custom_call_target="tpu_custom_call" | custom-call | bytes 1048576 | tf_op jit(solution)/shard_map/pallas_call | solution.py:449
  37.7 2.2 %collective-permute-done.10.refs_1_ = f32[64,512]{1,0:T(8,128)S(1)} collective-permute-done((f32[64,512]{1,0:T(8,128)S(1)}, f32[64,512]{1,0:T(8,128)S(1)}, u32[]{:S(2)}, u32[]{:S(2)}) %collective-permute-start.10) | collective-permute-done | bytes 131104 | tf_op jit(solution)/shard_map/ppermute | solution.py:323
  39.9 0.0 collective-permute-done.11.refs_2_
  39.9 0.8 %shard_map.107 = f32[4,64,512]{2,1,0:T(8,128)} custom-call(f32[4,64,512]{2,1,0:T(8,128)S(1)} %copy-done, f32[64,512]{1,0:T(8,128)S(1)} %collective-permute-done.10.refs_1_, f32[64,512]{1,0:T(8,128)S(1)} %collective-permute-done.11.refs_2_, f32[4,64,512]{2,1,0:T(8,128)} %shard_map.106.refs_3_), custom_call_target="tpu_custom_call", output_to_operand_aliasing={{}: (3, {})} | custom-call | bytes 1048576 | tf_op jit(solution)/shard_map/pallas_call | solution.py:449
  (11 shorter events, 0.1 us)
Async XLA Ops:
  0.7 9.3 %copy-start.1 = (f32[512,512]{1,0:T(8,128)S(1)}, f32[512,512]{1,0:T(8,128)}, u32[]{:S(2)}) copy-start(f32[512,512]{1,0:T(8,128)} %zonal.1) | copy-start | bytes 3145732
  3.3 6.6 %copy-start.2 = (f32[4,128,128]{2,1,0:T(8,128)S(1)}, f32[4,128,128]{2,1,0:T(8,128)}, u32[]{:S(2)}) copy-start(f32[4,128,128]{2,1,0:T(8,128)} %vert.1) | copy-start | bytes 786436
  3.3 7.1 %collective-permute-start = (f32[2,2,40,128]{3,2,1,0:T(8,128)S(1)}, f32[2,2,40,128]{3,2,1,0:T(8,128)S(1)}, u32[]{:S(2)}, u32[]{:S(2)}) collective-permute-start(f32[2,2,40,128]{3,2,1,0:T(8,128)S(1)} %get-tuple-element.24), channel_id=1, source_target_pairs={{0,2},{1,3},{2,0},{3,1},{4,6},{5,7},{6,4},{7,5},{8,10},{9,11},{10,... | collective-permute-start | bytes 245768 | tf_op jit(solution)/shard_map/ppermute | solution.py:323
  6.3 5.3 %collective-permute-start.1 = (f32[2,2,40,128]{3,2,1,0:T(8,128)S(1)}, f32[2,2,40,128]{3,2,1,0:T(8,128)S(1)}, u32[]{:S(2)}, u32[]{:S(2)}) collective-permute-start(f32[2,2,40,128]{3,2,1,0:T(8,128)S(1)} %get-tuple-element.25), channel_id=1, source_target_pairs={{0,4},{1,5},{2,6},{3,7},{4,0},{5,1},{6,2},{7,3},{8,12},{9,13},{10,... | collective-permute-start | bytes 245768 | tf_op jit(solution)/shard_map/ppermute | solution.py:323
  7.8 5.3 %collective-permute-start.2 = (f32[2,2,40,128]{3,2,1,0:T(8,128)S(1)}, f32[2,2,40,128]{3,2,1,0:T(8,128)S(1)}, u32[]{:S(2)}, u32[]{:S(2)}) collective-permute-start(f32[2,2,40,128]{3,2,1,0:T(8,128)S(1)} %get-tuple-element.26), channel_id=1, source_target_pairs={{0,6},{1,7},{2,4},{3,5},{4,2},{5,3},{6,0},{7,1},{8,14},{9,15},{10,... | collective-permute-start | bytes 245768 | tf_op jit(solution)/shard_map/ppermute | solution.py:323
  7.9 9.1 %collective-permute-start.5 = (f32[4,2,40,128]{3,2,1,0:T(8,128)S(1)}, f32[4,2,40,128]{3,2,1,0:T(8,128)S(1)}, u32[]{:S(2)}, u32[]{:S(2)}) collective-permute-start(f32[4,2,40,128]{3,2,1,0:T(8,128)S(1)} %get-tuple-element.28), channel_id=1, source_target_pairs={{0,8},{8,0},{16,24},{24,16},{1,9},{9,1},{17,25},{25,17},{2,10},{10... | collective-permute-start | bytes 491528 | tf_op jit(solution)/shard_map/ppermute | solution.py:316
  13.2 13.5 %collective-permute-start.3 = (f32[4,2,40,128]{3,2,1,0:T(8,128)S(1)}, f32[4,2,40,128]{3,2,1,0:T(8,128)S(1)}, u32[]{:S(2)}, u32[]{:S(2)}) collective-permute-start(f32[4,2,40,128]{3,2,1,0:T(8,128)S(1)} %pad_maximum_fusion), channel_id=1, source_target_pairs={{0,24},{8,16},{16,0},{24,8},{1,25},{9,17},{17,1},{25,9},{2,26},{10... | collective-permute-start | bytes 491528 | tf_op jit(solution)/shard_map/ppermute | solution.py:316
  16.9 9.8 %collective-permute-start.4 = (f32[4,2,40,128]{3,2,1,0:T(8,128)S(1)}, f32[4,2,40,128]{3,2,1,0:T(8,128)S(1)}, u32[]{:S(2)}, u32[]{:S(2)}) collective-permute-start(f32[4,2,40,128]{3,2,1,0:T(8,128)S(1)} %pad_maximum_fusion.1), channel_id=1, source_target_pairs={{0,16},{8,24},{16,8},{24,0},{1,17},{9,25},{17,9},{25,1},{2,18},{10... | collective-permute-start | bytes 491528 | tf_op jit(solution)/shard_map/ppermute | solution.py:316
  17.0 4.5 %collective-permute-start.6 = (f32[2,2,40,128]{3,2,1,0:T(8,128)S(1)}, f32[2,2,40,128]{3,2,1,0:T(8,128)S(1)}, u32[]{:S(2)}, u32[]{:S(2)}) collective-permute-start(f32[2,2,40,128]{3,2,1,0:T(8,128)S(1)} %pad_maximum_fusion.3), channel_id=1, source_target_pairs={{0,2},{1,3},{2,0},{3,1},{4,6},{5,7},{6,4},{7,5},{8,10},{9,11},{10,... | collective-permute-start | bytes 245768 | tf_op jit(solution)/shard_map/ppermute | solution.py:323
  17.6 4.4 %collective-permute-start.7 = (f32[2,2,40,128]{3,2,1,0:T(8,128)S(1)}, f32[2,2,40,128]{3,2,1,0:T(8,128)S(1)}, u32[]{:S(2)}, u32[]{:S(2)}) collective-permute-start(f32[2,2,40,128]{3,2,1,0:T(8,128)S(1)} %pad_maximum_fusion.4), channel_id=1, source_target_pairs={{0,4},{1,5},{2,6},{3,7},{4,0},{5,1},{6,2},{7,3},{8,12},{9,13},{10,... | collective-permute-start | bytes 245768 | tf_op jit(solution)/shard_map/ppermute | solution.py:323
  18.3 5.3 %collective-permute-start.8 = (f32[2,2,40,128]{3,2,1,0:T(8,128)S(1)}, f32[2,2,40,128]{3,2,1,0:T(8,128)S(1)}, u32[]{:S(2)}, u32[]{:S(2)}) collective-permute-start(f32[2,2,40,128]{3,2,1,0:T(8,128)S(1)} %pad_maximum_fusion.5), channel_id=1, source_target_pairs={{0,6},{1,7},{2,4},{3,5},{4,2},{5,3},{6,0},{7,1},{8,14},{9,15},{10,... | collective-permute-start | bytes 245768 | tf_op jit(solution)/shard_map/ppermute | solution.py:323
  28.6 2.0 %collective-permute-start.9 = (f32[256,512]{1,0:T(8,128)S(1)}, f32[256,512]{1,0:T(8,128)S(1)}, u32[]{:S(2)}, u32[]{:S(2)}) collective-permute-start(f32[256,512]{1,0:T(8,128)S(1)} %get-tuple-element.32), channel_id=1, source_target_pairs={{0,1},{1,0},{2,3},{3,2},{4,5},{5,4},{6,7},{7,6},{8,9},{9,8},{10,11... | collective-permute-start | bytes 1572872 | tf_op jit(solution)/shard_map/ppermute | solution.py:330
  29.3 7.7 %copy-start = (f32[4,64,512]{2,1,0:T(8,128)S(1)}, f32[4,64,512]{2,1,0:T(8,128)}, u32[]{:S(2)}) copy-start(f32[4,64,512]{2,1,0:T(8,128)} %refs_0_.3) | copy-start | bytes 1572868
  30.6 6.3 %collective-permute-start.12 = (f32[64,512]{1,0:T(8,128)S(1)}, f32[64,512]{1,0:T(8,128)S(1)}, u32[]{:S(2)}, u32[]{:S(2)}) collective-permute-start(f32[64,512]{1,0:T(8,128)S(1)} %get-tuple-element.36), channel_id=1, source_target_pairs={{0,2},{1,3},{2,0},{3,1},{4,6},{5,7},{6,4},{7,5},{8,10},{9,11},{10,... | collective-permute-start | bytes 393224 | tf_op jit(solution)/shard_map/ppermute | solution.py:323
  31.9 8.1 %collective-permute-start.10 = (f32[64,512]{1,0:T(8,128)S(1)}, f32[64,512]{1,0:T(8,128)S(1)}, u32[]{:S(2)}, u32[]{:S(2)}) collective-permute-start(f32[64,512]{1,0:T(8,128)S(1)} %get-tuple-element.33), channel_id=1, source_target_pairs={{0,4},{1,5},{2,6},{3,7},{4,0},{5,1},{6,2},{7,3},{8,12},{9,13},{10,... | collective-permute-start | bytes 393224 | tf_op jit(solution)/shard_map/ppermute | solution.py:323
  32.9 7.1 %collective-permute-start.11 = (f32[64,512]{1,0:T(8,128)S(1)}, f32[64,512]{1,0:T(8,128)S(1)}, u32[]{:S(2)}, u32[]{:S(2)}) collective-permute-start(f32[64,512]{1,0:T(8,128)S(1)} %get-tuple-element.34), channel_id=1, source_target_pairs={{0,6},{1,7},{2,4},{3,5},{4,2},{5,3},{6,0},{7,1},{8,14},{9,15},{10,... | collective-permute-start | bytes 393224 | tf_op jit(solution)/shard_map/ppermute | solution.py:323

commit v5 on v4

--- a/solution.py
+++ b/solution.py
@@ -47,8 +47,8 @@
         pltpu.make_async_copy(source, target, arrived.at[i])
         for i, (source, target) in enumerate(zip(sources, held))
     ]
-    for load in loads:
-        load.start()
+    for i in (1, 6, 0, 2, 3, 4, 5):
+        loads[i].start()
     count, dest, cell, offset, departure, rinv, weights = held
     n = weights.shape[0]
     rows = far[0].shape[2]
@@ -90,23 +90,21 @@
         live, rinv[...].reshape(1, n) * departure[...].reshape(1, n), jnp.float32(0.0)
     )
     columns = jnp.concatenate(
-        [
-            scaled,
-            lane.astype(jnp.float32),
-            offset_row.astype(jnp.float32),
-            jnp.zeros((SUBLANES - 3, n), jnp.float32),
-        ],
-        axis=0,
+        [scaled, offset_row.astype(jnp.float32), jnp.zeros((SUBLANES - 2, n), jnp.float32)], axis=0
     ).T
     lane_id = iota((n, LANES), 1)
-    lane_hit = (columns[:, 1:2].astype(jnp.int32) == lane_id).astype(jnp.bfloat16)
     label_rows = []
     for p in range(parts):
         for label in (cell_row, offset_row):
             mine = (iota((quads, n), 0) == quad) & (piece == p)
             label_rows.append(jnp.where(mine, label.astype(jnp.float32), 0.0))
-    labels = dot(jnp.concatenate(label_rows, axis=0).astype(jnp.bfloat16), lane_hit)
-    source = (lane_id & -KW) | ((lane_id - columns[:, 2:3].astype(jnp.int32)) & (KW - 1))
+    labels = lax.dot_general(
+        jnp.concatenate(label_rows, axis=0).astype(jnp.bfloat16),
+        one_hot(lane, LANES),
+        (((1,), (1,)), ((), ())),
+        preferred_element_type=jnp.float32,
+    )
+    source = (lane_id & -KW) | ((lane_id - columns[:, 1:2].astype(jnp.int32)) & (KW - 1))
     loads[6].wait()
     turned = jnp.take_along_axis(weights[...], source, axis=1, mode="promise_in_bounds")
     high, low = split(turned * columns[:, 0:1])

time: 40.8 us -> 40.7 us (level)
  no operation moved by 1% of the time
where the time goes in v5:
time: 40.7 us; the launch traced here: 40.6 us
  starting transfers between devices  17.5 us (43%)
  waiting for transfers between devices  14 us (34%)
  Pallas kernels  8.2 us (20%)
  between operations  0.82 us (2%)
    ppermute x9, starting transfers between devices, to_field(): lax.ppermute(x, 'lon', [(i, (i // members ^ q) * members + i % members) f...  11.7 us
    ppermute x9, waiting for transfers between devices, to_field(): lax.ppermute(x, 'lon', [(i, (i // members ^ q) * members + i % members) f...  10.8 us
    ppermute x3, starting transfers between devices, along_lat(): lax.ppermute(x, 'lat', [(i, i ^ d ^ (i & d & 2) >> 1) for i in range(lats)])  5.74 us
    pallas_call x1, Pallas kernels, per_device(): pl.pallas_call(functools.partial(pack_kernel, members, capacity, lats), o...  2.5 us
    pallas_call x1, Pallas kernels, per_device(): call(functools.partial(late_kernel, capacity, lon_cols, len(late)), [half...  1.9 us
    ppermute x3, waiting for transfers between devices, along_lat(): lax.ppermute(x, 'lat', [(i, i ^ d ^ (i & d & 2) >> 1) for i in range(lats)])  1.84 us
    pallas_call x2, Pallas kernels, per_device(): pl.pallas_call(functools.partial(finish_kernel, members, distances), out_...  1.51 us
    ppermute x1, waiting for transfers between devices, to_member(): lax.ppermute(x, 'lon', [(i, i // members * members + (i + e) % members) f...  1.31 us
  transfers between devices with their start and end apart: 13, of which 9 were waited for; matrix products, arithmetic and copies ran while one was open for 0% of the time, Pallas kernels for 7%

profile of v5, /device:TPU:0, one launch (start us, length us, event | category | flops | bytes accessed | tf_op | source)
XLA Modules:
  0.0 40.6 jit_solution(16242312549013305131)
XLA Ops:
  0.7 0.0 copy-start.1
  0.7 2.5 %shard_map.101 = (f32[2,2,40,128]{3,2,1,0:T(8,128)S(1)}, f32[2,2,40,128]{3,2,1,0:T(8,128)S(1)}, f32[2,2,40,128]{3,2,1,0:T(8,128)S(1)}, f32[2,2,40,128]{3,2,1,0:T...) custom-call(s32[1,1]{1,0:T(1,128)} %bitcast.2.refs_0_, s32[1,768]{1,0:T(1,128)} %bitcast.3, ...), custom_call_target="tpu_custom_call" | custom-call | flops 503316480 | bytes 1048576 | tf_op jit(solution)/shard_map/pallas_call | solution.py:361
  3.2 0.0 copy-start.2
  3.2 3.0 %collective-permute-start = (f32[2,2,40,128]{3,2,1,0:T(8,128)S(1)}, f32[2,2,40,128]{3,2,1,0:T(8,128)S(1)}, u32[]{:S(2)}, u32[]{:S(2)}) collective-permute-start(f32[2,2,40,128]{3,2,1,0:T(8,128)S(1)} %get-tuple-element.24), channel_id=1, source_target_pairs={{0,2},{1,3},{2,0},{3,1},{4,6},{5,7},{6,4},{7,5},{8,10},{9,11},{10,... | collective-permute-start | bytes 245768 | tf_op jit(solution)/shard_map/ppermute | solution.py:321
  6.2 1.5 %collective-permute-start.1 = (f32[2,2,40,128]{3,2,1,0:T(8,128)S(1)}, f32[2,2,40,128]{3,2,1,0:T(8,128)S(1)}, u32[]{:S(2)}, u32[]{:S(2)}) collective-permute-start(f32[2,2,40,128]{3,2,1,0:T(8,128)S(1)} %get-tuple-element.25), channel_id=1, source_target_pairs={{0,4},{1,5},{2,6},{3,7},{4,0},{5,1},{6,2},{7,3},{8,12},{9,13},{10,... | collective-permute-start | bytes 245768 | tf_op jit(solution)/shard_map/ppermute | solution.py:321
  7.7 0.0 collective-permute-start.2
  7.7 2.0 %collective-permute-start.5 = (f32[4,2,40,128]{3,2,1,0:T(8,128)S(1)}, f32[4,2,40,128]{3,2,1,0:T(8,128)S(1)}, u32[]{:S(2)}, u32[]{:S(2)}) collective-permute-start(f32[4,2,40,128]{3,2,1,0:T(8,128)S(1)} %get-tuple-element.28), channel_id=1, source_target_pairs={{0,8},{8,0},{16,24},{24,16},{1,9},{9,1},{17,25},{25,17},{2,10},{10... | collective-permute-start | bytes 491528 | tf_op jit(solution)/shard_map/ppermute | solution.py:314
  9.8 0.0 copy-done.1
  9.8 0.0 copy-done.2
  9.8 0.5 %shard_map.100 = (bf16[512,512]{1,0:T(8,128)(2,1)S(1)}, bf16[512,512]{1,0:T(8,128)(2,1)S(1)}, bf16[256,256]{1,0:T(8,128)(2,1)S(1)}) custom-call(f32[512,512]{1,0:T(8,128)S(1)} %copy-done.1, f32[4,128,128]{2,1,0:T(8,128)S(1)} %copy-done.2), custom_call_target="tpu_custom_call" | custom-call | bytes 2097152 | tf_op jit(solution)/shard_map/pallas_call | solution.py:403
  10.3 0.0 collective-permute-done
  10.3 1.2 %collective-permute-done.1 = f32[2,2,40,128]{3,2,1,0:T(8,128)S(1)} collective-permute-done((f32[2,2,40,128]{3,2,1,0:T(8,128)S(1)}, f32[2,2,40,128]{3,2,1,0:T(8,128)S(1)}, u32[]{:S(2)}, u32[]{:S(2)}) %collective-permute-start.1) | collective-permute-done | bytes 81952 | tf_op jit(solution)/shard_map/ppermute | solution.py:321
  11.5 1.5 %collective-permute-done.2 = f32[2,2,40,128]{3,2,1,0:T(8,128)S(1)} collective-permute-done((f32[2,2,40,128]{3,2,1,0:T(8,128)S(1)}, f32[2,2,40,128]{3,2,1,0:T(8,128)S(1)}, u32[]{:S(2)}, u32[]{:S(2)}) %collective-permute-start.2) | collective-permute-done | bytes 81952 | tf_op jit(solution)/shard_map/ppermute | solution.py:321
  13.1 3.7 %collective-permute-start.3 = (f32[4,2,40,128]{3,2,1,0:T(8,128)S(1)}, f32[4,2,40,128]{3,2,1,0:T(8,128)S(1)}, u32[]{:S(2)}, u32[]{:S(2)}) collective-permute-start(f32[4,2,40,128]{3,2,1,0:T(8,128)S(1)} %pad_maximum_fusion), channel_id=1, source_target_pairs={{0,24},{8,16},{16,0},{24,8},{1,25},{9,17},{17,1},{25,9},{2,26},{10... | collective-permute-start | bytes 491528 | tf_op jit(solution)/shard_map/ppermute | solution.py:314
  16.7 0.1 collective-permute-start.4
  16.8 0.0 collective-permute-done.5
  16.8 0.6 %collective-permute-start.6 = (f32[2,2,40,128]{3,2,1,0:T(8,128)S(1)}, f32[2,2,40,128]{3,2,1,0:T(8,128)S(1)}, u32[]{:S(2)}, u32[]{:S(2)}) collective-permute-start(f32[2,2,40,128]{3,2,1,0:T(8,128)S(1)} %pad_maximum_fusion.3), channel_id=1, source_target_pairs={{0,2},{1,3},{2,0},{3,1},{4,6},{5,7},{6,4},{7,5},{8,10},{9,11},{10,... | collective-permute-start | bytes 245768 | tf_op jit(solution)/shard_map/ppermute | solution.py:321
  17.5 0.7 %collective-permute-start.7 = (f32[2,2,40,128]{3,2,1,0:T(8,128)S(1)}, f32[2,2,40,128]{3,2,1,0:T(8,128)S(1)}, u32[]{:S(2)}, u32[]{:S(2)}) collective-permute-start(f32[2,2,40,128]{3,2,1,0:T(8,128)S(1)} %pad_maximum_fusion.4), channel_id=1, source_target_pairs={{0,4},{1,5},{2,6},{3,7},{4,0},{5,1},{6,2},{7,3},{8,12},{9,13},{10,... | collective-permute-start | bytes 245768 | tf_op jit(solution)/shard_map/ppermute | solution.py:321
  18.2 2.2 %collective-permute-start.8 = (f32[2,2,40,128]{3,2,1,0:T(8,128)S(1)}, f32[2,2,40,128]{3,2,1,0:T(8,128)S(1)}, u32[]{:S(2)}, u32[]{:S(2)}) collective-permute-start(f32[2,2,40,128]{3,2,1,0:T(8,128)S(1)} %pad_maximum_fusion.5), channel_id=1, source_target_pairs={{0,6},{1,7},{2,4},{3,5},{4,2},{5,3},{6,0},{7,1},{8,14},{9,15},{10,... | collective-permute-start | bytes 245768 | tf_op jit(solution)/shard_map/ppermute | solution.py:321
  20.4 0.9 %collective-permute-done.6.refs_1_ = f32[2,2,40,128]{3,2,1,0:T(8,128)S(1)} collective-permute-done((f32[2,2,40,128]{3,2,1,0:T(8,128)S(1)}, f32[2,2,40,128]{3,2,1,0:T(8,128)S(1)}, u32[]{:S(2)}, u32[]{:S(2)}) %collective-permute-start.6) | collective-permute-done | bytes 81952 | tf_op jit(solution)/shard_map/ppermute | solution.py:321
  21.4 0.5 %collective-permute-done.7.refs_2_ = f32[2,2,40,128]{3,2,1,0:T(8,128)S(1)} collective-permute-done((f32[2,2,40,128]{3,2,1,0:T(8,128)S(1)}, f32[2,2,40,128]{3,2,1,0:T(8,128)S(1)}, u32[]{:S(2)}, u32[]{:S(2)}) %collective-permute-start.7) | collective-permute-done | bytes 81952 | tf_op jit(solution)/shard_map/ppermute | solution.py:321
  21.9 1.6 %collective-permute-done.8.refs_3_ = f32[2,2,40,128]{3,2,1,0:T(8,128)S(1)} collective-permute-done((f32[2,2,40,128]{3,2,1,0:T(8,128)S(1)}, f32[2,2,40,128]{3,2,1,0:T(8,128)S(1)}, u32[]{:S(2)}, u32[]{:S(2)}) %collective-permute-start.8) | collective-permute-done | bytes 81952 | tf_op jit(solution)/shard_map/ppermute | solution.py:321
  23.5 1.2 %shard_map.102.refs_2_ = f32[8,256,128]{2,1,0:T(8,128)S(1)} custom-call(f32[2,2,40,128]{3,2,1,0:T(8,128)S(1)} %pad_maximum_fusion.2.refs_0_, f32[2,2,40,128]{3,2,1,0:T(8,128)S(1)} %collective-permute-done.6.refs_1_, f32[2,2,40,128]{3,2,1,0:T(8,128)S(1)} %collective-permute-done.7.refs_2_, f32[2,2,40,128]{3,2,1,0:T(8,128)S(1)} %collective-permute-done.8.refs_3_), custom_call_target="tpu_custom_call" | custom-call | flops 335544320 | bytes 2097152 | tf_op jit(solution)/shard_map/pallas_call | solution.py:414
  24.7 1.8 %collective-permute-done.3.refs_0_ = f32[4,2,40,128]{3,2,1,0:T(8,128)S(1)} collective-permute-done((f32[4,2,40,128]{3,2,1,0:T(8,128)S(1)}, f32[4,2,40,128]{3,2,1,0:T(8,128)S(1)}, u32[]{:S(2)}, u32[]{:S(2)}) %collective-permute-start.3) | collective-permute-done | bytes 163872 | tf_op jit(solution)/shard_map/ppermute | solution.py:314
  26.5 0.0 collective-permute-done.4.refs_1_
  26.5 1.9 %shard_map.103 = (bf16[512,512]{1,0:T(8,128)(2,1)S(1)}, bf16[512,512]{1,0:T(8,128)(2,1)S(1)}, f32[256,512]{1,0:T(8,128)S(1)}) custom-call(f32[4,2,40,128]{3,2,1,0:T(8,128)S(1)} %collective-permute-done.3.refs_0_, f32[4,2,40,128]{3,2,1,0:T(8,128)S(1)} %collective-permute-done.4.refs_1_, f32[8,256,128]{2,1,0:T(8,128)S(1)} %shard_map.102.refs_2_, ...), custom_call_target="tpu_custom_call" | custom-call | flops 805306368 | bytes 2097152 | tf_op jit(solution)/shard_map/pallas_call | solution.py:424
  28.5 0.1 collective-permute-start.9
  28.5 0.6 %shard_map.104.refs_0_ = f32[256,512]{1,0:T(8,128)S(1)} custom-call(bf16[512,512]{1,0:T(8,128)(2,1)S(1)} %get-tuple-element.21.refs_3_.zonal_high, bf16[512,512]{1,0:T(8,128)(2,1)S(1)} %get-tuple-element.22.refs_4_.zonal_low, bf16[512,512]{1,0:T(8,128)(2,1)S(1)} %get-tuple-element.30.high, bf16[512,512]{1,0:T(8,128)(2,1)S(1)} %get-tuple-element.31.low), custom_call_target="tpu_custom_call" | custom-call | flops 402653184 | bytes 1048576 | tf_op jit(solution)/shard_map/pallas_call | solution.py:433
  29.1 0.0 copy-start
  29.1 1.3 %collective-permute-done.9.refs_1_ = f32[256,512]{1,0:T(8,128)S(1)} collective-permute-done((f32[256,512]{1,0:T(8,128)S(1)}, f32[256,512]{1,0:T(8,128)S(1)}, u32[]{:S(2)}, u32[]{:S(2)}) %collective-permute-start.9) | collective-permute-done | bytes 524320 | tf_op jit(solution)/shard_map/ppermute | solution.py:328
  30.4 0.1 shard_map.105
  30.5 1.2 %collective-permute-start.12 = (f32[64,512]{1,0:T(8,128)S(1)}, f32[64,512]{1,0:T(8,128)S(1)}, u32[]{:S(2)}, u32[]{:S(2)}) collective-permute-start(f32[64,512]{1,0:T(8,128)S(1)} %get-tuple-element.36), channel_id=1, source_target_pairs={{0,2},{1,3},{2,0},{3,1},{4,6},{5,7},{6,4},{7,5},{8,10},{9,11},{10,... | collective-permute-start | bytes 393224 | tf_op jit(solution)/shard_map/ppermute | solution.py:321
  31.7 1.0 %collective-permute-start.10 = (f32[64,512]{1,0:T(8,128)S(1)}, f32[64,512]{1,0:T(8,128)S(1)}, u32[]{:S(2)}, u32[]{:S(2)}) collective-permute-start(f32[64,512]{1,0:T(8,128)S(1)} %get-tuple-element.33), channel_id=1, source_target_pairs={{0,4},{1,5},{2,6},{3,7},{4,0},{5,1},{6,2},{7,3},{8,12},{9,13},{10,... | collective-permute-start | bytes 393224 | tf_op jit(solution)/shard_map/ppermute | solution.py:321
  32.7 1.3 %collective-permute-start.11 = (f32[64,512]{1,0:T(8,128)S(1)}, f32[64,512]{1,0:T(8,128)S(1)}, u32[]{:S(2)}, u32[]{:S(2)}) collective-permute-start(f32[64,512]{1,0:T(8,128)S(1)} %get-tuple-element.34), channel_id=1, source_target_pairs={{0,6},{1,7},{2,4},{3,5},{4,2},{5,3},{6,0},{7,1},{8,14},{9,15},{10,... | collective-permute-start | bytes 393224 | tf_op jit(solution)/shard_map/ppermute | solution.py:321
  34.0 2.7 %collective-permute-done.12.refs_2_ = f32[64,512]{1,0:T(8,128)S(1)} collective-permute-done((f32[64,512]{1,0:T(8,128)S(1)}, f32[64,512]{1,0:T(8,128)S(1)}, u32[]{:S(2)}, u32[]{:S(2)}) %collective-permute-start.12) | collective-permute-done | bytes 131104 | tf_op jit(solution)/shard_map/ppermute | solution.py:321
  36.8 0.0 copy-done
  36.8 0.8 %shard_map.106.refs_3_ = f32[4,64,512]{2,1,0:T(8,128)} custom-call(f32[4,64,512]{2,1,0:T(8,128)S(1)} %copy-done, f32[64,512]{1,0:T(8,128)S(1)} %get-tuple-element.35.refs_1_, f32[64,512]{1,0:T(8,128)S(1)} %collective-permute-done.12.refs_2_), custom_call_target="tpu_custom_call" | custom-call | bytes 1048576 | tf_op jit(solution)/shard_map/pallas_call | solution.py:447
  37.6 2.2 %collective-permute-done.10.refs_1_ = f32[64,512]{1,0:T(8,128)S(1)} collective-permute-done((f32[64,512]{1,0:T(8,128)S(1)}, f32[64,512]{1,0:T(8,128)S(1)}, u32[]{:S(2)}, u32[]{:S(2)}) %collective-permute-start.10) | collective-permute-done | bytes 131104 | tf_op jit(solution)/shard_map/ppermute | solution.py:321
  39.8 0.0 collective-permute-done.11.refs_2_
  39.8 0.8 %shard_map.107 = f32[4,64,512]{2,1,0:T(8,128)} custom-call(f32[4,64,512]{2,1,0:T(8,128)S(1)} %copy-done, f32[64,512]{1,0:T(8,128)S(1)} %collective-permute-done.10.refs_1_, f32[64,512]{1,0:T(8,128)S(1)} %collective-permute-done.11.refs_2_, f32[4,64,512]{2,1,0:T(8,128)} %shard_map.106.refs_3_), custom_call_target="tpu_custom_call", output_to_operand_aliasing={{}: (3, {})} | custom-call | bytes 1048576 | tf_op jit(solution)/shard_map/pallas_call | solution.py:447
  (11 shorter events, 0.1 us)
Async XLA Ops:
  0.7 9.1 %copy-start.1 = (f32[512,512]{1,0:T(8,128)S(1)}, f32[512,512]{1,0:T(8,128)}, u32[]{:S(2)}) copy-start(f32[512,512]{1,0:T(8,128)} %zonal.1) | copy-start | bytes 3145732
  3.2 6.6 %copy-start.2 = (f32[4,128,128]{2,1,0:T(8,128)S(1)}, f32[4,128,128]{2,1,0:T(8,128)}, u32[]{:S(2)}) copy-start(f32[4,128,128]{2,1,0:T(8,128)} %vert.1) | copy-start | bytes 786436
  3.2 7.1 %collective-permute-start = (f32[2,2,40,128]{3,2,1,0:T(8,128)S(1)}, f32[2,2,40,128]{3,2,1,0:T(8,128)S(1)}, u32[]{:S(2)}, u32[]{:S(2)}) collective-permute-start(f32[2,2,40,128]{3,2,1,0:T(8,128)S(1)} %get-tuple-element.24), channel_id=1, source_target_pairs={{0,2},{1,3},{2,0},{3,1},{4,6},{5,7},{6,4},{7,5},{8,10},{9,11},{10,... | collective-permute-start | bytes 245768 | tf_op jit(solution)/shard_map/ppermute | solution.py:321
  6.2 5.3 %collective-permute-start.1 = (f32[2,2,40,128]{3,2,1,0:T(8,128)S(1)}, f32[2,2,40,128]{3,2,1,0:T(8,128)S(1)}, u32[]{:S(2)}, u32[]{:S(2)}) collective-permute-start(f32[2,2,40,128]{3,2,1,0:T(8,128)S(1)} %get-tuple-element.25), channel_id=1, source_target_pairs={{0,4},{1,5},{2,6},{3,7},{4,0},{5,1},{6,2},{7,3},{8,12},{9,13},{10,... | collective-permute-start | bytes 245768 | tf_op jit(solution)/shard_map/ppermute | solution.py:321
  7.7 5.3 %collective-permute-start.2 = (f32[2,2,40,128]{3,2,1,0:T(8,128)S(1)}, f32[2,2,40,128]{3,2,1,0:T(8,128)S(1)}, u32[]{:S(2)}, u32[]{:S(2)}) collective-permute-start(f32[2,2,40,128]{3,2,1,0:T(8,128)S(1)} %get-tuple-element.26), channel_id=1, source_target_pairs={{0,6},{1,7},{2,4},{3,5},{4,2},{5,3},{6,0},{7,1},{8,14},{9,15},{10,... | collective-permute-start | bytes 245768 | tf_op jit(solution)/shard_map/ppermute | solution.py:321
  7.7 9.1 %collective-permute-start.5 = (f32[4,2,40,128]{3,2,1,0:T(8,128)S(1)}, f32[4,2,40,128]{3,2,1,0:T(8,128)S(1)}, u32[]{:S(2)}, u32[]{:S(2)}) collective-permute-start(f32[4,2,40,128]{3,2,1,0:T(8,128)S(1)} %get-tuple-element.28), channel_id=1, source_target_pairs={{0,8},{8,0},{16,24},{24,16},{1,9},{9,1},{17,25},{25,17},{2,10},{10... | collective-permute-start | bytes 491528 | tf_op jit(solution)/shard_map/ppermute | solution.py:314
  13.1 13.5 %collective-permute-start.3 = (f32[4,2,40,128]{3,2,1,0:T(8,128)S(1)}, f32[4,2,40,128]{3,2,1,0:T(8,128)S(1)}, u32[]{:S(2)}, u32[]{:S(2)}) collective-permute-start(f32[4,2,40,128]{3,2,1,0:T(8,128)S(1)} %pad_maximum_fusion), channel_id=1, source_target_pairs={{0,24},{8,16},{16,0},{24,8},{1,25},{9,17},{17,1},{25,9},{2,26},{10... | collective-permute-start | bytes 491528 | tf_op jit(solution)/shard_map/ppermute | solution.py:314
  16.7 9.8 %collective-permute-start.4 = (f32[4,2,40,128]{3,2,1,0:T(8,128)S(1)}, f32[4,2,40,128]{3,2,1,0:T(8,128)S(1)}, u32[]{:S(2)}, u32[]{:S(2)}) collective-permute-start(f32[4,2,40,128]{3,2,1,0:T(8,128)S(1)} %pad_maximum_fusion.1), channel_id=1, source_target_pairs={{0,16},{8,24},{16,8},{24,0},{1,17},{9,25},{17,9},{25,1},{2,18},{10... | collective-permute-start | bytes 491528 | tf_op jit(solution)/shard_map/ppermute | solution.py:314
  16.8 4.5 %collective-permute-start.6 = (f32[2,2,40,128]{3,2,1,0:T(8,128)S(1)}, f32[2,2,40,128]{3,2,1,0:T(8,128)S(1)}, u32[]{:S(2)}, u32[]{:S(2)}) collective-permute-start(f32[2,2,40,128]{3,2,1,0:T(8,128)S(1)} %pad_maximum_fusion.3), channel_id=1, source_target_pairs={{0,2},{1,3},{2,0},{3,1},{4,6},{5,7},{6,4},{7,5},{8,10},{9,11},{10,... | collective-permute-start | bytes 245768 | tf_op jit(solution)/shard_map/ppermute | solution.py:321
  17.5 4.4 %collective-permute-start.7 = (f32[2,2,40,128]{3,2,1,0:T(8,128)S(1)}, f32[2,2,40,128]{3,2,1,0:T(8,128)S(1)}, u32[]{:S(2)}, u32[]{:S(2)}) collective-permute-start(f32[2,2,40,128]{3,2,1,0:T(8,128)S(1)} %pad_maximum_fusion.4), channel_id=1, source_target_pairs={{0,4},{1,5},{2,6},{3,7},{4,0},{5,1},{6,2},{7,3},{8,12},{9,13},{10,... | collective-permute-start | bytes 245768 | tf_op jit(solution)/shard_map/ppermute | solution.py:321
  18.2 5.3 %collective-permute-start.8 = (f32[2,2,40,128]{3,2,1,0:T(8,128)S(1)}, f32[2,2,40,128]{3,2,1,0:T(8,128)S(1)}, u32[]{:S(2)}, u32[]{:S(2)}) collective-permute-start(f32[2,2,40,128]{3,2,1,0:T(8,128)S(1)} %pad_maximum_fusion.5), channel_id=1, source_target_pairs={{0,6},{1,7},{2,4},{3,5},{4,2},{5,3},{6,0},{7,1},{8,14},{9,15},{10,... | collective-permute-start | bytes 245768 | tf_op jit(solution)/shard_map/ppermute | solution.py:321
  28.5 2.0 %collective-permute-start.9 = (f32[256,512]{1,0:T(8,128)S(1)}, f32[256,512]{1,0:T(8,128)S(1)}, u32[]{:S(2)}, u32[]{:S(2)}) collective-permute-start(f32[256,512]{1,0:T(8,128)S(1)} %get-tuple-element.32), channel_id=1, source_target_pairs={{0,1},{1,0},{2,3},{3,2},{4,5},{5,4},{6,7},{7,6},{8,9},{9,8},{10,11... | collective-permute-start | bytes 1572872 | tf_op jit(solution)/shard_map/ppermute | solution.py:328
  29.1 7.7 %copy-start = (f32[4,64,512]{2,1,0:T(8,128)S(1)}, f32[4,64,512]{2,1,0:T(8,128)}, u32[]{:S(2)}) copy-start(f32[4,64,512]{2,1,0:T(8,128)} %refs_0_.3) | copy-start | bytes 1572868
  30.5 6.3 %collective-permute-start.12 = (f32[64,512]{1,0:T(8,128)S(1)}, f32[64,512]{1,0:T(8,128)S(1)}, u32[]{:S(2)}, u32[]{:S(2)}) collective-permute-start(f32[64,512]{1,0:T(8,128)S(1)} %get-tuple-element.36), channel_id=1, source_target_pairs={{0,2},{1,3},{2,0},{3,1},{4,6},{5,7},{6,4},{7,5},{8,10},{9,11},{10,... | collective-permute-start | bytes 393224 | tf_op jit(solution)/shard_map/ppermute | solution.py:321
  31.7 8.1 %collective-permute-start.10 = (f32[64,512]{1,0:T(8,128)S(1)}, f32[64,512]{1,0:T(8,128)S(1)}, u32[]{:S(2)}, u32[]{:S(2)}) collective-permute-start(f32[64,512]{1,0:T(8,128)S(1)} %get-tuple-element.33), channel_id=1, source_target_pairs={{0,4},{1,5},{2,6},{3,7},{4,0},{5,1},{6,2},{7,3},{8,12},{9,13},{10,... | collective-permute-start | bytes 393224 | tf_op jit(solution)/shard_map/ppermute | solution.py:321
  32.7 7.1 %collective-permute-start.11 = (f32[64,512]{1,0:T(8,128)S(1)}, f32[64,512]{1,0:T(8,128)S(1)}, u32[]{:S(2)}, u32[]{:S(2)}) collective-permute-start(f32[64,512]{1,0:T(8,128)S(1)} %get-tuple-element.34), channel_id=1, source_target_pairs={{0,6},{1,7},{2,4},{3,5},{4,2},{5,3},{6,0},{7,1},{8,14},{9,15},{10,... | collective-permute-start | bytes 393224 | tf_op jit(solution)/shard_map/ppermute | solution.py:321

commit v6 on v5

--- a/solution.py
+++ b/solution.py
@@ -41,8 +41,10 @@
 
 
 def pack_kernel(members, capacity, lats, *refs):
-    sources, far, near = refs[:7], refs[7 : 7 + F], refs[7 + F : 7 + F + NEAR]
-    held, by_field, arrived = refs[7 + F + NEAR : -2], refs[-2], refs[-1]
+    sources, far = refs[:7], refs[7 : 7 + F]
+    quad_out, slot_out, pieces_out, labels_out = refs[7 + F : 11 + F]
+    held, by_field, arrived = refs[11 + F : -2], refs[-2], refs[-1]
+    far_bands = tuple(range(NEAR, lats))
     loads = [
         pltpu.make_async_copy(source, target, arrived.at[i])
         for i, (source, target) in enumerate(zip(sources, held))
@@ -109,22 +111,52 @@
     turned = jnp.take_along_axis(weights[...], source, axis=1, mode="promise_in_bounds")
     high, low = split(turned * columns[:, 0:1])
     pieces = jnp.concatenate([high, low], axis=1)
+    form_messages(
+        far_bands, capacity, members, quads, rows, quad, slot, pieces, labels, by_field
+    )
+    for k in range(len(far_bands)):
+        for half in range(members):
+            for q in range(F):
+                far[q][k, half] = by_field[field ^ q, k, half]
+    quad_out[...], slot_out[...] = quad, slot
+    pieces_out[...], labels_out[...] = pieces, labels
+
+
+def near_kernel(capacity, members, quad, slot, pieces, labels, *outs):
+    rows = outs[0].shape[2]
+    by_field = outs[-1]
+    outs = outs[:-1]
+    quads = labels.shape[0] // (2 * message_rows(capacity)[0])
+    field = lax.axis_index("lon") // members
+    bands = tuple(reversed(range(NEAR)))
+    form_messages(
+        bands, capacity, members, quads, rows, quad[...], slot[...], pieces[...], labels[...], by_field
+    )
+    for k, distance in enumerate(bands):
+        for half in range(members):
+            for q in range(F):
+                outs[distance][q, half] = by_field[field ^ q, k, half]
+
+
+def form_messages(
+    bands, capacity, members, quads, rows, quad, slot, pieces, labels, by_field
+):
+    parts, _ = message_rows(capacity)
     even = iota((rows, LANES), 1) & KW == 0
     lower = iota((rows, LANES), 1) < LANES // 2
     size = GROUPS * rows
     tail = capacity // SUBLANES * SUBLANES
     row_id = iota((rows - tail, LANES), 0) + tail
-    order = (*range(NEAR, lats), *reversed(range(NEAR)))
     hits = jnp.concatenate(
         [
             one_hot(jnp.where(quad == distance * members + half, slot, -1), size)
-            for distance in order
+            for distance in bands
             for half in range(members)
         ],
         axis=0,
     )
     both = dot(hits, pieces)
-    for step, distance in enumerate(order):
+    for step, distance in enumerate(bands):
         for half in range(members):
             at = (step * members + half) * size
             picked = both[at : at + size, :LANES] + both[at : at + size, LANES:]
@@ -148,14 +180,9 @@
                 k = i * quads + distance * members + half
                 extra = jnp.where(row_id == capacity + i, labels[k : k + 1], extra)
             for f in range(F):
-                message = jnp.concatenate([fields[f][:tail], fields[f][tail:] + extra], axis=0)
-                if distance < NEAR:
-                    near[distance][field ^ f, half] = message
-                else:
-                    by_field[distance - NEAR, half, f] = message
-            if distance >= NEAR:
-                for q in range(F):
-                    far[q][distance - NEAR, half] = by_field[distance - NEAR, half, field ^ q]
+                by_field[f, step, half] = jnp.concatenate(
+                    [fields[f][:tail], fields[f][tail:] + extra], axis=0
+                )
 
 
 def prepare_kernel(members, lon_cols, zonal, vert, zonal_high, zonal_low, vert_both, turned):
@@ -348,7 +375,7 @@
     members = lons // F
     n_obs = obs_cell.shape[0]
     capacity = max(2, 3 * n_obs // (2 * devices))
-    _, rows = message_rows(capacity)
+    parts, rows = message_rows(capacity)
     lat_rows, lon_cols, _ = control.shape
     columns = lat_rows * lon_cols
     blocks = lons
@@ -360,9 +387,15 @@
     near_messages = jax.ShapeDtypeStruct((F, members, rows, LANES), f32)
     messages = pl.pallas_call(
         functools.partial(pack_kernel, members, capacity, lats),
-        out_shape=[far_messages] * F + [near_messages] * NEAR,
+        out_shape=[far_messages] * F
+        + [
+            jax.ShapeDtypeStruct((1, n_obs), jnp.int32),
+            jax.ShapeDtypeStruct((1, n_obs), jnp.int32),
+            jax.ShapeDtypeStruct((n_obs, 2 * LANES), bf16),
+            jax.ShapeDtypeStruct((2 * parts * devices // GROUPS, LANES), f32),
+        ],
         in_specs=[pl.BlockSpec(memory_space=pltpu.HBM)] * 7,
-        out_specs=[pl.BlockSpec(memory_space=pltpu.VMEM)] * (F + NEAR),
+        out_specs=[pl.BlockSpec(memory_space=pltpu.VMEM)] * (F + 4),
         scratch_shapes=[
             pltpu.SMEM((1, 1), jnp.int32),
             pltpu.VMEM((1, n_obs), jnp.int32),
@@ -371,7 +404,7 @@
             pltpu.VMEM((n_obs,), f32),
             pltpu.VMEM((n_obs,), f32),
             pltpu.VMEM((n_obs, LANES), f32),
-            pltpu.VMEM((lats - NEAR, members, F, rows, LANES), f32),
+            pltpu.VMEM((F, lats - NEAR, members, rows, LANES), f32),
             pltpu.SemaphoreType.DMA((7,)),
         ],
         compiler_params=pltpu.CompilerParams(vmem_limit_bytes=24 * MIB),
@@ -392,8 +425,17 @@
             )
         )
     )
-    far, near = list(messages[:F]), list(messages[F:])
-    far = [to_field(far[q], q, members) for q in range(F)]
+    far = [to_field(messages[q], q, members) for q in range(F)]
+    near = list(
+        call(
+            functools.partial(near_kernel, capacity, members),
+            [near_messages] * NEAR,
+            4,
+            scratch=[pltpu.VMEM((F, NEAR, members, rows, LANES), f32)],
+            flops=4 * NEAR * members * GROUPS * rows * n_obs * LANES,
+            nbytes=1 << 20,
+        )(*messages[F:])
+    )
     late = [
         along_lat(jnp.stack([part[d - NEAR] for part in far]), d)
         for d in reversed(range(NEAR, lats))

time: 40.7 us -> 40.8 us (level)
    pallas_call x0 -> x1, Pallas kernels: none -> 0.58 us  [per_device(): call(functools.partial(near_kernel, capacity, members), [near_messages] *...]
    ppermute x9, waiting for transfers between devices: 10.8 us -> 10.3 us  [to_field(): lax.ppermute(x, 'lon', [(i, (i // members ^ q) * members + i % members) f...]
  transfers between devices with their start and end apart: 13 -> 13, of which waited for: 9 -> 9; matrix products, arithmetic and copies ran while one was open for 0% -> 0% of each run, Pallas kernels for 7% -> 9%
where the time goes in v6:
time: 40.8 us; the launch traced here: 40.7 us
  starting transfers between devices  17.5 us (43%)
  waiting for transfers between devices  13.6 us (33%)
  Pallas kernels  8.52 us (21%)
  between operations  0.83 us (2%)
    ppermute x9, starting transfers between devices, to_field(): lax.ppermute(x, 'lon', [(i, (i // members ^ q) * members + i % members) f...  11.7 us
    ppermute x9, waiting for transfers between devices, to_field(): lax.ppermute(x, 'lon', [(i, (i // members ^ q) * members + i % members) f...  10.3 us
    ppermute x3, starting transfers between devices, along_lat(): lax.ppermute(x, 'lat', [(i, i ^ d ^ (i & d & 2) >> 1) for i in range(lats)])  5.81 us
    pallas_call x1, Pallas kernels, per_device(): pl.pallas_call(functools.partial(pack_kernel, members, capacity, lats), o...  2.24 us
    ppermute x3, waiting for transfers between devices, along_lat(): lax.ppermute(x, 'lat', [(i, i ^ d ^ (i & d & 2) >> 1) for i in range(lats)])  1.99 us
    pallas_call x1, Pallas kernels, per_device(): call(functools.partial(late_kernel, capacity, lon_cols, len(late)), [half...  1.9 us
    pallas_call x2, Pallas kernels, per_device(): pl.pallas_call(functools.partial(finish_kernel, members, distances), out_...  1.51 us
    ppermute x1, waiting for transfers between devices, to_member(): lax.ppermute(x, 'lon', [(i, i // members * members + (i + e) % members) f...  1.31 us
  transfers between devices with their start and end apart: 13, of which 9 were waited for; matrix products, arithmetic and copies ran while one was open for 0% of the time, Pallas kernels for 9%

profile of v6, /device:TPU:0, one launch (start us, length us, event | category | flops | bytes accessed | tf_op | source)
XLA Modules:
  0.0 40.7 jit_solution(15549879388890213023)
XLA Ops:
  0.7 2.2 %shard_map.101 = (f32[2,2,40,128]{3,2,1,0:T(8,128)S(1)}, f32[2,2,40,128]{3,2,1,0:T(8,128)S(1)}, f32[2,2,40,128]{3,2,1,0:T(8,128)S(1)}, f32[2,2,40,128]{3,2,1,0:T...) custom-call(s32[1,1]{1,0:T(1,128)} %bitcast.2.refs_0_, ...), custom_call_target="tpu_custom_call" | custom-call | flops 503316480 | bytes 1048576 | tf_op jit(solution)/shard_map/pallas_call | solution.py:388
  2.9 0.0 copy-start.1
  2.9 3.0 %collective-permute-start = (f32[2,2,40,128]{3,2,1,0:T(8,128)S(1)}, f32[2,2,40,128]{3,2,1,0:T(8,128)S(1)}, u32[]{:S(2)}, u32[]{:S(2)}) collective-permute-start(f32[2,2,40,128]{3,2,1,0:T(8,128)S(1)} %get-tuple-element.28), channel_id=1, source_target_pairs={{0,2},{1,3},{2,0},{3,1},{4,6},{5,7},{6,4},{7,5},{8,10},{9,11},{10,... | collective-permute-start | bytes 245768 | tf_op jit(solution)/shard_map/ppermute | solution.py:348
  5.9 1.5 %collective-permute-start.1 = (f32[2,2,40,128]{3,2,1,0:T(8,128)S(1)}, f32[2,2,40,128]{3,2,1,0:T(8,128)S(1)}, u32[]{:S(2)}, u32[]{:S(2)}) collective-permute-start(f32[2,2,40,128]{3,2,1,0:T(8,128)S(1)} %get-tuple-element.29), channel_id=1, source_target_pairs={{0,4},{1,5},{2,6},{3,7},{4,0},{5,1},{6,2},{7,3},{8,12},{9,13},{10,... | collective-permute-start | bytes 245768 | tf_op jit(solution)/shard_map/ppermute | solution.py:348
  7.4 0.0 collective-permute-start.2
  7.5 0.6 %shard_map.102 = (f32[4,2,40,128]{3,2,1,0:T(8,128)S(1)}, f32[4,2,40,128]{3,2,1,0:T(8,128)S(1)}) custom-call(s32[1,768]{1,0:T(1,128)S(1)} %get-tuple-element.31.quad, s32[1,768]{1,0:T(1,128)S(1)} %get-tuple-element.32.slot, bf16[768,256]{1,0:T(8,128)(2,1)S(1)} %get-tuple-element.33.pieces, f32[32,128]{1,0:T(8,128)S(1)} %get-tuple-element.34.labels), custom_call_target="tpu_custom_call" | custom-call | flops 251658240 | bytes 1048576 | tf_op jit(solution)/shard_map/pallas_call | solution.py:430
  8.0 0.0 copy-start.2
  8.1 2.1 %collective-permute-start.5 = (f32[4,2,40,128]{3,2,1,0:T(8,128)S(1)}, f32[4,2,40,128]{3,2,1,0:T(8,128)S(1)}, u32[]{:S(2)}, u32[]{:S(2)}) collective-permute-start(f32[4,2,40,128]{3,2,1,0:T(8,128)S(1)} %get-tuple-element.36), channel_id=1, source_target_pairs={{0,8},{8,0},{16,24},{24,16},{1,9},{9,1},{17,25},{25,17},{2,10},{10... | collective-permute-start | bytes 491528 | tf_op jit(solution)/shard_map/ppermute | solution.py:341
  10.2 0.0 copy-done.1
  10.2 0.0 copy-done.2
  10.2 0.5 %shard_map.100 = (bf16[512,512]{1,0:T(8,128)(2,1)S(1)}, bf16[512,512]{1,0:T(8,128)(2,1)S(1)}, bf16[256,256]{1,0:T(8,128)(2,1)S(1)}) custom-call(f32[512,512]{1,0:T(8,128)S(1)} %copy-done.1, f32[4,128,128]{2,1,0:T(8,128)S(1)} %copy-done.2), custom_call_target="tpu_custom_call" | custom-call | bytes 2097152 | tf_op jit(solution)/shard_map/pallas_call | solution.py:445
  10.7 0.0 collective-permute-done
  10.7 0.5 %collective-permute-done.1 = f32[2,2,40,128]{3,2,1,0:T(8,128)S(1)} collective-permute-done((f32[2,2,40,128]{3,2,1,0:T(8,128)S(1)}, f32[2,2,40,128]{3,2,1,0:T(8,128)S(1)}, u32[]{:S(2)}, u32[]{:S(2)}) %collective-permute-start.1) | collective-permute-done | bytes 81952 | tf_op jit(solution)/shard_map/ppermute | solution.py:348
  11.2 1.5 %collective-permute-done.2 = f32[2,2,40,128]{3,2,1,0:T(8,128)S(1)} collective-permute-done((f32[2,2,40,128]{3,2,1,0:T(8,128)S(1)}, f32[2,2,40,128]{3,2,1,0:T(8,128)S(1)}, u32[]{:S(2)}, u32[]{:S(2)}) %collective-permute-start.2) | collective-permute-done | bytes 81952 | tf_op jit(solution)/shard_map/ppermute | solution.py:348
  12.8 3.7 %collective-permute-start.3 = (f32[4,2,40,128]{3,2,1,0:T(8,128)S(1)}, f32[4,2,40,128]{3,2,1,0:T(8,128)S(1)}, u32[]{:S(2)}, u32[]{:S(2)}) collective-permute-start(f32[4,2,40,128]{3,2,1,0:T(8,128)S(1)} %pad_maximum_fusion), channel_id=1, source_target_pairs={{0,24},{8,16},{16,0},{24,8},{1,25},{9,17},{17,1},{25,9},{2,26},{10... | collective-permute-start | bytes 491528 | tf_op jit(solution)/shard_map/ppermute | solution.py:341
  16.5 0.1 collective-permute-start.4
  16.5 0.0 collective-permute-done.5
  16.6 0.6 %collective-permute-start.6 = (f32[2,2,40,128]{3,2,1,0:T(8,128)S(1)}, f32[2,2,40,128]{3,2,1,0:T(8,128)S(1)}, u32[]{:S(2)}, u32[]{:S(2)}) collective-permute-start(f32[2,2,40,128]{3,2,1,0:T(8,128)S(1)} %pad_maximum_fusion.3), channel_id=1, source_target_pairs={{0,2},{1,3},{2,0},{3,1},{4,6},{5,7},{6,4},{7,5},{8,10},{9,11},{10,... | collective-permute-start | bytes 245768 | tf_op jit(solution)/shard_map/ppermute | solution.py:348
  17.2 0.9 %collective-permute-start.7 = (f32[2,2,40,128]{3,2,1,0:T(8,128)S(1)}, f32[2,2,40,128]{3,2,1,0:T(8,128)S(1)}, u32[]{:S(2)}, u32[]{:S(2)}) collective-permute-start(f32[2,2,40,128]{3,2,1,0:T(8,128)S(1)} %pad_maximum_fusion.4), channel_id=1, source_target_pairs={{0,4},{1,5},{2,6},{3,7},{4,0},{5,1},{6,2},{7,3},{8,12},{9,13},{10,... | collective-permute-start | bytes 245768 | tf_op jit(solution)/shard_map/ppermute | solution.py:348
  18.1 2.0 %collective-permute-start.8 = (f32[2,2,40,128]{3,2,1,0:T(8,128)S(1)}, f32[2,2,40,128]{3,2,1,0:T(8,128)S(1)}, u32[]{:S(2)}, u32[]{:S(2)}) collective-permute-start(f32[2,2,40,128]{3,2,1,0:T(8,128)S(1)} %pad_maximum_fusion.5), channel_id=1, source_target_pairs={{0,6},{1,7},{2,4},{3,5},{4,2},{5,3},{6,0},{7,1},{8,14},{9,15},{10,... | collective-permute-start | bytes 245768 | tf_op jit(solution)/shard_map/ppermute | solution.py:348
  20.2 0.9 %collective-permute-done.6.refs_1_ = f32[2,2,40,128]{3,2,1,0:T(8,128)S(1)} collective-permute-done((f32[2,2,40,128]{3,2,1,0:T(8,128)S(1)}, f32[2,2,40,128]{3,2,1,0:T(8,128)S(1)}, u32[]{:S(2)}, u32[]{:S(2)}) %collective-permute-start.6) | collective-permute-done | bytes 81952 | tf_op jit(solution)/shard_map/ppermute | solution.py:348
  21.1 0.5 %collective-permute-done.7.refs_2_ = f32[2,2,40,128]{3,2,1,0:T(8,128)S(1)} collective-permute-done((f32[2,2,40,128]{3,2,1,0:T(8,128)S(1)}, f32[2,2,40,128]{3,2,1,0:T(8,128)S(1)}, u32[]{:S(2)}, u32[]{:S(2)}) %collective-permute-start.7) | collective-permute-done | bytes 81952 | tf_op jit(solution)/shard_map/ppermute | solution.py:348
  21.6 1.8 %collective-permute-done.8.refs_3_ = f32[2,2,40,128]{3,2,1,0:T(8,128)S(1)} collective-permute-done((f32[2,2,40,128]{3,2,1,0:T(8,128)S(1)}, f32[2,2,40,128]{3,2,1,0:T(8,128)S(1)}, u32[]{:S(2)}, u32[]{:S(2)}) %collective-permute-start.8) | collective-permute-done | bytes 81952 | tf_op jit(solution)/shard_map/ppermute | solution.py:348
  23.5 1.2 %shard_map.103.refs_2_ = f32[8,256,128]{2,1,0:T(8,128)S(1)} custom-call(f32[2,2,40,128]{3,2,1,0:T(8,128)S(1)} %pad_maximum_fusion.2.refs_0_, f32[2,2,40,128]{3,2,1,0:T(8,128)S(1)} %collective-permute-done.6.refs_1_, f32[2,2,40,128]{3,2,1,0:T(8,128)S(1)} %collective-permute-done.7.refs_2_, f32[2,2,40,128]{3,2,1,0:T(8,128)S(1)} %collective-permute-done.8.refs_3_), custom_call_target="tpu_custom_call" | custom-call | flops 335544320 | bytes 2097152 | tf_op jit(solution)/shard_map/pallas_call | solution.py:456
  24.6 2.0 %collective-permute-done.3.refs_0_ = f32[4,2,40,128]{3,2,1,0:T(8,128)S(1)} collective-permute-done((f32[4,2,40,128]{3,2,1,0:T(8,128)S(1)}, f32[4,2,40,128]{3,2,1,0:T(8,128)S(1)}, u32[]{:S(2)}, u32[]{:S(2)}) %collective-permute-start.3) | collective-permute-done | bytes 163872 | tf_op jit(solution)/shard_map/ppermute | solution.py:341
  26.6 0.0 collective-permute-done.4.refs_1_
  26.6 1.9 %shard_map.104 = (bf16[512,512]{1,0:T(8,128)(2,1)S(1)}, bf16[512,512]{1,0:T(8,128)(2,1)S(1)}, f32[256,512]{1,0:T(8,128)S(1)}) custom-call(f32[4,2,40,128]{3,2,1,0:T(8,128)S(1)} %collective-permute-done.3.refs_0_, f32[4,2,40,128]{3,2,1,0:T(8,128)S(1)} %collective-permute-done.4.refs_1_, f32[8,256,128]{2,1,0:T(8,128)S(1)} %shard_map.103.refs_2_, ...), custom_call_target="tpu_custom_call" | custom-call | flops 805306368 | bytes 2097152 | tf_op jit(solution)/shard_map/pallas_call | solution.py:466
  28.5 0.1 collective-permute-start.9
  28.6 0.6 %shard_map.105.refs_0_ = f32[256,512]{1,0:T(8,128)S(1)} custom-call(bf16[512,512]{1,0:T(8,128)(2,1)S(1)} %get-tuple-element.25.refs_3_.zonal_high, bf16[512,512]{1,0:T(8,128)(2,1)S(1)} %get-tuple-element.26.refs_4_.zonal_low, bf16[512,512]{1,0:T(8,128)(2,1)S(1)} %get-tuple-element.38.high, bf16[512,512]{1,0:T(8,128)(2,1)S(1)} %get-tuple-element.39.low), custom_call_target="tpu_custom_call" | custom-call | flops 402653184 | bytes 1048576 | tf_op jit(solution)/shard_map/pallas_call | solution.py:475
  29.2 0.0 copy-start
  29.2 1.3 %collective-permute-done.9.refs_1_ = f32[256,512]{1,0:T(8,128)S(1)} collective-permute-done((f32[256,512]{1,0:T(8,128)S(1)}, f32[256,512]{1,0:T(8,128)S(1)}, u32[]{:S(2)}, u32[]{:S(2)}) %collective-permute-start.9) | collective-permute-done | bytes 524320 | tf_op jit(solution)/shard_map/ppermute | solution.py:355
  30.5 0.1 shard_map.106
  30.6 1.3 %collective-permute-start.12 = (f32[64,512]{1,0:T(8,128)S(1)}, f32[64,512]{1,0:T(8,128)S(1)}, u32[]{:S(2)}, u32[]{:S(2)}) collective-permute-start(f32[64,512]{1,0:T(8,128)S(1)} %get-tuple-element.44), channel_id=1, source_target_pairs={{0,2},{1,3},{2,0},{3,1},{4,6},{5,7},{6,4},{7,5},{8,10},{9,11},{10,... | collective-permute-start | bytes 393224 | tf_op jit(solution)/shard_map/ppermute | solution.py:348
  31.8 0.6 %collective-permute-start.10 = (f32[64,512]{1,0:T(8,128)S(1)}, f32[64,512]{1,0:T(8,128)S(1)}, u32[]{:S(2)}, u32[]{:S(2)}) collective-permute-start(f32[64,512]{1,0:T(8,128)S(1)} %get-tuple-element.41), channel_id=1, source_target_pairs={{0,4},{1,5},{2,6},{3,7},{4,0},{5,1},{6,2},{7,3},{8,12},{9,13},{10,... | collective-permute-start | bytes 393224 | tf_op jit(solution)/shard_map/ppermute | solution.py:348
  32.5 1.7 %collective-permute-start.11 = (f32[64,512]{1,0:T(8,128)S(1)}, f32[64,512]{1,0:T(8,128)S(1)}, u32[]{:S(2)}, u32[]{:S(2)}) collective-permute-start(f32[64,512]{1,0:T(8,128)S(1)} %get-tuple-element.42), channel_id=1, source_target_pairs={{0,6},{1,7},{2,4},{3,5},{4,2},{5,3},{6,0},{7,1},{8,14},{9,15},{10,... | collective-permute-start | bytes 393224 | tf_op jit(solution)/shard_map/ppermute | solution.py:348
  34.1 2.7 %collective-permute-done.12.refs_2_ = f32[64,512]{1,0:T(8,128)S(1)} collective-permute-done((f32[64,512]{1,0:T(8,128)S(1)}, f32[64,512]{1,0:T(8,128)S(1)}, u32[]{:S(2)}, u32[]{:S(2)}) %collective-permute-start.12) | collective-permute-done | bytes 131104 | tf_op jit(solution)/shard_map/ppermute | solution.py:348
  36.9 0.0 copy-done
  36.9 0.8 %shard_map.107.refs_3_ = f32[4,64,512]{2,1,0:T(8,128)} custom-call(f32[4,64,512]{2,1,0:T(8,128)S(1)} %copy-done, f32[64,512]{1,0:T(8,128)S(1)} %get-tuple-element.43.refs_1_, f32[64,512]{1,0:T(8,128)S(1)} %collective-permute-done.12.refs_2_), custom_call_target="tpu_custom_call" | custom-call | bytes 1048576 | tf_op jit(solution)/shard_map/pallas_call | solution.py:489
  37.6 2.3 %collective-permute-done.10.refs_1_ = f32[64,512]{1,0:T(8,128)S(1)} collective-permute-done((f32[64,512]{1,0:T(8,128)S(1)}, f32[64,512]{1,0:T(8,128)S(1)}, u32[]{:S(2)}, u32[]{:S(2)}) %collective-permute-start.10) | collective-permute-done | bytes 131104 | tf_op jit(solution)/shard_map/ppermute | solution.py:348
  39.9 0.0 collective-permute-done.11.refs_2_
  39.9 0.8 %shard_map.108 = f32[4,64,512]{2,1,0:T(8,128)} custom-call(f32[4,64,512]{2,1,0:T(8,128)S(1)} %copy-done, f32[64,512]{1,0:T(8,128)S(1)} %collective-permute-done.10.refs_1_, f32[64,512]{1,0:T(8,128)S(1)} %collective-permute-done.11.refs_2_, f32[4,64,512]{2,1,0:T(8,128)} %shard_map.107.refs_3_), custom_call_target="tpu_custom_call", output_to_operand_aliasing={{}: (3, {})} | custom-call | bytes 1048576 | tf_op jit(solution)/shard_map/pallas_call | solution.py:489
  (12 shorter events, 0.1 us)
Async XLA Ops:
  2.9 7.3 %copy-start.1 = (f32[512,512]{1,0:T(8,128)S(1)}, f32[512,512]{1,0:T(8,128)}, u32[]{:S(2)}) copy-start(f32[512,512]{1,0:T(8,128)} %zonal.1) | copy-start | bytes 3145732
  2.9 7.8 %collective-permute-start = (f32[2,2,40,128]{3,2,1,0:T(8,128)S(1)}, f32[2,2,40,128]{3,2,1,0:T(8,128)S(1)}, u32[]{:S(2)}, u32[]{:S(2)}) collective-permute-start(f32[2,2,40,128]{3,2,1,0:T(8,128)S(1)} %get-tuple-element.28), channel_id=1, source_target_pairs={{0,2},{1,3},{2,0},{3,1},{4,6},{5,7},{6,4},{7,5},{8,10},{9,11},{10,... | collective-permute-start | bytes 245768 | tf_op jit(solution)/shard_map/ppermute | solution.py:348
  5.9 5.3 %collective-permute-start.1 = (f32[2,2,40,128]{3,2,1,0:T(8,128)S(1)}, f32[2,2,40,128]{3,2,1,0:T(8,128)S(1)}, u32[]{:S(2)}, u32[]{:S(2)}) collective-permute-start(f32[2,2,40,128]{3,2,1,0:T(8,128)S(1)} %get-tuple-element.29), channel_id=1, source_target_pairs={{0,4},{1,5},{2,6},{3,7},{4,0},{5,1},{6,2},{7,3},{8,12},{9,13},{10,... | collective-permute-start | bytes 245768 | tf_op jit(solution)/shard_map/ppermute | solution.py:348
  7.4 5.3 %collective-permute-start.2 = (f32[2,2,40,128]{3,2,1,0:T(8,128)S(1)}, f32[2,2,40,128]{3,2,1,0:T(8,128)S(1)}, u32[]{:S(2)}, u32[]{:S(2)}) collective-permute-start(f32[2,2,40,128]{3,2,1,0:T(8,128)S(1)} %get-tuple-element.30), channel_id=1, source_target_pairs={{0,6},{1,7},{2,4},{3,5},{4,2},{5,3},{6,0},{7,1},{8,14},{9,15},{10,... | collective-permute-start | bytes 245768 | tf_op jit(solution)/shard_map/ppermute | solution.py:348
  8.0 2.2 %copy-start.2 = (f32[4,128,128]{2,1,0:T(8,128)S(1)}, f32[4,128,128]{2,1,0:T(8,128)}, u32[]{:S(2)}) copy-start(f32[4,128,128]{2,1,0:T(8,128)} %vert.1) | copy-start | bytes 786436
  8.1 8.5 %collective-permute-start.5 = (f32[4,2,40,128]{3,2,1,0:T(8,128)S(1)}, f32[4,2,40,128]{3,2,1,0:T(8,128)S(1)}, u32[]{:S(2)}, u32[]{:S(2)}) collective-permute-start(f32[4,2,40,128]{3,2,1,0:T(8,128)S(1)} %get-tuple-element.36), channel_id=1, source_target_pairs={{0,8},{8,0},{16,24},{24,16},{1,9},{9,1},{17,25},{25,17},{2,10},{10... | collective-permute-start | bytes 491528 | tf_op jit(solution)/shard_map/ppermute | solution.py:341
  12.8 13.8 %collective-permute-start.3 = (f32[4,2,40,128]{3,2,1,0:T(8,128)S(1)}, f32[4,2,40,128]{3,2,1,0:T(8,128)S(1)}, u32[]{:S(2)}, u32[]{:S(2)}) collective-permute-start(f32[4,2,40,128]{3,2,1,0:T(8,128)S(1)} %pad_maximum_fusion), channel_id=1, source_target_pairs={{0,24},{8,16},{16,0},{24,8},{1,25},{9,17},{17,1},{25,9},{2,26},{10... | collective-permute-start | bytes 491528 | tf_op jit(solution)/shard_map/ppermute | solution.py:341
  16.5 10.2 %collective-permute-start.4 = (f32[4,2,40,128]{3,2,1,0:T(8,128)S(1)}, f32[4,2,40,128]{3,2,1,0:T(8,128)S(1)}, u32[]{:S(2)}, u32[]{:S(2)}) collective-permute-start(f32[4,2,40,128]{3,2,1,0:T(8,128)S(1)} %pad_maximum_fusion.1), channel_id=1, source_target_pairs={{0,16},{8,24},{16,8},{24,0},{1,17},{9,25},{17,9},{25,1},{2,18},{10... | collective-permute-start | bytes 491528 | tf_op jit(solution)/shard_map/ppermute | solution.py:341
  16.6 4.5 %collective-permute-start.6 = (f32[2,2,40,128]{3,2,1,0:T(8,128)S(1)}, f32[2,2,40,128]{3,2,1,0:T(8,128)S(1)}, u32[]{:S(2)}, u32[]{:S(2)}) collective-permute-start(f32[2,2,40,128]{3,2,1,0:T(8,128)S(1)} %pad_maximum_fusion.3), channel_id=1, source_target_pairs={{0,2},{1,3},{2,0},{3,1},{4,6},{5,7},{6,4},{7,5},{8,10},{9,11},{10,... | collective-permute-start | bytes 245768 | tf_op jit(solution)/shard_map/ppermute | solution.py:348
  17.2 4.4 %collective-permute-start.7 = (f32[2,2,40,128]{3,2,1,0:T(8,128)S(1)}, f32[2,2,40,128]{3,2,1,0:T(8,128)S(1)}, u32[]{:S(2)}, u32[]{:S(2)}) collective-permute-start(f32[2,2,40,128]{3,2,1,0:T(8,128)S(1)} %pad_maximum_fusion.4), channel_id=1, source_target_pairs={{0,4},{1,5},{2,6},{3,7},{4,0},{5,1},{6,2},{7,3},{8,12},{9,13},{10,... | collective-permute-start | bytes 245768 | tf_op jit(solution)/shard_map/ppermute | solution.py:348
  18.1 5.3 %collective-permute-start.8 = (f32[2,2,40,128]{3,2,1,0:T(8,128)S(1)}, f32[2,2,40,128]{3,2,1,0:T(8,128)S(1)}, u32[]{:S(2)}, u32[]{:S(2)}) collective-permute-start(f32[2,2,40,128]{3,2,1,0:T(8,128)S(1)} %pad_maximum_fusion.5), channel_id=1, source_target_pairs={{0,6},{1,7},{2,4},{3,5},{4,2},{5,3},{6,0},{7,1},{8,14},{9,15},{10,... | collective-permute-start | bytes 245768 | tf_op jit(solution)/shard_map/ppermute | solution.py:348
  28.5 2.0 %collective-permute-start.9 = (f32[256,512]{1,0:T(8,128)S(1)}, f32[256,512]{1,0:T(8,128)S(1)}, u32[]{:S(2)}, u32[]{:S(2)}) collective-permute-start(f32[256,512]{1,0:T(8,128)S(1)} %get-tuple-element.40), channel_id=1, source_target_pairs={{0,1},{1,0},{2,3},{3,2},{4,5},{5,4},{6,7},{7,6},{8,9},{9,8},{10,11... | collective-permute-start | bytes 1572872 | tf_op jit(solution)/shard_map/ppermute | solution.py:355
  29.2 7.7 %copy-start = (f32[4,64,512]{2,1,0:T(8,128)S(1)}, f32[4,64,512]{2,1,0:T(8,128)}, u32[]{:S(2)}) copy-start(f32[4,64,512]{2,1,0:T(8,128)} %refs_0_.3) | copy-start | bytes 1572868
  30.6 6.3 %collective-permute-start.12 = (f32[64,512]{1,0:T(8,128)S(1)}, f32[64,512]{1,0:T(8,128)S(1)}, u32[]{:S(2)}, u32[]{:S(2)}) collective-permute-start(f32[64,512]{1,0:T(8,128)S(1)} %get-tuple-element.44), channel_id=1, source_target_pairs={{0,2},{1,3},{2,0},{3,1},{4,6},{5,7},{6,4},{7,5},{8,10},{9,11},{10,... | collective-permute-start | bytes 393224 | tf_op jit(solution)/shard_map/ppermute | solution.py:348
  31.8 8.1 %collective-permute-start.10 = (f32[64,512]{1,0:T(8,128)S(1)}, f32[64,512]{1,0:T(8,128)S(1)}, u32[]{:S(2)}, u32[]{:S(2)}) collective-permute-start(f32[64,512]{1,0:T(8,128)S(1)} %get-tuple-element.41), channel_id=1, source_target_pairs={{0,4},{1,5},{2,6},{3,7},{4,0},{5,1},{6,2},{7,3},{8,12},{9,13},{10,... | collective-permute-start | bytes 393224 | tf_op jit(solution)/shard_map/ppermute | solution.py:348
  32.5 7.4 %collective-permute-start.11 = (f32[64,512]{1,0:T(8,128)S(1)}, f32[64,512]{1,0:T(8,128)S(1)}, u32[]{:S(2)}, u32[]{:S(2)}) collective-permute-start(f32[64,512]{1,0:T(8,128)S(1)} %get-tuple-element.42), channel_id=1, source_target_pairs={{0,6},{1,7},{2,4},{3,5},{4,2},{5,3},{6,0},{7,1},{8,14},{9,15},{10,... | collective-permute-start | bytes 393224 | tf_op jit(solution)/shard_map/ppermute | solution.py:348

commit v7 on v5

--- a/solution.py
+++ b/solution.py
@@ -115,15 +115,21 @@
     tail = capacity // SUBLANES * SUBLANES
     row_id = iota((rows - tail, LANES), 0) + tail
     order = (*range(NEAR, lats), *reversed(range(NEAR)))
-    hits = jnp.concatenate(
-        [
-            one_hot(jnp.where(quad == distance * members + half, slot, -1), size)
-            for distance in order
-            for half in range(members)
-        ],
-        axis=0,
-    )
-    both = dot(hits, pieces)
+    products = [
+        dot(
+            jnp.concatenate(
+                [
+                    one_hot(jnp.where(quad == distance * members + half, slot, -1), size)
+                    for distance in bands
+                    for half in range(members)
+                ],
+                axis=0,
+            ),
+            pieces,
+        )
+        for bands in (order[: lats - NEAR], order[lats - NEAR :])
+    ]
+    both = jnp.concatenate(products, axis=0)
     for step, distance in enumerate(order):
         for half in range(members):
             at = (step * members + half) * size

time: 40.7 us -> 40.7 us (level)
  no operation moved by 1% of the time
where the time goes in v7:
time: 40.7 us; the launch traced here: 40.6 us
  starting transfers between devices  17.5 us (43%)
  waiting for transfers between devices  13.9 us (34%)
  Pallas kernels  8.19 us (20%)
  between operations  0.82 us (2%)
    ppermute x9, starting transfers between devices, to_field(): lax.ppermute(x, 'lon', [(i, (i // members ^ q) * members + i % members) f...  11.7 us
    ppermute x9, waiting for transfers between devices, to_field(): lax.ppermute(x, 'lon', [(i, (i // members ^ q) * members + i % members) f...  10.8 us
    ppermute x3, starting transfers between devices, along_lat(): lax.ppermute(x, 'lat', [(i, i ^ d ^ (i & d & 2) >> 1) for i in range(lats)])  5.75 us
    pallas_call x1, Pallas kernels, per_device(): pl.pallas_call(functools.partial(pack_kernel, members, capacity, lats), o...  2.49 us
    pallas_call x1, Pallas kernels, per_device(): call(functools.partial(late_kernel, capacity, lon_cols, len(late)), [half...  1.91 us
    ppermute x3, waiting for transfers between devices, along_lat(): lax.ppermute(x, 'lat', [(i, i ^ d ^ (i & d & 2) >> 1) for i in range(lats)])  1.84 us
    pallas_call x2, Pallas kernels, per_device(): pl.pallas_call(functools.partial(finish_kernel, members, distances), out_...  1.51 us
    ppermute x1, waiting for transfers between devices, to_member(): lax.ppermute(x, 'lon', [(i, i // members * members + (i + e) % members) f...  1.31 us
  transfers between devices with their start and end apart: 13, of which 9 were waited for; matrix products, arithmetic and copies ran while one was open for 0% of the time, Pallas kernels for 7%

profile of v7, /device:TPU:0, one launch (start us, length us, event | category | flops | bytes accessed | tf_op | source)
XLA Modules:
  0.0 40.6 jit_solution(14952600923705384913)
XLA Ops:
  0.7 0.0 copy-start.1
  0.7 2.5 %shard_map.101 = (f32[2,2,40,128]{3,2,1,0:T(8,128)S(1)}, f32[2,2,40,128]{3,2,1,0:T(8,128)S(1)}, f32[2,2,40,128]{3,2,1,0:T(8,128)S(1)}, f32[2,2,40,128]{3,2,1,0:T...) custom-call(s32[1,1]{1,0:T(1,128)} %bitcast.2.refs_0_, s32[1,768]{1,0:T(1,128)} %bitcast.3, ...), custom_call_target="tpu_custom_call" | custom-call | flops 503316480 | bytes 1048576 | tf_op jit(solution)/shard_map/pallas_call | solution.py:367
  3.2 0.0 copy-start.2
  3.2 3.0 %collective-permute-start = (f32[2,2,40,128]{3,2,1,0:T(8,128)S(1)}, f32[2,2,40,128]{3,2,1,0:T(8,128)S(1)}, u32[]{:S(2)}, u32[]{:S(2)}) collective-permute-start(f32[2,2,40,128]{3,2,1,0:T(8,128)S(1)} %get-tuple-element.24), channel_id=1, source_target_pairs={{0,2},{1,3},{2,0},{3,1},{4,6},{5,7},{6,4},{7,5},{8,10},{9,11},{10,... | collective-permute-start | bytes 245768 | tf_op jit(solution)/shard_map/ppermute | solution.py:327
  6.2 1.5 %collective-permute-start.1 = (f32[2,2,40,128]{3,2,1,0:T(8,128)S(1)}, f32[2,2,40,128]{3,2,1,0:T(8,128)S(1)}, u32[]{:S(2)}, u32[]{:S(2)}) collective-permute-start(f32[2,2,40,128]{3,2,1,0:T(8,128)S(1)} %get-tuple-element.25), channel_id=1, source_target_pairs={{0,4},{1,5},{2,6},{3,7},{4,0},{5,1},{6,2},{7,3},{8,12},{9,13},{10,... | collective-permute-start | bytes 245768 | tf_op jit(solution)/shard_map/ppermute | solution.py:327
  7.7 0.0 collective-permute-start.2
  7.7 2.0 %collective-permute-start.5 = (f32[4,2,40,128]{3,2,1,0:T(8,128)S(1)}, f32[4,2,40,128]{3,2,1,0:T(8,128)S(1)}, u32[]{:S(2)}, u32[]{:S(2)}) collective-permute-start(f32[4,2,40,128]{3,2,1,0:T(8,128)S(1)} %get-tuple-element.28), channel_id=1, source_target_pairs={{0,8},{8,0},{16,24},{24,16},{1,9},{9,1},{17,25},{25,17},{2,10},{10... | collective-permute-start | bytes 491528 | tf_op jit(solution)/shard_map/ppermute | solution.py:320
  9.8 0.0 copy-done.1
  9.8 0.0 copy-done.2
  9.8 0.5 %shard_map.100 = (bf16[512,512]{1,0:T(8,128)(2,1)S(1)}, bf16[512,512]{1,0:T(8,128)(2,1)S(1)}, bf16[256,256]{1,0:T(8,128)(2,1)S(1)}) custom-call(f32[512,512]{1,0:T(8,128)S(1)} %copy-done.1, f32[4,128,128]{2,1,0:T(8,128)S(1)} %copy-done.2), custom_call_target="tpu_custom_call" | custom-call | bytes 2097152 | tf_op jit(solution)/shard_map/pallas_call | solution.py:409
  10.3 0.0 collective-permute-done
  10.3 1.2 %collective-permute-done.1 = f32[2,2,40,128]{3,2,1,0:T(8,128)S(1)} collective-permute-done((f32[2,2,40,128]{3,2,1,0:T(8,128)S(1)}, f32[2,2,40,128]{3,2,1,0:T(8,128)S(1)}, u32[]{:S(2)}, u32[]{:S(2)}) %collective-permute-start.1) | collective-permute-done | bytes 81952 | tf_op jit(solution)/shard_map/ppermute | solution.py:327
  11.5 1.5 %collective-permute-done.2 = f32[2,2,40,128]{3,2,1,0:T(8,128)S(1)} collective-permute-done((f32[2,2,40,128]{3,2,1,0:T(8,128)S(1)}, f32[2,2,40,128]{3,2,1,0:T(8,128)S(1)}, u32[]{:S(2)}, u32[]{:S(2)}) %collective-permute-start.2) | collective-permute-done | bytes 81952 | tf_op jit(solution)/shard_map/ppermute | solution.py:327
  13.1 3.7 %collective-permute-start.3 = (f32[4,2,40,128]{3,2,1,0:T(8,128)S(1)}, f32[4,2,40,128]{3,2,1,0:T(8,128)S(1)}, u32[]{:S(2)}, u32[]{:S(2)}) collective-permute-start(f32[4,2,40,128]{3,2,1,0:T(8,128)S(1)} %pad_maximum_fusion), channel_id=1, source_target_pairs={{0,24},{8,16},{16,0},{24,8},{1,25},{9,17},{17,1},{25,9},{2,26},{10... | collective-permute-start | bytes 491528 | tf_op jit(solution)/shard_map/ppermute | solution.py:320
  16.7 0.1 collective-permute-start.4
  16.8 0.0 collective-permute-done.5
  16.8 0.6 %collective-permute-start.6 = (f32[2,2,40,128]{3,2,1,0:T(8,128)S(1)}, f32[2,2,40,128]{3,2,1,0:T(8,128)S(1)}, u32[]{:S(2)}, u32[]{:S(2)}) collective-permute-start(f32[2,2,40,128]{3,2,1,0:T(8,128)S(1)} %pad_maximum_fusion.3), channel_id=1, source_target_pairs={{0,2},{1,3},{2,0},{3,1},{4,6},{5,7},{6,4},{7,5},{8,10},{9,11},{10,... | collective-permute-start | bytes 245768 | tf_op jit(solution)/shard_map/ppermute | solution.py:327
  17.4 0.7 %collective-permute-start.7 = (f32[2,2,40,128]{3,2,1,0:T(8,128)S(1)}, f32[2,2,40,128]{3,2,1,0:T(8,128)S(1)}, u32[]{:S(2)}, u32[]{:S(2)}) collective-permute-start(f32[2,2,40,128]{3,2,1,0:T(8,128)S(1)} %pad_maximum_fusion.4), channel_id=1, source_target_pairs={{0,4},{1,5},{2,6},{3,7},{4,0},{5,1},{6,2},{7,3},{8,12},{9,13},{10,... | collective-permute-start | bytes 245768 | tf_op jit(solution)/shard_map/ppermute | solution.py:327
  18.2 2.2 %collective-permute-start.8 = (f32[2,2,40,128]{3,2,1,0:T(8,128)S(1)}, f32[2,2,40,128]{3,2,1,0:T(8,128)S(1)}, u32[]{:S(2)}, u32[]{:S(2)}) collective-permute-start(f32[2,2,40,128]{3,2,1,0:T(8,128)S(1)} %pad_maximum_fusion.5), channel_id=1, source_target_pairs={{0,6},{1,7},{2,4},{3,5},{4,2},{5,3},{6,0},{7,1},{8,14},{9,15},{10,... | collective-permute-start | bytes 245768 | tf_op jit(solution)/shard_map/ppermute | solution.py:327
  20.4 0.9 %collective-permute-done.6.refs_1_ = f32[2,2,40,128]{3,2,1,0:T(8,128)S(1)} collective-permute-done((f32[2,2,40,128]{3,2,1,0:T(8,128)S(1)}, f32[2,2,40,128]{3,2,1,0:T(8,128)S(1)}, u32[]{:S(2)}, u32[]{:S(2)}) %collective-permute-start.6) | collective-permute-done | bytes 81952 | tf_op jit(solution)/shard_map/ppermute | solution.py:327
  21.4 0.5 %collective-permute-done.7.refs_2_ = f32[2,2,40,128]{3,2,1,0:T(8,128)S(1)} collective-permute-done((f32[2,2,40,128]{3,2,1,0:T(8,128)S(1)}, f32[2,2,40,128]{3,2,1,0:T(8,128)S(1)}, u32[]{:S(2)}, u32[]{:S(2)}) %collective-permute-start.7) | collective-permute-done | bytes 81952 | tf_op jit(solution)/shard_map/ppermute | solution.py:327
  21.9 1.6 %collective-permute-done.8.refs_3_ = f32[2,2,40,128]{3,2,1,0:T(8,128)S(1)} collective-permute-done((f32[2,2,40,128]{3,2,1,0:T(8,128)S(1)}, f32[2,2,40,128]{3,2,1,0:T(8,128)S(1)}, u32[]{:S(2)}, u32[]{:S(2)}) %collective-permute-start.8) | collective-permute-done | bytes 81952 | tf_op jit(solution)/shard_map/ppermute | solution.py:327
  23.5 1.2 %shard_map.102.refs_2_ = f32[8,256,128]{2,1,0:T(8,128)S(1)} custom-call(f32[2,2,40,128]{3,2,1,0:T(8,128)S(1)} %pad_maximum_fusion.2.refs_0_, f32[2,2,40,128]{3,2,1,0:T(8,128)S(1)} %collective-permute-done.6.refs_1_, f32[2,2,40,128]{3,2,1,0:T(8,128)S(1)} %collective-permute-done.7.refs_2_, f32[2,2,40,128]{3,2,1,0:T(8,128)S(1)} %collective-permute-done.8.refs_3_), custom_call_target="tpu_custom_call" | custom-call | flops 335544320 | bytes 2097152 | tf_op jit(solution)/shard_map/pallas_call | solution.py:420
  24.7 1.8 %collective-permute-done.3.refs_0_ = f32[4,2,40,128]{3,2,1,0:T(8,128)S(1)} collective-permute-done((f32[4,2,40,128]{3,2,1,0:T(8,128)S(1)}, f32[4,2,40,128]{3,2,1,0:T(8,128)S(1)}, u32[]{:S(2)}, u32[]{:S(2)}) %collective-permute-start.3) | collective-permute-done | bytes 163872 | tf_op jit(solution)/shard_map/ppermute | solution.py:320
  26.5 0.0 collective-permute-done.4.refs_1_
  26.6 1.9 %shard_map.103 = (bf16[512,512]{1,0:T(8,128)(2,1)S(1)}, bf16[512,512]{1,0:T(8,128)(2,1)S(1)}, f32[256,512]{1,0:T(8,128)S(1)}) custom-call(f32[4,2,40,128]{3,2,1,0:T(8,128)S(1)} %collective-permute-done.3.refs_0_, f32[4,2,40,128]{3,2,1,0:T(8,128)S(1)} %collective-permute-done.4.refs_1_, f32[8,256,128]{2,1,0:T(8,128)S(1)} %shard_map.102.refs_2_, ...), custom_call_target="tpu_custom_call" | custom-call | flops 805306368 | bytes 2097152 | tf_op jit(solution)/shard_map/pallas_call | solution.py:430
  28.5 0.1 collective-permute-start.9
  28.5 0.6 %shard_map.104.refs_0_ = f32[256,512]{1,0:T(8,128)S(1)} custom-call(bf16[512,512]{1,0:T(8,128)(2,1)S(1)} %get-tuple-element.21.refs_3_.zonal_high, bf16[512,512]{1,0:T(8,128)(2,1)S(1)} %get-tuple-element.22.refs_4_.zonal_low, bf16[512,512]{1,0:T(8,128)(2,1)S(1)} %get-tuple-element.30.high, bf16[512,512]{1,0:T(8,128)(2,1)S(1)} %get-tuple-element.31.low), custom_call_target="tpu_custom_call" | custom-call | flops 402653184 | bytes 1048576 | tf_op jit(solution)/shard_map/pallas_call | solution.py:439
  29.1 0.0 copy-start
  29.1 1.3 %collective-permute-done.9.refs_1_ = f32[256,512]{1,0:T(8,128)S(1)} collective-permute-done((f32[256,512]{1,0:T(8,128)S(1)}, f32[256,512]{1,0:T(8,128)S(1)}, u32[]{:S(2)}, u32[]{:S(2)}) %collective-permute-start.9) | collective-permute-done | bytes 524320 | tf_op jit(solution)/shard_map/ppermute | solution.py:334
  30.4 0.1 shard_map.105
  30.5 1.2 %collective-permute-start.12 = (f32[64,512]{1,0:T(8,128)S(1)}, f32[64,512]{1,0:T(8,128)S(1)}, u32[]{:S(2)}, u32[]{:S(2)}) collective-permute-start(f32[64,512]{1,0:T(8,128)S(1)} %get-tuple-element.36), channel_id=1, source_target_pairs={{0,2},{1,3},{2,0},{3,1},{4,6},{5,7},{6,4},{7,5},{8,10},{9,11},{10,... | collective-permute-start | bytes 393224 | tf_op jit(solution)/shard_map/ppermute | solution.py:327
  31.7 1.0 %collective-permute-start.10 = (f32[64,512]{1,0:T(8,128)S(1)}, f32[64,512]{1,0:T(8,128)S(1)}, u32[]{:S(2)}, u32[]{:S(2)}) collective-permute-start(f32[64,512]{1,0:T(8,128)S(1)} %get-tuple-element.33), channel_id=1, source_target_pairs={{0,4},{1,5},{2,6},{3,7},{4,0},{5,1},{6,2},{7,3},{8,12},{9,13},{10,... | collective-permute-start | bytes 393224 | tf_op jit(solution)/shard_map/ppermute | solution.py:327
  32.7 1.3 %collective-permute-start.11 = (f32[64,512]{1,0:T(8,128)S(1)}, f32[64,512]{1,0:T(8,128)S(1)}, u32[]{:S(2)}, u32[]{:S(2)}) collective-permute-start(f32[64,512]{1,0:T(8,128)S(1)} %get-tuple-element.34), channel_id=1, source_target_pairs={{0,6},{1,7},{2,4},{3,5},{4,2},{5,3},{6,0},{7,1},{8,14},{9,15},{10,... | collective-permute-start | bytes 393224 | tf_op jit(solution)/shard_map/ppermute | solution.py:327
  34.1 2.8 %collective-permute-done.12.refs_2_ = f32[64,512]{1,0:T(8,128)S(1)} collective-permute-done((f32[64,512]{1,0:T(8,128)S(1)}, f32[64,512]{1,0:T(8,128)S(1)}, u32[]{:S(2)}, u32[]{:S(2)}) %collective-permute-start.12) | collective-permute-done | bytes 131104 | tf_op jit(solution)/shard_map/ppermute | solution.py:327
  36.8 0.0 copy-done
  36.8 0.8 %shard_map.106.refs_3_ = f32[4,64,512]{2,1,0:T(8,128)} custom-call(f32[4,64,512]{2,1,0:T(8,128)S(1)} %copy-done, f32[64,512]{1,0:T(8,128)S(1)} %get-tuple-element.35.refs_1_, f32[64,512]{1,0:T(8,128)S(1)} %collective-permute-done.12.refs_2_), custom_call_target="tpu_custom_call" | custom-call | bytes 1048576 | tf_op jit(solution)/shard_map/pallas_call | solution.py:453
  37.6 2.2 %collective-permute-done.10.refs_1_ = f32[64,512]{1,0:T(8,128)S(1)} collective-permute-done((f32[64,512]{1,0:T(8,128)S(1)}, f32[64,512]{1,0:T(8,128)S(1)}, u32[]{:S(2)}, u32[]{:S(2)}) %collective-permute-start.10) | collective-permute-done | bytes 131104 | tf_op jit(solution)/shard_map/ppermute | solution.py:327
  39.8 0.0 collective-permute-done.11.refs_2_
  39.8 0.8 %shard_map.107 = f32[4,64,512]{2,1,0:T(8,128)} custom-call(f32[4,64,512]{2,1,0:T(8,128)S(1)} %copy-done, f32[64,512]{1,0:T(8,128)S(1)} %collective-permute-done.10.refs_1_, f32[64,512]{1,0:T(8,128)S(1)} %collective-permute-done.11.refs_2_, f32[4,64,512]{2,1,0:T(8,128)} %shard_map.106.refs_3_), custom_call_target="tpu_custom_call", output_to_operand_aliasing={{}: (3, {})} | custom-call | bytes 1048576 | tf_op jit(solution)/shard_map/pallas_call | solution.py:453
  (11 shorter events, 0.1 us)
Async XLA Ops:
  0.7 9.1 %copy-start.1 = (f32[512,512]{1,0:T(8,128)S(1)}, f32[512,512]{1,0:T(8,128)}, u32[]{:S(2)}) copy-start(f32[512,512]{1,0:T(8,128)} %zonal.1) | copy-start | bytes 3145732
  3.2 6.6 %copy-start.2 = (f32[4,128,128]{2,1,0:T(8,128)S(1)}, f32[4,128,128]{2,1,0:T(8,128)}, u32[]{:S(2)}) copy-start(f32[4,128,128]{2,1,0:T(8,128)} %vert.1) | copy-start | bytes 786436
  3.2 7.1 %collective-permute-start = (f32[2,2,40,128]{3,2,1,0:T(8,128)S(1)}, f32[2,2,40,128]{3,2,1,0:T(8,128)S(1)}, u32[]{:S(2)}, u32[]{:S(2)}) collective-permute-start(f32[2,2,40,128]{3,2,1,0:T(8,128)S(1)} %get-tuple-element.24), channel_id=1, source_target_pairs={{0,2},{1,3},{2,0},{3,1},{4,6},{5,7},{6,4},{7,5},{8,10},{9,11},{10,... | collective-permute-start | bytes 245768 | tf_op jit(solution)/shard_map/ppermute | solution.py:327
  6.2 5.3 %collective-permute-start.1 = (f32[2,2,40,128]{3,2,1,0:T(8,128)S(1)}, f32[2,2,40,128]{3,2,1,0:T(8,128)S(1)}, u32[]{:S(2)}, u32[]{:S(2)}) collective-permute-start(f32[2,2,40,128]{3,2,1,0:T(8,128)S(1)} %get-tuple-element.25), channel_id=1, source_target_pairs={{0,4},{1,5},{2,6},{3,7},{4,0},{5,1},{6,2},{7,3},{8,12},{9,13},{10,... | collective-permute-start | bytes 245768 | tf_op jit(solution)/shard_map/ppermute | solution.py:327
  7.7 5.3 %collective-permute-start.2 = (f32[2,2,40,128]{3,2,1,0:T(8,128)S(1)}, f32[2,2,40,128]{3,2,1,0:T(8,128)S(1)}, u32[]{:S(2)}, u32[]{:S(2)}) collective-permute-start(f32[2,2,40,128]{3,2,1,0:T(8,128)S(1)} %get-tuple-element.26), channel_id=1, source_target_pairs={{0,6},{1,7},{2,4},{3,5},{4,2},{5,3},{6,0},{7,1},{8,14},{9,15},{10,... | collective-permute-start | bytes 245768 | tf_op jit(solution)/shard_map/ppermute | solution.py:327
  7.7 9.1 %collective-permute-start.5 = (f32[4,2,40,128]{3,2,1,0:T(8,128)S(1)}, f32[4,2,40,128]{3,2,1,0:T(8,128)S(1)}, u32[]{:S(2)}, u32[]{:S(2)}) collective-permute-start(f32[4,2,40,128]{3,2,1,0:T(8,128)S(1)} %get-tuple-element.28), channel_id=1, source_target_pairs={{0,8},{8,0},{16,24},{24,16},{1,9},{9,1},{17,25},{25,17},{2,10},{10... | collective-permute-start | bytes 491528 | tf_op jit(solution)/shard_map/ppermute | solution.py:320
  13.1 13.5 %collective-permute-start.3 = (f32[4,2,40,128]{3,2,1,0:T(8,128)S(1)}, f32[4,2,40,128]{3,2,1,0:T(8,128)S(1)}, u32[]{:S(2)}, u32[]{:S(2)}) collective-permute-start(f32[4,2,40,128]{3,2,1,0:T(8,128)S(1)} %pad_maximum_fusion), channel_id=1, source_target_pairs={{0,24},{8,16},{16,0},{24,8},{1,25},{9,17},{17,1},{25,9},{2,26},{10... | collective-permute-start | bytes 491528 | tf_op jit(solution)/shard_map/ppermute | solution.py:320
  16.7 9.8 %collective-permute-start.4 = (f32[4,2,40,128]{3,2,1,0:T(8,128)S(1)}, f32[4,2,40,128]{3,2,1,0:T(8,128)S(1)}, u32[]{:S(2)}, u32[]{:S(2)}) collective-permute-start(f32[4,2,40,128]{3,2,1,0:T(8,128)S(1)} %pad_maximum_fusion.1), channel_id=1, source_target_pairs={{0,16},{8,24},{16,8},{24,0},{1,17},{9,25},{17,9},{25,1},{2,18},{10... | collective-permute-start | bytes 491528 | tf_op jit(solution)/shard_map/ppermute | solution.py:320
  16.8 4.5 %collective-permute-start.6 = (f32[2,2,40,128]{3,2,1,0:T(8,128)S(1)}, f32[2,2,40,128]{3,2,1,0:T(8,128)S(1)}, u32[]{:S(2)}, u32[]{:S(2)}) collective-permute-start(f32[2,2,40,128]{3,2,1,0:T(8,128)S(1)} %pad_maximum_fusion.3), channel_id=1, source_target_pairs={{0,2},{1,3},{2,0},{3,1},{4,6},{5,7},{6,4},{7,5},{8,10},{9,11},{10,... | collective-permute-start | bytes 245768 | tf_op jit(solution)/shard_map/ppermute | solution.py:327
  17.4 4.4 %collective-permute-start.7 = (f32[2,2,40,128]{3,2,1,0:T(8,128)S(1)}, f32[2,2,40,128]{3,2,1,0:T(8,128)S(1)}, u32[]{:S(2)}, u32[]{:S(2)}) collective-permute-start(f32[2,2,40,128]{3,2,1,0:T(8,128)S(1)} %pad_maximum_fusion.4), channel_id=1, source_target_pairs={{0,4},{1,5},{2,6},{3,7},{4,0},{5,1},{6,2},{7,3},{8,12},{9,13},{10,... | collective-permute-start | bytes 245768 | tf_op jit(solution)/shard_map/ppermute | solution.py:327
  18.2 5.3 %collective-permute-start.8 = (f32[2,2,40,128]{3,2,1,0:T(8,128)S(1)}, f32[2,2,40,128]{3,2,1,0:T(8,128)S(1)}, u32[]{:S(2)}, u32[]{:S(2)}) collective-permute-start(f32[2,2,40,128]{3,2,1,0:T(8,128)S(1)} %pad_maximum_fusion.5), channel_id=1, source_target_pairs={{0,6},{1,7},{2,4},{3,5},{4,2},{5,3},{6,0},{7,1},{8,14},{9,15},{10,... | collective-permute-start | bytes 245768 | tf_op jit(solution)/shard_map/ppermute | solution.py:327
  28.5 2.0 %collective-permute-start.9 = (f32[256,512]{1,0:T(8,128)S(1)}, f32[256,512]{1,0:T(8,128)S(1)}, u32[]{:S(2)}, u32[]{:S(2)}) collective-permute-start(f32[256,512]{1,0:T(8,128)S(1)} %get-tuple-element.32), channel_id=1, source_target_pairs={{0,1},{1,0},{2,3},{3,2},{4,5},{5,4},{6,7},{7,6},{8,9},{9,8},{10,11... | collective-permute-start | bytes 1572872 | tf_op jit(solution)/shard_map/ppermute | solution.py:334
  29.1 7.7 %copy-start = (f32[4,64,512]{2,1,0:T(8,128)S(1)}, f32[4,64,512]{2,1,0:T(8,128)}, u32[]{:S(2)}) copy-start(f32[4,64,512]{2,1,0:T(8,128)} %refs_0_.3) | copy-start | bytes 1572868
  30.5 6.3 %collective-permute-start.12 = (f32[64,512]{1,0:T(8,128)S(1)}, f32[64,512]{1,0:T(8,128)S(1)}, u32[]{:S(2)}, u32[]{:S(2)}) collective-permute-start(f32[64,512]{1,0:T(8,128)S(1)} %get-tuple-element.36), channel_id=1, source_target_pairs={{0,2},{1,3},{2,0},{3,1},{4,6},{5,7},{6,4},{7,5},{8,10},{9,11},{10,... | collective-permute-start | bytes 393224 | tf_op jit(solution)/shard_map/ppermute | solution.py:327
  31.7 8.1 %collective-permute-start.10 = (f32[64,512]{1,0:T(8,128)S(1)}, f32[64,512]{1,0:T(8,128)S(1)}, u32[]{:S(2)}, u32[]{:S(2)}) collective-permute-start(f32[64,512]{1,0:T(8,128)S(1)} %get-tuple-element.33), channel_id=1, source_target_pairs={{0,4},{1,5},{2,6},{3,7},{4,0},{5,1},{6,2},{7,3},{8,12},{9,13},{10,... | collective-permute-start | bytes 393224 | tf_op jit(solution)/shard_map/ppermute | solution.py:327
  32.7 7.1 %collective-permute-start.11 = (f32[64,512]{1,0:T(8,128)S(1)}, f32[64,512]{1,0:T(8,128)S(1)}, u32[]{:S(2)}, u32[]{:S(2)}) collective-permute-start(f32[64,512]{1,0:T(8,128)S(1)} %get-tuple-element.34), channel_id=1, source_target_pairs={{0,6},{1,7},{2,4},{3,5},{4,2},{5,3},{6,0},{7,1},{8,14},{9,15},{10,... | collective-permute-start | bytes 393224 | tf_op jit(solution)/shard_map/ppermute | solution.py:327

commit v8 on v5

--- a/solution.py
+++ b/solution.py
@@ -178,7 +178,7 @@
 def scatter(pieces, half, capacity, columns):
     rows = pieces[0].shape[0]
     count = len(pieces)
-    slots = -(-count * rows // LANES) * LANES
+    slots = -(-count * rows // (2 * LANES)) * 2 * LANES
     parts, _ = message_rows(capacity)
     row_id, lane_id = iota((rows, LANES), 0), iota((rows, LANES), 1)
     piece_id = row_id >> (KW.bit_length() - 1)

time: 40.7 us -> 40.8 us (level)
  no operation moved by 1% of the time
where the time goes in v8:
time: 40.8 us; the launch traced here: 40.6 us
  starting transfers between devices  17.5 us (43%)
  waiting for transfers between devices  14 us (34%)
  Pallas kernels  8.23 us (20%)
  between operations  0.82 us (2%)
    ppermute x9, starting transfers between devices, to_field(): lax.ppermute(x, 'lon', [(i, (i // members ^ q) * members + i % members) f...  11.7 us
    ppermute x9, waiting for transfers between devices, to_field(): lax.ppermute(x, 'lon', [(i, (i // members ^ q) * members + i % members) f...  10.8 us
    ppermute x3, starting transfers between devices, along_lat(): lax.ppermute(x, 'lat', [(i, i ^ d ^ (i & d & 2) >> 1) for i in range(lats)])  5.74 us
    pallas_call x1, Pallas kernels, per_device(): pl.pallas_call(functools.partial(pack_kernel, members, capacity, lats), o...  2.5 us
    pallas_call x1, Pallas kernels, per_device(): call(functools.partial(late_kernel, capacity, lon_cols, len(late)), [half...  1.95 us
    ppermute x3, waiting for transfers between devices, along_lat(): lax.ppermute(x, 'lat', [(i, i ^ d ^ (i & d & 2) >> 1) for i in range(lats)])  1.84 us
    pallas_call x2, Pallas kernels, per_device(): pl.pallas_call(functools.partial(finish_kernel, members, distances), out_...  1.51 us
    ppermute x1, waiting for transfers between devices, to_member(): lax.ppermute(x, 'lon', [(i, i // members * members + (i + e) % members) f...  1.31 us
  transfers between devices with their start and end apart: 13, of which 9 were waited for; matrix products, arithmetic and copies ran while one was open for 0% of the time, Pallas kernels for 7%

profile of v8, /device:TPU:0, one launch (start us, length us, event | category | flops | bytes accessed | tf_op | source)
XLA Modules:
  0.0 40.6 jit_solution(4481033780769077845)
XLA Ops:
  0.7 0.0 copy-start.1
  0.7 2.5 %shard_map.101 = (f32[2,2,40,128]{3,2,1,0:T(8,128)S(1)}, f32[2,2,40,128]{3,2,1,0:T(8,128)S(1)}, f32[2,2,40,128]{3,2,1,0:T(8,128)S(1)}, f32[2,2,40,128]{3,2,1,0:T...) custom-call(s32[1,1]{1,0:T(1,128)} %bitcast.2.refs_0_, s32[1,768]{1,0:T(1,128)} %bitcast.3, ...), custom_call_target="tpu_custom_call" | custom-call | flops 503316480 | bytes 1048576 | tf_op jit(solution)/shard_map/pallas_call | solution.py:361
  3.2 0.0 copy-start.2
  3.2 3.0 %collective-permute-start = (f32[2,2,40,128]{3,2,1,0:T(8,128)S(1)}, f32[2,2,40,128]{3,2,1,0:T(8,128)S(1)}, u32[]{:S(2)}, u32[]{:S(2)}) collective-permute-start(f32[2,2,40,128]{3,2,1,0:T(8,128)S(1)} %get-tuple-element.24), channel_id=1, source_target_pairs={{0,2},{1,3},{2,0},{3,1},{4,6},{5,7},{6,4},{7,5},{8,10},{9,11},{10,... | collective-permute-start | bytes 245768 | tf_op jit(solution)/shard_map/ppermute | solution.py:321
  6.2 1.5 %collective-permute-start.1 = (f32[2,2,40,128]{3,2,1,0:T(8,128)S(1)}, f32[2,2,40,128]{3,2,1,0:T(8,128)S(1)}, u32[]{:S(2)}, u32[]{:S(2)}) collective-permute-start(f32[2,2,40,128]{3,2,1,0:T(8,128)S(1)} %get-tuple-element.25), channel_id=1, source_target_pairs={{0,4},{1,5},{2,6},{3,7},{4,0},{5,1},{6,2},{7,3},{8,12},{9,13},{10,... | collective-permute-start | bytes 245768 | tf_op jit(solution)/shard_map/ppermute | solution.py:321
  7.7 0.0 collective-permute-start.2
  7.7 2.0 %collective-permute-start.5 = (f32[4,2,40,128]{3,2,1,0:T(8,128)S(1)}, f32[4,2,40,128]{3,2,1,0:T(8,128)S(1)}, u32[]{:S(2)}, u32[]{:S(2)}) collective-permute-start(f32[4,2,40,128]{3,2,1,0:T(8,128)S(1)} %get-tuple-element.28), channel_id=1, source_target_pairs={{0,8},{8,0},{16,24},{24,16},{1,9},{9,1},{17,25},{25,17},{2,10},{10... | collective-permute-start | bytes 491528 | tf_op jit(solution)/shard_map/ppermute | solution.py:314
  9.8 0.0 copy-done.1
  9.8 0.0 copy-done.2
  9.8 0.5 %shard_map.100 = (bf16[512,512]{1,0:T(8,128)(2,1)S(1)}, bf16[512,512]{1,0:T(8,128)(2,1)S(1)}, bf16[256,256]{1,0:T(8,128)(2,1)S(1)}) custom-call(f32[512,512]{1,0:T(8,128)S(1)} %copy-done.1, f32[4,128,128]{2,1,0:T(8,128)S(1)} %copy-done.2), custom_call_target="tpu_custom_call" | custom-call | bytes 2097152 | tf_op jit(solution)/shard_map/pallas_call | solution.py:403
  10.3 0.0 collective-permute-done
  10.3 1.2 %collective-permute-done.1 = f32[2,2,40,128]{3,2,1,0:T(8,128)S(1)} collective-permute-done((f32[2,2,40,128]{3,2,1,0:T(8,128)S(1)}, f32[2,2,40,128]{3,2,1,0:T(8,128)S(1)}, u32[]{:S(2)}, u32[]{:S(2)}) %collective-permute-start.1) | collective-permute-done | bytes 81952 | tf_op jit(solution)/shard_map/ppermute | solution.py:321
  11.5 1.5 %collective-permute-done.2 = f32[2,2,40,128]{3,2,1,0:T(8,128)S(1)} collective-permute-done((f32[2,2,40,128]{3,2,1,0:T(8,128)S(1)}, f32[2,2,40,128]{3,2,1,0:T(8,128)S(1)}, u32[]{:S(2)}, u32[]{:S(2)}) %collective-permute-start.2) | collective-permute-done | bytes 81952 | tf_op jit(solution)/shard_map/ppermute | solution.py:321
  13.1 3.7 %collective-permute-start.3 = (f32[4,2,40,128]{3,2,1,0:T(8,128)S(1)}, f32[4,2,40,128]{3,2,1,0:T(8,128)S(1)}, u32[]{:S(2)}, u32[]{:S(2)}) collective-permute-start(f32[4,2,40,128]{3,2,1,0:T(8,128)S(1)} %pad_maximum_fusion), channel_id=1, source_target_pairs={{0,24},{8,16},{16,0},{24,8},{1,25},{9,17},{17,1},{25,9},{2,26},{10... | collective-permute-start | bytes 491528 | tf_op jit(solution)/shard_map/ppermute | solution.py:314
  16.7 0.1 collective-permute-start.4
  16.8 0.0 collective-permute-done.5
  16.8 0.6 %collective-permute-start.6 = (f32[2,2,40,128]{3,2,1,0:T(8,128)S(1)}, f32[2,2,40,128]{3,2,1,0:T(8,128)S(1)}, u32[]{:S(2)}, u32[]{:S(2)}) collective-permute-start(f32[2,2,40,128]{3,2,1,0:T(8,128)S(1)} %pad_maximum_fusion.3), channel_id=1, source_target_pairs={{0,2},{1,3},{2,0},{3,1},{4,6},{5,7},{6,4},{7,5},{8,10},{9,11},{10,... | collective-permute-start | bytes 245768 | tf_op jit(solution)/shard_map/ppermute | solution.py:321
  17.5 0.7 %collective-permute-start.7 = (f32[2,2,40,128]{3,2,1,0:T(8,128)S(1)}, f32[2,2,40,128]{3,2,1,0:T(8,128)S(1)}, u32[]{:S(2)}, u32[]{:S(2)}) collective-permute-start(f32[2,2,40,128]{3,2,1,0:T(8,128)S(1)} %pad_maximum_fusion.4), channel_id=1, source_target_pairs={{0,4},{1,5},{2,6},{3,7},{4,0},{5,1},{6,2},{7,3},{8,12},{9,13},{10,... | collective-permute-start | bytes 245768 | tf_op jit(solution)/shard_map/ppermute | solution.py:321
  18.2 2.2 %collective-permute-start.8 = (f32[2,2,40,128]{3,2,1,0:T(8,128)S(1)}, f32[2,2,40,128]{3,2,1,0:T(8,128)S(1)}, u32[]{:S(2)}, u32[]{:S(2)}) collective-permute-start(f32[2,2,40,128]{3,2,1,0:T(8,128)S(1)} %pad_maximum_fusion.5), channel_id=1, source_target_pairs={{0,6},{1,7},{2,4},{3,5},{4,2},{5,3},{6,0},{7,1},{8,14},{9,15},{10,... | collective-permute-start | bytes 245768 | tf_op jit(solution)/shard_map/ppermute | solution.py:321
  20.4 0.9 %collective-permute-done.6.refs_1_ = f32[2,2,40,128]{3,2,1,0:T(8,128)S(1)} collective-permute-done((f32[2,2,40,128]{3,2,1,0:T(8,128)S(1)}, f32[2,2,40,128]{3,2,1,0:T(8,128)S(1)}, u32[]{:S(2)}, u32[]{:S(2)}) %collective-permute-start.6) | collective-permute-done | bytes 81952 | tf_op jit(solution)/shard_map/ppermute | solution.py:321
  21.4 0.5 %collective-permute-done.7.refs_2_ = f32[2,2,40,128]{3,2,1,0:T(8,128)S(1)} collective-permute-done((f32[2,2,40,128]{3,2,1,0:T(8,128)S(1)}, f32[2,2,40,128]{3,2,1,0:T(8,128)S(1)}, u32[]{:S(2)}, u32[]{:S(2)}) %collective-permute-start.7) | collective-permute-done | bytes 81952 | tf_op jit(solution)/shard_map/ppermute | solution.py:321
  21.9 1.6 %collective-permute-done.8.refs_3_ = f32[2,2,40,128]{3,2,1,0:T(8,128)S(1)} collective-permute-done((f32[2,2,40,128]{3,2,1,0:T(8,128)S(1)}, f32[2,2,40,128]{3,2,1,0:T(8,128)S(1)}, u32[]{:S(2)}, u32[]{:S(2)}) %collective-permute-start.8) | collective-permute-done | bytes 81952 | tf_op jit(solution)/shard_map/ppermute | solution.py:321
  23.5 1.2 %shard_map.102.refs_2_ = f32[8,256,128]{2,1,0:T(8,128)S(1)} custom-call(f32[2,2,40,128]{3,2,1,0:T(8,128)S(1)} %pad_maximum_fusion.2.refs_0_, f32[2,2,40,128]{3,2,1,0:T(8,128)S(1)} %collective-permute-done.6.refs_1_, f32[2,2,40,128]{3,2,1,0:T(8,128)S(1)} %collective-permute-done.7.refs_2_, f32[2,2,40,128]{3,2,1,0:T(8,128)S(1)} %collective-permute-done.8.refs_3_), custom_call_target="tpu_custom_call" | custom-call | flops 335544320 | bytes 2097152 | tf_op jit(solution)/shard_map/pallas_call | solution.py:414
  24.7 1.8 %collective-permute-done.3.refs_0_ = f32[4,2,40,128]{3,2,1,0:T(8,128)S(1)} collective-permute-done((f32[4,2,40,128]{3,2,1,0:T(8,128)S(1)}, f32[4,2,40,128]{3,2,1,0:T(8,128)S(1)}, u32[]{:S(2)}, u32[]{:S(2)}) %collective-permute-start.3) | collective-permute-done | bytes 163872 | tf_op jit(solution)/shard_map/ppermute | solution.py:314
  26.5 0.0 collective-permute-done.4.refs_1_
  26.5 1.9 %shard_map.103 = (bf16[512,512]{1,0:T(8,128)(2,1)S(1)}, bf16[512,512]{1,0:T(8,128)(2,1)S(1)}, f32[256,512]{1,0:T(8,128)S(1)}) custom-call(f32[4,2,40,128]{3,2,1,0:T(8,128)S(1)} %collective-permute-done.3.refs_0_, f32[4,2,40,128]{3,2,1,0:T(8,128)S(1)} %collective-permute-done.4.refs_1_, f32[8,256,128]{2,1,0:T(8,128)S(1)} %shard_map.102.refs_2_, ...), custom_call_target="tpu_custom_call" | custom-call | flops 805306368 | bytes 2097152 | tf_op jit(solution)/shard_map/pallas_call | solution.py:424
  28.5 0.1 collective-permute-start.9
  28.6 0.6 %shard_map.104.refs_0_ = f32[256,512]{1,0:T(8,128)S(1)} custom-call(bf16[512,512]{1,0:T(8,128)(2,1)S(1)} %get-tuple-element.21.refs_3_.zonal_high, bf16[512,512]{1,0:T(8,128)(2,1)S(1)} %get-tuple-element.22.refs_4_.zonal_low, bf16[512,512]{1,0:T(8,128)(2,1)S(1)} %get-tuple-element.30.high, bf16[512,512]{1,0:T(8,128)(2,1)S(1)} %get-tuple-element.31.low), custom_call_target="tpu_custom_call" | custom-call | flops 402653184 | bytes 1048576 | tf_op jit(solution)/shard_map/pallas_call | solution.py:433
  29.2 0.0 copy-start
  29.2 1.3 %collective-permute-done.9.refs_1_ = f32[256,512]{1,0:T(8,128)S(1)} collective-permute-done((f32[256,512]{1,0:T(8,128)S(1)}, f32[256,512]{1,0:T(8,128)S(1)}, u32[]{:S(2)}, u32[]{:S(2)}) %collective-permute-start.9) | collective-permute-done | bytes 524320 | tf_op jit(solution)/shard_map/ppermute | solution.py:328
  30.5 0.1 shard_map.105
  30.5 1.2 %collective-permute-start.12 = (f32[64,512]{1,0:T(8,128)S(1)}, f32[64,512]{1,0:T(8,128)S(1)}, u32[]{:S(2)}, u32[]{:S(2)}) collective-permute-start(f32[64,512]{1,0:T(8,128)S(1)} %get-tuple-element.36), channel_id=1, source_target_pairs={{0,2},{1,3},{2,0},{3,1},{4,6},{5,7},{6,4},{7,5},{8,10},{9,11},{10,... | collective-permute-start | bytes 393224 | tf_op jit(solution)/shard_map/ppermute | solution.py:321
  31.8 1.0 %collective-permute-start.10 = (f32[64,512]{1,0:T(8,128)S(1)}, f32[64,512]{1,0:T(8,128)S(1)}, u32[]{:S(2)}, u32[]{:S(2)}) collective-permute-start(f32[64,512]{1,0:T(8,128)S(1)} %get-tuple-element.33), channel_id=1, source_target_pairs={{0,4},{1,5},{2,6},{3,7},{4,0},{5,1},{6,2},{7,3},{8,12},{9,13},{10,... | collective-permute-start | bytes 393224 | tf_op jit(solution)/shard_map/ppermute | solution.py:321
  32.8 1.3 %collective-permute-start.11 = (f32[64,512]{1,0:T(8,128)S(1)}, f32[64,512]{1,0:T(8,128)S(1)}, u32[]{:S(2)}, u32[]{:S(2)}) collective-permute-start(f32[64,512]{1,0:T(8,128)S(1)} %get-tuple-element.34), channel_id=1, source_target_pairs={{0,6},{1,7},{2,4},{3,5},{4,2},{5,3},{6,0},{7,1},{8,14},{9,15},{10,... | collective-permute-start | bytes 393224 | tf_op jit(solution)/shard_map/ppermute | solution.py:321
  34.1 2.8 %collective-permute-done.12.refs_2_ = f32[64,512]{1,0:T(8,128)S(1)} collective-permute-done((f32[64,512]{1,0:T(8,128)S(1)}, f32[64,512]{1,0:T(8,128)S(1)}, u32[]{:S(2)}, u32[]{:S(2)}) %collective-permute-start.12) | collective-permute-done | bytes 131104 | tf_op jit(solution)/shard_map/ppermute | solution.py:321
  36.8 0.0 copy-done
  36.8 0.8 %shard_map.106.refs_3_ = f32[4,64,512]{2,1,0:T(8,128)} custom-call(f32[4,64,512]{2,1,0:T(8,128)S(1)} %copy-done, f32[64,512]{1,0:T(8,128)S(1)} %get-tuple-element.35.refs_1_, f32[64,512]{1,0:T(8,128)S(1)} %collective-permute-done.12.refs_2_), custom_call_target="tpu_custom_call" | custom-call | bytes 1048576 | tf_op jit(solution)/shard_map/pallas_call | solution.py:447
  37.6 2.2 %collective-permute-done.10.refs_1_ = f32[64,512]{1,0:T(8,128)S(1)} collective-permute-done((f32[64,512]{1,0:T(8,128)S(1)}, f32[64,512]{1,0:T(8,128)S(1)}, u32[]{:S(2)}, u32[]{:S(2)}) %collective-permute-start.10) | collective-permute-done | bytes 131104 | tf_op jit(solution)/shard_map/ppermute | solution.py:321
  39.8 0.0 collective-permute-done.11.refs_2_
  39.8 0.8 %shard_map.107 = f32[4,64,512]{2,1,0:T(8,128)} custom-call(f32[4,64,512]{2,1,0:T(8,128)S(1)} %copy-done, f32[64,512]{1,0:T(8,128)S(1)} %collective-permute-done.10.refs_1_, f32[64,512]{1,0:T(8,128)S(1)} %collective-permute-done.11.refs_2_, f32[4,64,512]{2,1,0:T(8,128)} %shard_map.106.refs_3_), custom_call_target="tpu_custom_call", output_to_operand_aliasing={{}: (3, {})} | custom-call | bytes 1048576 | tf_op jit(solution)/shard_map/pallas_call | solution.py:447
  (11 shorter events, 0.1 us)
Async XLA Ops:
  0.7 9.1 %copy-start.1 = (f32[512,512]{1,0:T(8,128)S(1)}, f32[512,512]{1,0:T(8,128)}, u32[]{:S(2)}) copy-start(f32[512,512]{1,0:T(8,128)} %zonal.1) | copy-start | bytes 3145732
  3.2 6.6 %copy-start.2 = (f32[4,128,128]{2,1,0:T(8,128)S(1)}, f32[4,128,128]{2,1,0:T(8,128)}, u32[]{:S(2)}) copy-start(f32[4,128,128]{2,1,0:T(8,128)} %vert.1) | copy-start | bytes 786436
  3.2 7.1 %collective-permute-start = (f32[2,2,40,128]{3,2,1,0:T(8,128)S(1)}, f32[2,2,40,128]{3,2,1,0:T(8,128)S(1)}, u32[]{:S(2)}, u32[]{:S(2)}) collective-permute-start(f32[2,2,40,128]{3,2,1,0:T(8,128)S(1)} %get-tuple-element.24), channel_id=1, source_target_pairs={{0,2},{1,3},{2,0},{3,1},{4,6},{5,7},{6,4},{7,5},{8,10},{9,11},{10,... | collective-permute-start | bytes 245768 | tf_op jit(solution)/shard_map/ppermute | solution.py:321
  6.2 5.3 %collective-permute-start.1 = (f32[2,2,40,128]{3,2,1,0:T(8,128)S(1)}, f32[2,2,40,128]{3,2,1,0:T(8,128)S(1)}, u32[]{:S(2)}, u32[]{:S(2)}) collective-permute-start(f32[2,2,40,128]{3,2,1,0:T(8,128)S(1)} %get-tuple-element.25), channel_id=1, source_target_pairs={{0,4},{1,5},{2,6},{3,7},{4,0},{5,1},{6,2},{7,3},{8,12},{9,13},{10,... | collective-permute-start | bytes 245768 | tf_op jit(solution)/shard_map/ppermute | solution.py:321
  7.7 5.3 %collective-permute-start.2 = (f32[2,2,40,128]{3,2,1,0:T(8,128)S(1)}, f32[2,2,40,128]{3,2,1,0:T(8,128)S(1)}, u32[]{:S(2)}, u32[]{:S(2)}) collective-permute-start(f32[2,2,40,128]{3,2,1,0:T(8,128)S(1)} %get-tuple-element.26), channel_id=1, source_target_pairs={{0,6},{1,7},{2,4},{3,5},{4,2},{5,3},{6,0},{7,1},{8,14},{9,15},{10,... | collective-permute-start | bytes 245768 | tf_op jit(solution)/shard_map/ppermute | solution.py:321
  7.7 9.1 %collective-permute-start.5 = (f32[4,2,40,128]{3,2,1,0:T(8,128)S(1)}, f32[4,2,40,128]{3,2,1,0:T(8,128)S(1)}, u32[]{:S(2)}, u32[]{:S(2)}) collective-permute-start(f32[4,2,40,128]{3,2,1,0:T(8,128)S(1)} %get-tuple-element.28), channel_id=1, source_target_pairs={{0,8},{8,0},{16,24},{24,16},{1,9},{9,1},{17,25},{25,17},{2,10},{10... | collective-permute-start | bytes 491528 | tf_op jit(solution)/shard_map/ppermute | solution.py:314
  13.1 13.5 %collective-permute-start.3 = (f32[4,2,40,128]{3,2,1,0:T(8,128)S(1)}, f32[4,2,40,128]{3,2,1,0:T(8,128)S(1)}, u32[]{:S(2)}, u32[]{:S(2)}) collective-permute-start(f32[4,2,40,128]{3,2,1,0:T(8,128)S(1)} %pad_maximum_fusion), channel_id=1, source_target_pairs={{0,24},{8,16},{16,0},{24,8},{1,25},{9,17},{17,1},{25,9},{2,26},{10... | collective-permute-start | bytes 491528 | tf_op jit(solution)/shard_map/ppermute | solution.py:314
  16.7 9.8 %collective-permute-start.4 = (f32[4,2,40,128]{3,2,1,0:T(8,128)S(1)}, f32[4,2,40,128]{3,2,1,0:T(8,128)S(1)}, u32[]{:S(2)}, u32[]{:S(2)}) collective-permute-start(f32[4,2,40,128]{3,2,1,0:T(8,128)S(1)} %pad_maximum_fusion.1), channel_id=1, source_target_pairs={{0,16},{8,24},{16,8},{24,0},{1,17},{9,25},{17,9},{25,1},{2,18},{10... | collective-permute-start | bytes 491528 | tf_op jit(solution)/shard_map/ppermute | solution.py:314
  16.8 4.5 %collective-permute-start.6 = (f32[2,2,40,128]{3,2,1,0:T(8,128)S(1)}, f32[2,2,40,128]{3,2,1,0:T(8,128)S(1)}, u32[]{:S(2)}, u32[]{:S(2)}) collective-permute-start(f32[2,2,40,128]{3,2,1,0:T(8,128)S(1)} %pad_maximum_fusion.3), channel_id=1, source_target_pairs={{0,2},{1,3},{2,0},{3,1},{4,6},{5,7},{6,4},{7,5},{8,10},{9,11},{10,... | collective-permute-start | bytes 245768 | tf_op jit(solution)/shard_map/ppermute | solution.py:321
  17.5 4.4 %collective-permute-start.7 = (f32[2,2,40,128]{3,2,1,0:T(8,128)S(1)}, f32[2,2,40,128]{3,2,1,0:T(8,128)S(1)}, u32[]{:S(2)}, u32[]{:S(2)}) collective-permute-start(f32[2,2,40,128]{3,2,1,0:T(8,128)S(1)} %pad_maximum_fusion.4), channel_id=1, source_target_pairs={{0,4},{1,5},{2,6},{3,7},{4,0},{5,1},{6,2},{7,3},{8,12},{9,13},{10,... | collective-permute-start | bytes 245768 | tf_op jit(solution)/shard_map/ppermute | solution.py:321
  18.2 5.3 %collective-permute-start.8 = (f32[2,2,40,128]{3,2,1,0:T(8,128)S(1)}, f32[2,2,40,128]{3,2,1,0:T(8,128)S(1)}, u32[]{:S(2)}, u32[]{:S(2)}) collective-permute-start(f32[2,2,40,128]{3,2,1,0:T(8,128)S(1)} %pad_maximum_fusion.5), channel_id=1, source_target_pairs={{0,6},{1,7},{2,4},{3,5},{4,2},{5,3},{6,0},{7,1},{8,14},{9,15},{10,... | collective-permute-start | bytes 245768 | tf_op jit(solution)/shard_map/ppermute | solution.py:321
  28.5 2.0 %collective-permute-start.9 = (f32[256,512]{1,0:T(8,128)S(1)}, f32[256,512]{1,0:T(8,128)S(1)}, u32[]{:S(2)}, u32[]{:S(2)}) collective-permute-start(f32[256,512]{1,0:T(8,128)S(1)} %get-tuple-element.32), channel_id=1, source_target_pairs={{0,1},{1,0},{2,3},{3,2},{4,5},{5,4},{6,7},{7,6},{8,9},{9,8},{10,11... | collective-permute-start | bytes 1572872 | tf_op jit(solution)/shard_map/ppermute | solution.py:328
  29.2 7.7 %copy-start = (f32[4,64,512]{2,1,0:T(8,128)S(1)}, f32[4,64,512]{2,1,0:T(8,128)}, u32[]{:S(2)}) copy-start(f32[4,64,512]{2,1,0:T(8,128)} %refs_0_.3) | copy-start | bytes 1572868
  30.5 6.3 %collective-permute-start.12 = (f32[64,512]{1,0:T(8,128)S(1)}, f32[64,512]{1,0:T(8,128)S(1)}, u32[]{:S(2)}, u32[]{:S(2)}) collective-permute-start(f32[64,512]{1,0:T(8,128)S(1)} %get-tuple-element.36), channel_id=1, source_target_pairs={{0,2},{1,3},{2,0},{3,1},{4,6},{5,7},{6,4},{7,5},{8,10},{9,11},{10,... | collective-permute-start | bytes 393224 | tf_op jit(solution)/shard_map/ppermute | solution.py:321
  31.8 8.1 %collective-permute-start.10 = (f32[64,512]{1,0:T(8,128)S(1)}, f32[64,512]{1,0:T(8,128)S(1)}, u32[]{:S(2)}, u32[]{:S(2)}) collective-permute-start(f32[64,512]{1,0:T(8,128)S(1)} %get-tuple-element.33), channel_id=1, source_target_pairs={{0,4},{1,5},{2,6},{3,7},{4,0},{5,1},{6,2},{7,3},{8,12},{9,13},{10,... | collective-permute-start | bytes 393224 | tf_op jit(solution)/shard_map/ppermute | solution.py:321
  32.8 7.1 %collective-permute-start.11 = (f32[64,512]{1,0:T(8,128)S(1)}, f32[64,512]{1,0:T(8,128)S(1)}, u32[]{:S(2)}, u32[]{:S(2)}) collective-permute-start(f32[64,512]{1,0:T(8,128)S(1)} %get-tuple-element.34), channel_id=1, source_target_pairs={{0,6},{1,7},{2,4},{3,5},{4,2},{5,3},{6,0},{7,1},{8,14},{9,15},{10,... | collective-permute-start | bytes 393224 | tf_op jit(solution)/shard_map/ppermute | solution.py:321
